TPU v7x, 32 devices: a whole 2x2x4 slice. The times are simulated.
32 devices in a mesh: dp: 8 (over z, x), fsdp: 4 (over y, core).
Axes of the slice: x: 2, y: 2, z: 4, core: 2. Of those that a mesh axis runs over, the one named last changes fastest.
Arguments:
- latents: int32 [512, 96, 32], P(('dp', 'fsdp')), may hold values from 0 to 31
- targets: int32 [512, 48, 32], P(('dp', 'fsdp')), may hold values from 0 to 31
- horizon: int32 [512], P(('dp', 'fsdp')), may hold values from 8 to 48, as said below
- memory_valid: int32 [512], P(('dp', 'fsdp')), may hold values 0 or 1
- embed: float32 [1024, 256], P('dp', 'fsdp'), may hold values from -1 to 1
- qkv_weight: float32 [3, 256, 768], P(None, 'fsdp', 'dp'), may hold values from -0.375 to 0.375
- out_weight: float32 [3, 256, 256], P(None, 'fsdp', 'dp'), may hold values from -2 to 2
- up_weight: float32 [3, 256, 1024], P(None, 'fsdp', 'dp'), may hold values from -0.375 to 0.375
- down_weight: float32 [3, 1024, 256], P(None, 'dp', 'fsdp'), may hold values from -0.1875 to 0.1875
- head_weight: float32 [256, 1024], P('fsdp', 'dp'), may hold values from -0.375 to 0.375
- gains: float32 [7, 256], replicated, may hold values from 0.4 to 2.2
- embed_rows: float32 [1024], P('dp'), may hold values from 9.6270915e-11 to 3.8508366e-10
- embed_cols: float32 [256], P('fsdp'), may hold values from 9.6270915e-11 to 3.8508366e-10
- qkv_rows: float32 [3, 256], P(None, 'fsdp'), may hold values from 9.6270915e-11 to 3.8508366e-10
- qkv_cols: float32 [3, 768], P(None, 'dp'), may hold values from 9.6270915e-11 to 3.8508366e-10
- out_rows: float32 [3, 256], P(None, 'fsdp'), may hold values from 9.6270915e-11 to 3.8508366e-10
- out_cols: float32 [3, 256], P(None, 'dp'), may hold values from 9.6270915e-11 to 3.8508366e-10
- up_rows: float32 [3, 256], P(None, 'fsdp'), may hold values from 9.6270915e-11 to 3.8508366e-10
- up_cols: float32 [3, 1024], P(None, 'dp'), may hold values from 9.6270915e-11 to 3.8508366e-10
- down_rows: float32 [3, 1024], P(None, 'dp'), may hold values from 9.6270915e-11 to 3.8508366e-10
- down_cols: float32 [3, 256], P(None, 'fsdp'), may hold values from 9.6270915e-11 to 3.8508366e-10
- head_rows: float32 [256], P('fsdp'), may hold values from 9.6270915e-11 to 3.8508366e-10
- head_cols: float32 [1024], P('dp'), may hold values from 9.6270915e-11 to 3.8508366e-10
- gain_second: float32 [7, 256], replicated, may hold values from 9.627091e-10 to 3.8508365e-09
Outputs:
- loss_sum: float32 [], replicated
- position_count: float32 [], replicated
- grad_norm: float32 [], replicated
- embed_new: float32 [1024, 256], P('dp', 'fsdp')
- embed_grad: float32 [1024, 256], P('dp', 'fsdp')
- embed_rows_new: float32 [1024], P('dp')
- embed_cols_new: float32 [256], P('fsdp')
- qkv_new: float32 [3, 256, 768], P(None, 'fsdp', 'dp')
- qkv_grad: float32 [3, 256, 768], P(None, 'fsdp', 'dp')
- qkv_rows_new: float32 [3, 256], P(None, 'fsdp')
- qkv_cols_new: float32 [3, 768], P(None, 'dp')
- out_new: float32 [3, 256, 256], P(None, 'fsdp', 'dp')
- out_grad: float32 [3, 256, 256], P(None, 'fsdp', 'dp')
- out_rows_new: float32 [3, 256], P(None, 'fsdp')
- out_cols_new: float32 [3, 256], P(None, 'dp')
- up_new: float32 [3, 256, 1024], P(None, 'fsdp', 'dp')
- up_grad: float32 [3, 256, 1024], P(None, 'fsdp', 'dp')
- up_rows_new: float32 [3, 256], P(None, 'fsdp')
- up_cols_new: float32 [3, 1024], P(None, 'dp')
- down_new: float32 [3, 1024, 256], P(None, 'dp', 'fsdp')
- down_grad: float32 [3, 1024, 256], P(None, 'dp', 'fsdp')
- down_rows_new: float32 [3, 1024], P(None, 'dp')
- down_cols_new: float32 [3, 256], P(None, 'fsdp')
- head_new: float32 [256, 1024], P('fsdp', 'dp')
- head_grad: float32 [256, 1024], P('fsdp', 'dp')
- head_rows_new: float32 [256], P('fsdp')
- head_cols_new: float32 [1024], P('dp')
- gains_new: float32 [7, 256], replicated
- gains_grad: float32 [7, 256], replicated
- gain_second_new: float32 [7, 256], replicated
Inputs may be any that keep to these rules, and one draw needn't show every extreme that they name: `horizon`: some sample has all 48 positions counted.
All inputs are finite; a program needn't handle non-finite values. No bound on the sum of `memory_valid` on one device may be relied on, other than what follows from the above.
Results may differ from a plain program's by a relative error of at most 0.0095.
The roundings to bfloat16 on the way count: a program that leaves them out, or rounds other values in their place, can miss the bound.
Values may be sent and summed in bfloat16 or wider, within the bound.
No kernel may reach another device: no remote copies, remote signals or barrier semaphores. Data moves between devices by JAX's collectives and lax.ppermute only.
A program may use at most 192 MiB of HBM per device.

v0:
```python
import jax
import jax.numpy as jnp
from jax import lax
from jax.sharding import PartitionSpec as P

D = 256
HEADS = 8
FF = 1024
CATS = 32
CLASSES = 32
LAYERS = 3
SEG = 48
MEM = 48
CTX = 96
VOCAB = 1024


decay_two = 0.9
step_rate = 0.3
clip_limit = 0.05
tiny_term = 1e-30
norm_eps = 1e-06
masked_score = -1e30


def matmul(left, right):
    return jnp.dot(left, right, preferred_element_type=jnp.float32)


def matmul_tn(left, right):
    return lax.dot_general(
        left, right, (((0,), (0,)), ((), ())), preferred_element_type=jnp.float32
    )


def matmul_nt(left, right):
    return lax.dot_general(
        left, right, (((1,), (1,)), ((), ())), preferred_element_type=jnp.float32
    )


def rms_norm(values, gain_row):
    return (
        values * lax.rsqrt(jnp.mean(values * values, axis=-1, keepdims=True) + norm_eps) * gain_row
    )


def in_blocks(array, block):
    return array.reshape((array.shape[0] // block, block) + array.shape[1:])


def split_qkv(qkv, samples, block):
    heads_of = [
        qkv[:, start * D : (start + 1) * D].reshape(samples, CTX, HEADS, D // HEADS)
        for start in range(3)
    ]
    return [in_blocks(piece, block) for piece in heads_of]


def block_scores(queries, key_rows, allowed):
    scores = jnp.einsum("bqhd,bkhd->bhqk", queries, key_rows, preferred_element_type=jnp.float32)
    return jnp.where(allowed, scores * queries.shape[-1] ** (-0.5), masked_score)


def attend_block(inputs):
    queries, key_rows, value_rows, allowed = inputs
    scores = block_scores(queries, key_rows, allowed)
    peak_score = jnp.max(scores, axis=-1, keepdims=True)
    exponent = jnp.exp(scores - peak_score)
    total = jnp.sum(exponent, axis=-1, keepdims=True)
    probability = (exponent / total).astype(jnp.bfloat16)
    mixture = jnp.einsum(
        "bhqk,bkhd->bqhd", probability, value_rows, preferred_element_type=jnp.float32
    )
    return (mixture, peak_score[..., 0] + jnp.log(total[..., 0]))


def attend_back(inputs):
    queries, key_rows, value_rows, allowed, upstream, log_total = inputs
    scale_factor = queries.shape[-1] ** (-0.5)
    probability = jnp.exp(block_scores(queries, key_rows, allowed) - log_total[..., None])
    dprob = jnp.einsum("bqhd,bkhd->bhqk", upstream, value_rows, preferred_element_type=jnp.float32)
    dscore = (probability * (dprob - jnp.sum(probability * dprob, axis=-1, keepdims=True))).astype(
        jnp.bfloat16
    )
    dvalues = jnp.einsum(
        "bhqk,bqhd->bkhd",
        probability.astype(jnp.bfloat16),
        upstream,
        preferred_element_type=jnp.float32,
    )
    dqueries = (
        jnp.einsum("bhqk,bkhd->bqhd", dscore, key_rows, preferred_element_type=jnp.float32)
        * scale_factor
    )
    dkeys = (
        jnp.einsum("bhqk,bqhd->bkhd", dscore, queries, preferred_element_type=jnp.float32)
        * scale_factor
    )
    return (dqueries, dkeys, dvalues)


def attention(qkv, allowed):
    samples = allowed.shape[0]
    block = min(samples, 8)
    queries, key_rows, value_rows = split_qkv(qkv, samples, block)
    mixture, log_total = lax.map(
        attend_block, (queries, key_rows, value_rows, in_blocks(allowed, block))
    )
    return (mixture.reshape(samples * CTX, D), log_total)


def attention_back(qkv, allowed, upstream, log_total):
    samples = allowed.shape[0]
    block = min(samples, 8)
    queries, key_rows, value_rows = split_qkv(qkv, samples, block)
    upstream_blocks = in_blocks(upstream.reshape(samples, CTX, HEADS, D // HEADS), block)
    dqueries, dkeys, dvalues = lax.map(
        attend_back,
        (queries, key_rows, value_rows, in_blocks(allowed, block), upstream_blocks, log_total),
    )
    return jnp.concatenate(
        [
            dqueries.reshape(samples * CTX, D),
            dkeys.reshape(samples * CTX, D),
            dvalues.reshape(samples * CTX, D),
        ],
        axis=1,
    )


def layer_forward(hidden, w_qkv, w_out, w_up, w_down, gain_att, gain_ffn, allowed):
    normed, att_pull = jax.vjp(rms_norm, hidden, gain_att)
    normed_low = normed.astype(jnp.bfloat16)
    qkv = matmul(normed_low, w_qkv).astype(jnp.bfloat16)
    mixture, log_total = attention(qkv, allowed)
    mixture = mixture.astype(jnp.bfloat16)
    middle = hidden + matmul(mixture, w_out)
    normed_two, ffn_pull = jax.vjp(rms_norm, middle, gain_ffn)
    normed_two = normed_two.astype(jnp.bfloat16)
    inner_act, gelu_pull = jax.vjp(jax.nn.gelu, matmul(normed_two, w_up))
    activated = inner_act.astype(jnp.bfloat16)
    output = middle + matmul(activated, w_down)
    return (
        output,
        (att_pull, normed_low, qkv, mixture, log_total, ffn_pull, normed_two, gelu_pull, activated),
    )


def layer_backward(hidden, w_qkv, w_out, w_up, w_down, gain_att, gain_ffn, allowed, upstream):
    output, saved = layer_forward(hidden, w_qkv, w_out, w_up, w_down, gain_att, gain_ffn, allowed)
    att_pull, normed_low, qkv, mixture, log_total, ffn_pull, normed_two, gelu_pull, activated = (
        saved
    )
    dout = upstream.astype(jnp.bfloat16)
    grad_down = matmul_tn(activated, dout)
    dinner = gelu_pull(matmul_nt(dout, w_down))[0].astype(jnp.bfloat16)
    grad_up = matmul_tn(normed_two, dinner)
    dmiddle_norm, dgain_ffn = ffn_pull(matmul_nt(dinner, w_up))
    dmiddle = upstream + dmiddle_norm
    dattend = dmiddle.astype(jnp.bfloat16)
    grad_out = matmul_tn(mixture, dattend)
    dmixture = matmul_nt(dattend, w_out).astype(jnp.bfloat16)
    dqkv = attention_back(qkv, allowed, dmixture, log_total).astype(jnp.bfloat16)
    grad_qkv = matmul_tn(normed_low, dqkv)
    dhidden_norm, dgain_att = att_pull(matmul_nt(dqkv, w_qkv))
    return (dmiddle + dhidden_norm, (grad_qkv, grad_out, grad_up, grad_down), dgain_att, dgain_ffn)


def per_weight(items):
    return jnp.concatenate([jnp.sum(item, axis=-1).reshape(-1) for item in items])


def shards(
    latents,
    targets,
    horizon,
    memory_valid,
    embed,
    qkv_weight,
    out_weight,
    up_weight,
    down_weight,
    head_weight,
    gains,
    embed_rows,
    embed_cols,
    qkv_rows,
    qkv_cols,
    out_rows,
    out_cols,
    up_rows,
    up_cols,
    down_rows,
    down_cols,
    head_rows,
    head_cols,
    gain_second,
):
    samples = latents.shape[0]
    outer_count = lax.axis_size("dp")
    inner_count = lax.axis_size("fsdp")
    embed_piece, head_piece = (
        lax.all_gather(embed.astype(jnp.bfloat16), "fsdp", axis=1, tiled=True),
        lax.all_gather(head_weight.astype(jnp.bfloat16), "fsdp", axis=0, tiled=True),
    )
    embed_full, head_full = (
        lax.all_gather(embed_piece, "dp", axis=0, tiled=True),
        lax.all_gather(head_piece, "dp", axis=1, tiled=True),
    )

    def fetch_layer(layer_at):
        piece_qkv, piece_out, piece_up, piece_down = (
            lax.all_gather(qkv_weight[layer_at].astype(jnp.bfloat16), "fsdp", axis=0, tiled=True),
            lax.all_gather(out_weight[layer_at].astype(jnp.bfloat16), "fsdp", axis=0, tiled=True),
            lax.all_gather(up_weight[layer_at].astype(jnp.bfloat16), "fsdp", axis=0, tiled=True),
            lax.all_gather(down_weight[layer_at].astype(jnp.bfloat16), "fsdp", axis=1, tiled=True),
        )
        return (
            lax.all_gather(piece_qkv, "dp", axis=1, tiled=True),
            lax.all_gather(piece_out, "dp", axis=1, tiled=True),
            lax.all_gather(piece_up, "dp", axis=1, tiled=True),
            lax.all_gather(piece_down, "dp", axis=0, tiled=True),
        )

    classes = jnp.arange(CLASSES, dtype=jnp.int32)
    one_hot = (latents[..., None] == classes).astype(jnp.bfloat16).reshape(samples * CTX, VOCAB)
    positions = jnp.arange(CTX, dtype=jnp.int32)
    causal = positions[None, :] <= positions[:, None]
    crosses = (positions[:, None] >= MEM) & (positions[None, :] < MEM)
    allowed = causal[None, None] & jnp.logical_not(
        crosses[None, None] & (memory_valid[:, None, None, None] == 0)
    )
    hidden = matmul(one_hot, embed_full)
    inputs = []
    for layer_at in range(LAYERS):
        fetched = fetch_layer(layer_at)
        inputs.append(hidden)
        hidden = layer_forward(
            hidden,
            fetched[0],
            fetched[1],
            fetched[2],
            fetched[3],
            gains[layer_at],
            gains[LAYERS + layer_at],
            allowed,
        )[0]
    latest = hidden.reshape(samples, CTX, D)[:, MEM:].reshape(samples * SEG, D)
    final, final_pull = jax.vjp(rms_norm, latest, gains[2 * LAYERS])
    final_low = final.astype(jnp.bfloat16)
    logits = matmul(final_low, head_full).reshape(samples, SEG, CATS, CLASSES)
    peak_logit = jnp.max(logits, axis=-1, keepdims=True)
    shifted = jnp.exp(logits - peak_logit)
    total = jnp.sum(shifted, axis=-1, keepdims=True)
    log_total = peak_logit[..., 0] + jnp.log(total[..., 0])
    target_hot = targets[..., None] == classes
    chosen = jnp.sum(jnp.where(target_hot, logits, 0.0), axis=-1)
    counted = jnp.arange(SEG, dtype=jnp.int32)[None, :] < horizon[:, None]
    per_position = jnp.sum(log_total - chosen, axis=-1)
    loss_local = jnp.sum(jnp.where(counted, per_position, 0.0))
    count_local = jnp.sum(horizon).astype(jnp.float32)
    loss_total, count_total = lax.psum((loss_local, count_local), ("dp", "fsdp"))
    dlogits = (shifted / total - target_hot.astype(jnp.float32)) * counted[:, :, None, None].astype(
        jnp.float32
    )
    dlogits = dlogits.reshape(samples * SEG, VOCAB).astype(jnp.bfloat16)
    head_term = matmul_tn(final_low, dlogits)
    dlatest, dgain_final = final_pull(matmul_nt(dlogits, head_full))
    upstream = jnp.concatenate(
        [jnp.zeros((samples, MEM, D), jnp.float32), dlatest.reshape(samples, SEG, D)], axis=1
    )
    upstream = upstream.reshape(samples * CTX, D)
    layer_sums = [None] * LAYERS
    att_terms = [None] * LAYERS
    ffn_terms = [None] * LAYERS
    for layer_at in reversed(range(LAYERS)):
        weights_now = fetch_layer(layer_at)
        upstream, terms, att_terms[layer_at], ffn_terms[layer_at] = layer_backward(
            inputs[layer_at],
            weights_now[0],
            weights_now[1],
            weights_now[2],
            weights_now[3],
            gains[layer_at],
            gains[LAYERS + layer_at],
            allowed,
            upstream,
        )
        term_qkv, term_out, term_up, term_down = terms
        term_qkv, term_out, term_up, term_down = (
            lax.psum_scatter(
                term_qkv.astype(jnp.bfloat16), "dp", scatter_dimension=1, tiled=True
            ).astype(jnp.float32),
            lax.psum_scatter(
                term_out.astype(jnp.bfloat16), "dp", scatter_dimension=1, tiled=True
            ).astype(jnp.float32),
            lax.psum_scatter(
                term_up.astype(jnp.bfloat16), "dp", scatter_dimension=1, tiled=True
            ).astype(jnp.float32),
            lax.psum_scatter(
                term_down.astype(jnp.bfloat16), "dp", scatter_dimension=0, tiled=True
            ).astype(jnp.float32),
        )
        layer_sums[layer_at] = (
            lax.psum_scatter(
                term_qkv.astype(jnp.bfloat16), "fsdp", scatter_dimension=0, tiled=True
            ).astype(jnp.float32),
            lax.psum_scatter(
                term_out.astype(jnp.bfloat16), "fsdp", scatter_dimension=0, tiled=True
            ).astype(jnp.float32),
            lax.psum_scatter(
                term_up.astype(jnp.bfloat16), "fsdp", scatter_dimension=0, tiled=True
            ).astype(jnp.float32),
            lax.psum_scatter(
                term_down.astype(jnp.bfloat16), "fsdp", scatter_dimension=1, tiled=True
            ).astype(jnp.float32),
        )
    embed_term = matmul_tn(one_hot, upstream.astype(jnp.bfloat16))
    embed_term, head_term = (
        lax.psum_scatter(
            embed_term.astype(jnp.bfloat16), "dp", scatter_dimension=0, tiled=True
        ).astype(jnp.float32),
        lax.psum_scatter(
            head_term.astype(jnp.bfloat16), "dp", scatter_dimension=1, tiled=True
        ).astype(jnp.float32),
    )
    embed_raw, head_raw = (
        lax.psum_scatter(
            embed_term.astype(jnp.bfloat16), "fsdp", scatter_dimension=1, tiled=True
        ).astype(jnp.float32),
        lax.psum_scatter(
            head_term.astype(jnp.bfloat16), "fsdp", scatter_dimension=0, tiled=True
        ).astype(jnp.float32),
    )
    gain_local = jnp.stack(att_terms + ffn_terms + [dgain_final])
    masters = [embed, qkv_weight, out_weight, up_weight, down_weight, head_weight]
    raws = (
        [embed_raw]
        + [
            jnp.stack([layer_sums[layer_at][which] for layer_at in range(LAYERS)])
            for which in range(4)
        ]
        + [head_raw]
    )
    row_old = [embed_rows, qkv_rows, out_rows, up_rows, down_rows, head_rows]
    column_old = [embed_cols, qkv_cols, out_cols, up_cols, down_cols, head_cols]
    row_part = [jnp.sum(raw * raw, axis=-1) for raw in raws]
    column_part = [jnp.sum(raw * raw, axis=-2) for raw in raws]
    dp_sums = lax.psum(
        (
            column_part[0],
            row_part[1],
            row_part[2],
            row_part[3],
            column_part[4],
            row_part[5],
            gain_local,
        ),
        "dp",
    )
    fsdp_sums = lax.psum(
        (
            row_part[0],
            column_part[1],
            column_part[2],
            column_part[3],
            row_part[4],
            column_part[5],
            dp_sums[6],
        ),
        "fsdp",
    )
    row_global = [fsdp_sums[0], dp_sums[1], dp_sums[2], dp_sums[3], fsdp_sums[4], dp_sums[5]]
    column_global = [dp_sums[0], fsdp_sums[1], fsdp_sums[2], fsdp_sums[3], dp_sums[4], fsdp_sums[5]]
    gain_sum = fsdp_sums[6]
    replicas = [inner_count, outer_count, outer_count, outer_count, inner_count, outer_count]
    row_count = [VOCAB, D, D, D, FF, D]
    column_count = [D, 3 * D, D, FF, D, VOCAB]
    bounds = [0, 1, 1 + LAYERS, 1 + 2 * LAYERS, 1 + 3 * LAYERS, 1 + 4 * LAYERS, 2 + 4 * LAYERS]
    square_local = jnp.zeros((), jnp.float32)
    for part_sum in row_part:
        square_local = square_local + jnp.sum(part_sum)
    weight_square = per_weight([jnp.sum(master * master, axis=-1) for master in masters])

    def moments(scaling):
        rows_new = [
            decay_two * row_old[which]
            + (1 - decay_two)
            * (scaling * scaling * row_global[which] / column_count[which] + tiny_term)
            for which in range(6)
        ]
        columns_new = [
            decay_two * column_old[which]
            + (1 - decay_two)
            * (scaling * scaling * column_global[which] / row_count[which] + tiny_term)
            for which in range(6)
        ]
        return (rows_new, columns_new)

    square_total = lax.psum(square_local, ("dp", "fsdp"))
    norm_value = jnp.sqrt(square_total + jnp.sum(gain_sum * gain_sum)) / count_total
    scaling = jnp.minimum(1.0, clip_limit / norm_value) / count_total
    rows_new, columns_new = moments(scaling)
    row_vector, weight_total = lax.psum(
        (per_weight([rows_new[which] / replicas[which] for which in range(6)]), weight_square),
        ("dp", "fsdp"),
    )
    results = [loss_total, count_total, norm_value]
    for which in range(6):
        leading = masters[which].shape[:-2]
        mean_rows = (
            row_vector[bounds[which] : bounds[which + 1]].reshape(leading) / row_count[which]
        )
        spread = jnp.sqrt(
            weight_total[bounds[which] : bounds[which + 1]].reshape(leading)
            / (row_count[which] * column_count[which])
        )
        grad = raws[which] * scaling
        second = (
            rows_new[which][..., :, None]
            * columns_new[which][..., None, :]
            / mean_rows[..., None, None]
        )
        updated = masters[which] - step_rate * spread[..., None, None] * grad * lax.rsqrt(second)
        results = results + [updated, grad, rows_new[which], columns_new[which]]
    gain_grad = gain_sum * scaling
    gain_second_new = decay_two * gain_second + (1 - decay_two) * (
        gain_grad * gain_grad + tiny_term
    )
    gains_new = gains - step_rate * jnp.sqrt(
        jnp.mean(gains * gains, axis=-1, keepdims=True)
    ) * gain_grad * lax.rsqrt(gain_second_new)
    results = results + [gains_new, gain_grad, gain_second_new]
    return tuple(results)


def solution(mesh):
    return jax.shard_map(
        shards,
        mesh=mesh,
        in_specs=(
            P(("dp", "fsdp"), None, None),
            P(("dp", "fsdp"), None, None),
            P(("dp", "fsdp")),
            P(("dp", "fsdp")),
            P("dp", "fsdp"),
            P(None, "fsdp", "dp"),
            P(None, "fsdp", "dp"),
            P(None, "fsdp", "dp"),
            P(None, "dp", "fsdp"),
            P("fsdp", "dp"),
            P(),
            P("dp"),
            P("fsdp"),
            P(None, "fsdp"),
            P(None, "dp"),
            P(None, "fsdp"),
            P(None, "dp"),
            P(None, "fsdp"),
            P(None, "dp"),
            P(None, "dp"),
            P(None, "fsdp"),
            P("fsdp"),
            P("dp"),
            P(),
        ),
        out_specs=(
            P(),
            P(),
            P(),
            P("dp", "fsdp"),
            P("dp", "fsdp"),
            P("dp"),
            P("fsdp"),
            P(None, "fsdp", "dp"),
            P(None, "fsdp", "dp"),
            P(None, "fsdp"),
            P(None, "dp"),
            P(None, "fsdp", "dp"),
            P(None, "fsdp", "dp"),
            P(None, "fsdp"),
            P(None, "dp"),
            P(None, "fsdp", "dp"),
            P(None, "fsdp", "dp"),
            P(None, "fsdp"),
            P(None, "dp"),
            P(None, "dp", "fsdp"),
            P(None, "dp", "fsdp"),
            P(None, "dp"),
            P(None, "fsdp"),
            P("fsdp", "dp"),
            P("fsdp", "dp"),
            P("fsdp"),
            P("dp"),
            P(),
            P(),
            P(),
        ),
        check_vma=False,
    )
```

profile of v0, /device:TPU:0, one launch (start us, length us, event | category | flops | bytes accessed | tf_op | source)
XLA Modules:
  0.0 2111.8 jit_solution(3363845899177932197)
XLA Ops:
  84.3 33.0 %all-gather.19 = bf16[1,256,256]{1,2,0:T(8,128)(2,1)} all-gather(bf16[1,256,32]{1,2,0:T(8,128)(2,1)S(1)} %copy.426), channel_id=21, replica_groups=mesh['dp'=8,'fsdp'=4] {'dp'}, dimensions={2}, use_global_device_ids=true | all-gather | bytes 147456 | tf_op jit(solution)/shard_map/all_gather | solution.py:221
  122.8 32.5 %all-gather.11 = bf16[1,256,256]{1,2,0:T(8,128)(2,1)} all-gather(bf16[1,256,32]{1,2,0:T(8,128)(2,1)S(1)} %copy.416), channel_id=13, replica_groups=mesh['dp'=8,'fsdp'=4] {'dp'}, dimensions={2}, use_global_device_ids=true | all-gather | bytes 147456 | tf_op jit(solution)/shard_map/all_gather | solution.py:221
  160.9 30.6 %all-gather.3 = bf16[1,256,256]{1,2,0:T(8,128)(2,1)S(1)} all-gather(bf16[1,256,32]{1,2,0:T(8,128)(2,1)S(1)} %copy.406), channel_id=5, replica_groups=mesh['dp'=8,'fsdp'=4] {'dp'}, dimensions={2}, use_global_device_ids=true | all-gather | bytes 147456 | tf_op jit(solution)/shard_map/all_gather | solution.py:221
  191.6 31.1 %all-gather.1 = bf16[1,256,768]{1,2,0:T(8,128)(2,1)S(1)} all-gather(bf16[1,256,96]{1,2,0:T(8,128)(2,1)S(1)} %copy.397), channel_id=3, replica_groups=mesh['dp'=8,'fsdp'=4] {'dp'}, dimensions={2}, use_global_device_ids=true | all-gather | bytes 442368 | tf_op jit(solution)/shard_map/all_gather | solution.py:220
  222.8 33.0 %all-gather.9 = bf16[1,256,768]{1,2,0:T(8,128)(2,1)} all-gather(bf16[1,256,96]{1,2,0:T(8,128)(2,1)S(1)} %copy.408), channel_id=11, replica_groups=mesh['dp'=8,'fsdp'=4] {'dp'}, dimensions={2}, use_global_device_ids=true | all-gather | bytes 442368 | tf_op jit(solution)/shard_map/all_gather | solution.py:220
  255.7 33.2 %all-gather.17 = bf16[1,256,768]{1,2,0:T(8,128)(2,1)} all-gather(bf16[1,256,96]{1,2,0:T(8,128)(2,1)S(1)} %copy.418), channel_id=19, replica_groups=mesh['dp'=8,'fsdp'=4] {'dp'}, dimensions={2}, use_global_device_ids=true | all-gather | bytes 442368 | tf_op jit(solution)/shard_map/all_gather | solution.py:220
  289.0 28.7 %all-gather.5 = bf16[1,256,1024]{2,1,0:T(8,128)(2,1)} all-gather(bf16[1,256,128]{2,1,0:T(8,128)(2,1)S(1)} %all-gather.4), channel_id=7, replica_groups=mesh['dp'=8,'fsdp'=4] {'dp'}, dimensions={2}, use_global_device_ids=true | all-gather | bytes 589824 | tf_op jit(solution)/shard_map/all_gather | solution.py:222
  317.7 28.6 %all-gather.13 = bf16[1,256,1024]{2,1,0:T(8,128)(2,1)} all-gather(bf16[1,256,128]{2,1,0:T(8,128)(2,1)S(1)} %all-gather.12), channel_id=15, replica_groups=mesh['dp'=8,'fsdp'=4] {'dp'}, dimensions={2}, use_global_device_ids=true | all-gather | bytes 589824 | tf_op jit(solution)/shard_map/all_gather | solution.py:222
  346.3 28.1 %all-gather.21 = bf16[1,256,1024]{2,1,0:T(8,128)(2,1)} all-gather(bf16[1,256,128]{2,1,0:T(8,128)(2,1)S(1)} %all-gather.20), channel_id=23, replica_groups=mesh['dp'=8,'fsdp'=4] {'dp'}, dimensions={2}, use_global_device_ids=true | all-gather | bytes 589824 | tf_op jit(solution)/shard_map/all_gather | solution.py:222
  374.4 28.7 %all-gather.7 = bf16[1,1024,256]{1,2,0:T(8,128)(2,1)} all-gather(bf16[1,128,256]{1,2,0:T(8,128)(2,1)S(1)} %all-gather.6), channel_id=9, replica_groups=mesh['dp'=8,'fsdp'=4] {'dp'}, dimensions={1}, use_global_device_ids=true | all-gather | bytes 589824 | tf_op jit(solution)/shard_map/all_gather | solution.py:223
  403.2 29.0 %all-gather.15 = bf16[1,1024,256]{1,2,0:T(8,128)(2,1)} all-gather(bf16[1,128,256]{1,2,0:T(8,128)(2,1)S(1)} %all-gather.14), channel_id=17, replica_groups=mesh['dp'=8,'fsdp'=4] {'dp'}, dimensions={1}, use_global_device_ids=true | all-gather | bytes 589824 | tf_op jit(solution)/shard_map/all_gather | solution.py:223
  432.2 28.6 %all-gather.23 = bf16[1,1024,256]{1,2,0:T(8,128)(2,1)} all-gather(bf16[1,128,256]{1,2,0:T(8,128)(2,1)S(1)} %all-gather.22), channel_id=25, replica_groups=mesh['dp'=8,'fsdp'=4] {'dp'}, dimensions={1}, use_global_device_ids=true | all-gather | bytes 589824 | tf_op jit(solution)/shard_map/all_gather | solution.py:223
  460.9 27.0 %all_gather.135 = bf16[256,1024]{1,0:T(8,128)(2,1)S(1)} all-gather(bf16[256,128]{1,0:T(8,128)(2,1)S(1)} %all_gather.134), channel_id=1, replica_groups=mesh['dp'=8,'fsdp'=4] {'dp'}, dimensions={1}, use_global_device_ids=true | all-gather | bytes 589824 | tf_op jit(solution)/shard_map/all_gather | solution.py:209
  487.9 27.0 %all_gather.109 = bf16[1024,256]{0,1:T(8,128)(2,1)S(1)} all-gather(bf16[128,256]{0,1:T(8,128)(2,1)S(1)} %all_gather.108), channel_id=1, replica_groups=mesh['dp'=8,'fsdp'=4] {'dp'}, dimensions={0}, use_global_device_ids=true | all-gather | bytes 589824 | tf_op jit(solution)/shard_map/all_gather | solution.py:208
  519.9 10.0 eq.38
  631.0 10.0 while.111
  751.4 19.3 while.112
  831.8 20.8 while.114
  900.1 19.5 while.116
  984.2 20.6 reduce-scatter.63.cloned.1.call-done
  1006.4 61.9 %reduce-scatter.61.cloned.1.call-done = bf16[256,96]{0,1:T(8,128)(2,1)} async-done(((bf16[256,768]{0,1:T(8,128)(2,1)}), bf16[256,96]{0,1:T(8,128)(2,1)}) %reduce-scatter.61.cloned.1.call-update) | async-done | bytes 49168 | tf_op jit(solution)/shard_map/reduce_scatter | solution.py:292
  1069.9 62.0 %reduce-scatter.59.cloned.1.call-done = bf16[256,96]{0,1:T(8,128)(2,1)} async-done(((bf16[256,768]{0,1:T(8,128)(2,1)}), bf16[256,96]{0,1:T(8,128)(2,1)}) %reduce-scatter.59.cloned.1.call-update) | async-done | bytes 49168 | tf_op jit(solution)/shard_map/reduce_scatter | solution.py:292
  1135.5 60.6 %reduce-scatter.81.cloned.1.call-done = bf16[128,256]{1,0:T(8,128)(2,1)} async-done(((bf16[1024,256]{1,0:T(8,128)(2,1)}), bf16[128,256]{1,0:T(8,128)(2,1)}) %reduce-scatter.81.cloned.1.call-update) | async-done | bytes 65552 | tf_op jit(solution)/shard_map/reduce_scatter | solution.py:301
  1197.8 63.0 %reduce-scatter.79.cloned.1.call-done = bf16[128,256]{1,0:T(8,128)(2,1)} async-done(((bf16[1024,256]{1,0:T(8,128)(2,1)}), bf16[128,256]{1,0:T(8,128)(2,1)}) %reduce-scatter.79.cloned.1.call-update) | async-done | bytes 65552 | tf_op jit(solution)/shard_map/reduce_scatter | solution.py:301
  1262.5 62.7 %reduce-scatter.77.cloned.1.call-done = bf16[128,256]{1,0:T(8,128)(2,1)} async-done(((bf16[1024,256]{1,0:T(8,128)(2,1)}), bf16[128,256]{1,0:T(8,128)(2,1)}) %reduce-scatter.77.cloned.1.call-update) | async-done | bytes 65552 | tf_op jit(solution)/shard_map/reduce_scatter | solution.py:301
  1326.8 62.8 %reduce-scatter.57.cloned.1.call-done = bf16[128,256]{1,0:T(8,128)(2,1)} async-done(((bf16[1024,256]{1,0:T(8,128)(2,1)}), bf16[128,256]{1,0:T(8,128)(2,1)}) %reduce-scatter.57.cloned.1.call-update) | async-done | bytes 65552 | tf_op jit(solution)/shard_map/reduce_scatter | solution.py:321
  1391.4 62.5 %reduce-scatter.103.cloned.1.call-done = bf16[128,256]{1,0:T(8,128)(2,1)} async-done(((bf16[1024,256]{1,0:T(8,128)(2,1)}), bf16[128,256]{1,0:T(8,128)(2,1)}) %reduce-scatter.103.cloned.1.call-update) | async-done | bytes 65552
  1455.6 62.9 %reduce-scatter.101.cloned.1.call-done = bf16[128,256]{1,0:T(8,128)(2,1)} async-done(((bf16[1024,256]{1,0:T(8,128)(2,1)}), bf16[128,256]{1,0:T(8,128)(2,1)}) %reduce-scatter.101.cloned.1.call-update) | async-done | bytes 65552
  1520.3 62.5 %reduce-scatter.99.cloned.1.call-done = bf16[128,256]{1,0:T(8,128)(2,1)} async-done(((bf16[1024,256]{1,0:T(8,128)(2,1)}), bf16[128,256]{1,0:T(8,128)(2,1)}) %reduce-scatter.99.cloned.1.call-update) | async-done | bytes 65552
  1588.6 15.7 reduce-scatter.97.cloned.1.call-done
  1605.0 21.5 %reduce-scatter.95.cloned.1.call-done = bf16[64,32]{1,0:T(8,128)(2,1)} async-done(((bf16[256,32]{1,0:T(8,128)(2,1)}), bf16[64,32]{1,0:T(8,128)(2,1)}) %reduce-scatter.95.cloned.1.call-update) | async-done | bytes 4112
  1627.3 21.1 reduce-scatter.93.cloned.1.call-done
  1649.8 20.9 reduce-scatter.91.cloned.1.call-done
  1671.5 21.6 %reduce-scatter.89.cloned.1.call-done = bf16[64,96]{1,0:T(8,128)(2,1)} async-done(((bf16[256,96]{1,0:T(8,128)(2,1)}), bf16[64,96]{1,0:T(8,128)(2,1)}) %reduce-scatter.89.cloned.1.call-update) | async-done | bytes 12304
  1694.0 21.6 %reduce-scatter.87.cloned.1.call-done = bf16[64,96]{1,0:T(8,128)(2,1)} async-done(((bf16[256,96]{1,0:T(8,128)(2,1)}), bf16[64,96]{1,0:T(8,128)(2,1)}) %reduce-scatter.87.cloned.1.call-update) | async-done | bytes 12304
  1717.1 64.0 %reduce-scatter.111.cloned.1.call-done = bf16[128,256]{1,0:T(8,128)(2,1)} async-done(((bf16[1024,256]{1,0:T(8,128)(2,1)}), bf16[128,256]{1,0:T(8,128)(2,1)}) %reduce-scatter.111.cloned.1.call-update) | async-done | bytes 65552
  1782.7 19.3 reduce-scatter.109.cloned.1.call-done
  1802.9 21.2 %reduce-scatter.107.cloned.1.call-done = bf16[64,128]{1,0:T(8,128)(2,1)} async-done(((bf16[256,128]{1,0:T(8,128)(2,1)}), bf16[64,128]{1,0:T(8,128)(2,1)}) %reduce-scatter.107.cloned.1.call-update) | async-done | bytes 16400
  1824.9 21.1 reduce-scatter.105.cloned.1.call-done
  1846.8 21.6 %reduce-scatter.85.cloned.1.call-done = bf16[64,128]{1,0:T(8,128)(2,1)} async-done(((bf16[256,128]{1,0:T(8,128)(2,1)}), bf16[64,128]{1,0:T(8,128)(2,1)}) %reduce-scatter.85.cloned.1.call-update) | async-done | bytes 16400
  1871.8 18.5 reduce-scatter.75.cloned.1.call-done
  1890.3 21.9 %reduce-scatter.73.cloned.1.call-done = bf16[64,128]{1,0:T(8,128)(2,1)} async-done(((bf16[256,128]{1,0:T(8,128)(2,1)}), bf16[64,128]{1,0:T(8,128)(2,1)}) %reduce-scatter.73.cloned.1.call-update) | async-done | bytes 16400 | tf_op jit(solution)/shard_map/reduce_scatter | solution.py:312
  1912.2 21.7 %reduce-scatter.71.cloned.1.call-done = bf16[64,128]{1,0:T(8,128)(2,1)} async-done(((bf16[256,128]{1,0:T(8,128)(2,1)}), bf16[64,128]{1,0:T(8,128)(2,1)}) %reduce-scatter.71.cloned.1.call-update) | async-done | bytes 16400 | tf_op jit(solution)/shard_map/reduce_scatter | solution.py:312
  1937.3 19.1 reduce-scatter.83.cloned.1.call-done
  1958.5 37.1 %all-reduce.3 = (f32[7,256]{1,0:T(8,128)S(1)}, f32[3,64]{1,0:T(4,128)S(1)}, f32[3,64]{1,0:T(4,128)S(1)}, f32[3,64]{1,0:T(4,128)S(1)}, f32[64]{0:T(128)S(1)}, /*index=5*/f32[64]{0:T(128)S(1)}, f32[3,64]{1,0:T(4,128)S(1)}) all-reduce(f32[7,256]{1,0:T(8,128)S(1)} %stack.102, ...), channel_id=1, replica_groups=mesh['dp'=8,'fsdp'=4] {'dp'}, use_global_device_ids=true, to_apply=%region_100.101 | all-reduce | flops 2688 | bytes 21504 | tf_op jit(solution)/shard_map/psum | solution.py:350
  1995.6 10.3 all-reduce.4
  2006.5 36.8 %all-reduce.2 = (f32[]{:T(128)}, f32[]{:T(128)}) all-reduce(f32[]{:T(128)S(6)} %convert_element_type.390, f32[]{:T(128)S(6)} %add.502), channel_id=1, replica_groups=mesh['dp'=8,'fsdp'=4] {'dp','fsdp'}, use_global_device_ids=true, to_apply=%region_26.27 | all-reduce | flops 2 | bytes 16 | tf_op jit(solution)/shard_map/psum | solution.py:263
  2049.9 41.8 %all-reduce.1 = (f32[]{:T(128)}, f32[14]{0:T(128)S(1)}, f32[14]{0:T(128)S(1)}) all-reduce(f32[]{:T(128)} %select_reduce_fusion.1, f32[14]{0:T(128)S(1)} %concatenate.26, f32[14]{0:T(128)S(1)} %concatenate.25), channel_id=1, replica_groups=mesh['dp'=8,'fsdp'=4] {'dp','fsdp'}, use_global_device_ids=true, to_apply=%region_24.25 | all-reduce | flops 29 | bytes 232 | tf_op jit(solution)/shard_map/psum | solution.py:263
  (942 shorter events, 631.9 us)
Async XLA Ops:
  7.2 972.3 %reduce-scatter.69.cloned.1.call-start = ((), (), s32[]{:S(2)}) async-start(), calls=%async_computation.34 | async-start | bytes 147456 | tf_op jit(solution)/shard_map/reduce_scatter | solution.py:295
  9.6 555.3 %copy-start.146 = (f32[1,256]{1,0:T(1,128)}, f32[1,256]{1,0:T(1,128)S(1)}, u32[]{:S(2)}) copy-start(f32[1,256]{1,0:T(1,128)S(1)} %get-tuple-element.1191) | copy-start | bytes 3076
  9.6 560.3 %copy-start.157 = (f32[1,256]{1,0:T(1,128)}, f32[1,256]{1,0:T(1,128)S(1)}, u32[]{:S(2)}) copy-start(f32[1,256]{1,0:T(1,128)S(1)} %get-tuple-element.1190) | copy-start | bytes 3076
  9.6 589.4 %copy-start.149 = (f32[1,256]{1,0:T(1,128)}, f32[1,256]{1,0:T(1,128)S(1)}, u32[]{:S(2)}) copy-start(f32[1,256]{1,0:T(1,128)S(1)} %get-tuple-element.1189) | copy-start | bytes 3076
  9.6 595.5 %copy-start.160 = (f32[1,256]{1,0:T(1,128)}, f32[1,256]{1,0:T(1,128)S(1)}, u32[]{:S(2)}) copy-start(f32[1,256]{1,0:T(1,128)S(1)} %get-tuple-element.1188) | copy-start | bytes 3076
  720.5 260.7 %reduce-scatter.67.cloned.1.call-start = ((), (), s32[]{:S(2)}) async-start(), calls=%async_computation.33 | async-start | bytes 147456 | tf_op jit(solution)/shard_map/reduce_scatter | solution.py:295
  801.6 181.2 %reduce-scatter.65.cloned.1.call-start = ((), (), s32[]{:S(2)}) async-start(), calls=%async_computation.32 | async-start | bytes 147456 | tf_op jit(solution)/shard_map/reduce_scatter | solution.py:295
  883.0 121.8 %reduce-scatter.63.cloned.1.call-start = ((), (), s32[]{:S(2)}) async-start(), calls=%async_computation.31 | async-start | bytes 442368 | tf_op jit(solution)/shard_map/reduce_scatter | solution.py:292
  886.9 181.5 %reduce-scatter.61.cloned.1.call-start = ((), (), s32[]{:S(2)}) async-start(), calls=%async_computation.30 | async-start | bytes 442368 | tf_op jit(solution)/shard_map/reduce_scatter | solution.py:292
  890.7 241.2 %reduce-scatter.59.cloned.1.call-start = ((), (), s32[]{:S(2)}) async-start(), calls=%async_computation.29 | async-start | bytes 442368 | tf_op jit(solution)/shard_map/reduce_scatter | solution.py:292
  935.4 260.8 %reduce-scatter.81.cloned.1.call-start = ((), (), s32[]{:S(2)}) async-start(), calls=%async_computation.40 | async-start | bytes 589824 | tf_op jit(solution)/shard_map/reduce_scatter | solution.py:301
  942.0 318.9 %reduce-scatter.79.cloned.1.call-start = ((), (), s32[]{:S(2)}) async-start(), calls=%async_computation.39 | async-start | bytes 589824 | tf_op jit(solution)/shard_map/reduce_scatter | solution.py:301
  948.2 376.9 %reduce-scatter.77.cloned.1.call-start = ((), (), s32[]{:S(2)}) async-start(), calls=%async_computation.38 | async-start | bytes 589824 | tf_op jit(solution)/shard_map/reduce_scatter | solution.py:301
  955.2 434.5 %reduce-scatter.57.cloned.1.call-start = ((), (), s32[]{:S(2)}) async-start(), calls=%async_computation.28 | async-start | bytes 589824 | tf_op jit(solution)/shard_map/reduce_scatter | solution.py:321
  961.2 492.7 %reduce-scatter.103.cloned.1.call-start = ((), (), s32[]{:S(2)}) async-start(), calls=%async_computation.51 | async-start | bytes 589824
  967.3 551.2 %reduce-scatter.101.cloned.1.call-start = ((), (), s32[]{:S(2)}) async-start(), calls=%async_computation.50 | async-start | bytes 589824
  973.4 609.4 %reduce-scatter.99.cloned.1.call-start = ((), (), s32[]{:S(2)}) async-start(), calls=%async_computation.49 | async-start | bytes 589824
  979.5 540.7 %copy-start.42 = (f32[16,48,32]{1,2,0:T(8,128)S(1)}, f32[16,48,32]{1,2,0:T(8,128)}, u32[]{:S(2)}) copy-start(f32[16,48,32]{1,2,0:T(8,128)} %copy-done.41) | copy-start | bytes 294916
  979.5 624.8 %reduce-scatter.97.cloned.1.call-start = ((), (), s32[]{:S(2)}) async-start(), calls=%async_computation.48 | async-start | bytes 81920
  981.1 645.5 %reduce-scatter.95.cloned.1.call-start = ((), (), s32[]{:S(2)}) async-start(), calls=%async_computation.47 | async-start | bytes 81920
  982.6 665.8 %reduce-scatter.93.cloned.1.call-start = ((), (), s32[]{:S(2)}) async-start(), calls=%async_computation.46 | async-start | bytes 81920
  984.2 686.5 %reduce-scatter.91.cloned.1.call-start = ((), (), s32[]{:S(2)}) async-start(), calls=%async_computation.45 | async-start | bytes 81920
  1006.4 686.8 %reduce-scatter.89.cloned.1.call-start = ((), (), s32[]{:S(2)}) async-start(), calls=%async_computation.44 | async-start | bytes 81920
  1069.9 645.7 %reduce-scatter.87.cloned.1.call-start = ((), (), s32[]{:S(2)}) async-start(), calls=%async_computation.43 | async-start | bytes 81920
  1133.4 647.7 %reduce-scatter.111.cloned.1.call-start = ((), (), s32[]{:S(2)}) async-start(), calls=%async_computation.55 | async-start | bytes 589824
  1134.3 911.7 %copy-start.198 = (f32[128]{0:T(128)S(1)}, f32[128]{0:T(128)}, u32[]{:S(2)}) copy-start(f32[128]{0:T(128)} %param.53) | copy-start | bytes 1540
  1134.3 912.3 %copy-start.199 = (f32[64]{0:T(128)S(1)}, f32[64]{0:T(128)}, u32[]{:S(2)}) copy-start(f32[64]{0:T(128)} %param.63) | copy-start | bytes 772
  1134.4 912.9 %copy-start.182 = (f32[3,64]{1,0:T(4,128)S(1)}, f32[3,64]{1,0:T(4,128)}, u32[]{:S(2)}) copy-start(f32[3,64]{1,0:T(4,128)} %param.57) | copy-start | bytes 2308
  1134.4 913.1 %copy-start.183 = (f32[3,64]{1,0:T(4,128)S(1)}, f32[3,64]{1,0:T(4,128)}, u32[]{:S(2)}) copy-start(f32[3,64]{1,0:T(4,128)} %param.59) | copy-start | bytes 2308
  1134.4 913.2 %copy-start.184 = (f32[3,64]{1,0:T(4,128)S(1)}, f32[3,64]{1,0:T(4,128)}, u32[]{:S(2)}) copy-start(f32[3,64]{1,0:T(4,128)} %param.55) | copy-start | bytes 2308
  1134.4 913.3 %copy-start.185 = (f32[3,128]{1,0:T(4,128)S(1)}, f32[3,128]{1,0:T(4,128)}, u32[]{:S(2)}) copy-start(f32[3,128]{1,0:T(4,128)} %param.61) | copy-start | bytes 4612
  1134.4 960.0 %copy-start.200 = (f32[64]{0:T(128)S(1)}, f32[64]{0:T(128)}, u32[]{:S(2)}) copy-start(f32[64]{0:T(128)} %param.54) | copy-start | bytes 772
  1134.4 962.1 %copy-start.187 = (f32[3,96]{1,0:T(4,128)S(1)}, f32[3,96]{1,0:T(4,128)}, u32[]{:S(2)}) copy-start(f32[3,96]{1,0:T(4,128)} %param.56) | copy-start | bytes 3460
  1135.4 962.0 %copy-start.188 = (f32[3,64]{1,0:T(4,128)S(1)}, f32[3,64]{1,0:T(4,128)}, u32[]{:S(2)}) copy-start(f32[3,64]{1,0:T(4,128)} %param.62) | copy-start | bytes 2308
  1135.5 666.6 %reduce-scatter.109.cloned.1.call-start = ((), (), s32[]{:S(2)}) async-start(), calls=%async_computation.54 | async-start | bytes 81920
  1197.8 626.3 %reduce-scatter.107.cloned.1.call-start = ((), (), s32[]{:S(2)}) async-start(), calls=%async_computation.53 | async-start | bytes 81920
  1262.4 583.5 %reduce-scatter.105.cloned.1.call-start = ((), (), s32[]{:S(2)}) async-start(), calls=%async_computation.52 | async-start | bytes 81920
  1326.7 773.1 %copy-start.201 = (f32[128]{0:T(128)S(1)}, f32[128]{0:T(128)}, u32[]{:S(2)}) copy-start(f32[128]{0:T(128)} %param.64) | copy-start | bytes 1540
  1326.8 773.1 %copy-start.189 = (f32[3,32]{1,0:T(4,128)S(1)}, f32[3,32]{1,0:T(4,128)}, u32[]{:S(2)}) copy-start(f32[3,32]{1,0:T(4,128)} %param.58) | copy-start | bytes 1156
  1326.8 773.2 %copy-start.190 = (f32[3,128]{1,0:T(4,128)S(1)}, f32[3,128]{1,0:T(4,128)}, u32[]{:S(2)}) copy-start(f32[3,128]{1,0:T(4,128)} %param.60) | copy-start | bytes 4612
  1326.8 773.8 %copy-start.171 = (f32[7,256]{1,0:T(8,128)S(1)}, f32[7,256]{1,0:T(8,128)}, u32[]{:S(2)}) copy-start(f32[7,256]{1,0:T(8,128)} %param.65) | copy-start | bytes 21508
  1326.8 541.6 %reduce-scatter.85.cloned.1.call-start = ((), (), s32[]{:S(2)}) async-start(), calls=%async_computation.42 | async-start | bytes 81920
  1391.3 499.0 %reduce-scatter.75.cloned.1.call-start = ((), (), s32[]{:S(2)}) async-start(), calls=%async_computation.37 | async-start | bytes 81920 | tf_op jit(solution)/shard_map/reduce_scatter | solution.py:312
  1455.5 646.5 %copy-start.110 = (f32[3,64,128]{2,1,0:T(8,128)S(1)}, f32[3,64,128]{2,1,0:T(8,128)}, u32[]{:S(2)}) copy-start(f32[3,64,128]{2,1,0:T(8,128)} %param.49) | copy-start | bytes 294916
  1455.6 456.6 %reduce-scatter.73.cloned.1.call-start = ((), (), s32[]{:S(2)}) async-start(), calls=%async_computation.36 | async-start | bytes 81920 | tf_op jit(solution)/shard_map/reduce_scatter | solution.py:312
  1520.1 413.8 %reduce-scatter.71.cloned.1.call-start = ((), (), s32[]{:S(2)}) async-start(), calls=%async_computation.35 | async-start | bytes 81920 | tf_op jit(solution)/shard_map/reduce_scatter | solution.py:312
  1520.2 582.6 %copy-start.120 = (f32[64,128]{1,0:T(8,128)S(1)}, f32[64,128]{1,0:T(8,128)}, u32[]{:S(2)}) copy-start(f32[64,128]{1,0:T(8,128)} %param.51) | copy-start | bytes 98308
  1584.4 372.1 %reduce-scatter.83.cloned.1.call-start = ((), (), s32[]{:S(2)}) async-start(), calls=%async_computation.41 | async-start | bytes 81920 | tf_op jit(solution)/shard_map/reduce_scatter | solution.py:332
  (220 other events, 11720.6 us)
Sparse Core Ops, SparseCore 0:
  720.6 58.1 reduce-scatter.68
  801.7 58.1 reduce-scatter.66
  883.1 58.1 reduce-scatter.64
  944.4 60.3 reduce-scatter.62
  1007.9 60.3 reduce-scatter.60
  1071.5 60.3 reduce-scatter.58
  1135.2 60.8 reduce-scatter.80
  1199.9 60.9 reduce-scatter.78
  1264.2 60.9 reduce-scatter.76
  1328.7 60.8 reduce-scatter.56
  1393.0 60.9 reduce-scatter.102
  1457.5 60.9 reduce-scatter.100
  1521.8 60.8 reduce-scatter.98
  1585.8 18.4 reduce-scatter.96
  1607.1 19.4 reduce-scatter.94
  1629.0 19.4 reduce-scatter.92
  1651.3 19.4 reduce-scatter.90
  1673.7 19.4 reduce-scatter.88
  1696.2 19.4 reduce-scatter.86
  1719.2 61.9 reduce-scatter.110
  1783.5 18.4 reduce-scatter.108
  1804.6 19.4 reduce-scatter.106
  1826.5 19.4 reduce-scatter.104
  1848.9 19.4 reduce-scatter.84
  1870.8 19.4 reduce-scatter.74
  1892.7 19.4 reduce-scatter.72
  1914.4 19.4 reduce-scatter.70
  1937.0 19.4 reduce-scatter.82
where the time goes:
time: 2120 us; the launch traced here: 2110 us
  waiting for transfers between devices  933 us (44%)
  blocking collectives  621 us (29%)
  local copies, waits for them, and re-layouts  280 us (13%)
  matrix products  185 us (9%)
  other arithmetic  60.7 us (3%)
  between operations  28.9 us (1%)
    unnamed x42, waiting for transfers between devices  458 us
    reduce_scatter x3, waiting for transfers between devices, shards(): lax.psum_scatter(term_down.astype(jnp.bfloat16), 'dp', scatter_dimension=...  186 us
    reduce_scatter x3, waiting for transfers between devices, shards(): lax.psum_scatter(term_qkv.astype(jnp.bfloat16), 'dp', scatter_dimension=1...  144 us
    all_gather x3, blocking collectives, fetch_layer(): lax.all_gather(piece_qkv, 'dp', axis=1, tiled=True)  97.3 us
    all_gather x3, blocking collectives, fetch_layer(): lax.all_gather(piece_out, 'dp', axis=1, tiled=True)  96.2 us
    all_gather x3, blocking collectives, fetch_layer(): lax.all_gather(piece_down, 'dp', axis=0, tiled=True)  86.4 us
    all_gather x3, blocking collectives, fetch_layer(): lax.all_gather(piece_up, 'dp', axis=1, tiled=True)  85.5 us
    psum x2, blocking collectives, shards(): lax.psum((loss_local, count_local), ('dp', 'fsdp'))  78.6 us
  transfers between devices with their start and end apart: 28, of which 25 were waited for; matrix products, arithmetic and copies ran while one was open for 13% of the time, Pallas kernels for 0%

commit v1 on v0

v1 whole, which is shorter than its diff:
```python
import jax
import jax.numpy as jnp
from jax import lax
from jax.sharding import PartitionSpec as P

D = 256
HEADS = 8
FF = 1024
CATS = 32
CLASSES = 32
LAYERS = 3
SEG = 48
MEM = 48
CTX = 96
VOCAB = 1024


decay_two = 0.9
step_rate = 0.3
clip_limit = 0.05
tiny_term = 1e-30
norm_eps = 1e-06
masked_score = -1e30


def matmul(left, right):
    return jnp.dot(left, right, preferred_element_type=jnp.float32)


def matmul_tn(left, right):
    return lax.dot_general(
        left, right, (((0,), (0,)), ((), ())), preferred_element_type=jnp.float32
    )


def matmul_nt(left, right):
    return lax.dot_general(
        left, right, (((1,), (1,)), ((), ())), preferred_element_type=jnp.float32
    )


def rms_norm(values, gain_row):
    return (
        values * lax.rsqrt(jnp.mean(values * values, axis=-1, keepdims=True) + norm_eps) * gain_row
    )


def in_blocks(array, block):
    return array.reshape((array.shape[0] // block, block) + array.shape[1:])


def split_qkv(qkv, samples, block):
    heads_of = [
        qkv[:, start * D : (start + 1) * D].reshape(samples, CTX, HEADS, D // HEADS)
        for start in range(3)
    ]
    return [in_blocks(piece, block) for piece in heads_of]


def block_scores(queries, key_rows, allowed):
    scores = jnp.einsum("bqhd,bkhd->bhqk", queries, key_rows, preferred_element_type=jnp.float32)
    return jnp.where(allowed, scores * queries.shape[-1] ** (-0.5), masked_score)


def attend_block(inputs):
    queries, key_rows, value_rows, allowed = inputs
    scores = block_scores(queries, key_rows, allowed)
    peak_score = jnp.max(scores, axis=-1, keepdims=True)
    exponent = jnp.exp(scores - peak_score)
    total = jnp.sum(exponent, axis=-1, keepdims=True)
    probability = (exponent / total).astype(jnp.bfloat16)
    mixture = jnp.einsum(
        "bhqk,bkhd->bqhd", probability, value_rows, preferred_element_type=jnp.float32
    )
    return (mixture, peak_score[..., 0] + jnp.log(total[..., 0]))


def attend_back(inputs):
    queries, key_rows, value_rows, allowed, upstream, log_total = inputs
    scale_factor = queries.shape[-1] ** (-0.5)
    probability = jnp.exp(block_scores(queries, key_rows, allowed) - log_total[..., None])
    dprob = jnp.einsum("bqhd,bkhd->bhqk", upstream, value_rows, preferred_element_type=jnp.float32)
    dscore = (probability * (dprob - jnp.sum(probability * dprob, axis=-1, keepdims=True))).astype(
        jnp.bfloat16
    )
    dvalues = jnp.einsum(
        "bhqk,bqhd->bkhd",
        probability.astype(jnp.bfloat16),
        upstream,
        preferred_element_type=jnp.float32,
    )
    dqueries = (
        jnp.einsum("bhqk,bkhd->bqhd", dscore, key_rows, preferred_element_type=jnp.float32)
        * scale_factor
    )
    dkeys = (
        jnp.einsum("bhqk,bqhd->bkhd", dscore, queries, preferred_element_type=jnp.float32)
        * scale_factor
    )
    return (dqueries, dkeys, dvalues)


def attention(qkv, allowed):
    samples = allowed.shape[0]
    block = min(samples, 8)
    queries, key_rows, value_rows = split_qkv(qkv, samples, block)
    mixture, log_total = lax.map(
        attend_block, (queries, key_rows, value_rows, in_blocks(allowed, block))
    )
    return (mixture.reshape(samples * CTX, D), log_total)


def attention_back(qkv, allowed, upstream, log_total):
    samples = allowed.shape[0]
    block = min(samples, 8)
    queries, key_rows, value_rows = split_qkv(qkv, samples, block)
    upstream_blocks = in_blocks(upstream.reshape(samples, CTX, HEADS, D // HEADS), block)
    dqueries, dkeys, dvalues = lax.map(
        attend_back,
        (queries, key_rows, value_rows, in_blocks(allowed, block), upstream_blocks, log_total),
    )
    return jnp.concatenate(
        [
            dqueries.reshape(samples * CTX, D),
            dkeys.reshape(samples * CTX, D),
            dvalues.reshape(samples * CTX, D),
        ],
        axis=1,
    )


def layer_forward(hidden, w_qkv, w_out, w_up, w_down, gain_att, gain_ffn, allowed):
    normed, att_pull = jax.vjp(rms_norm, hidden, gain_att)
    normed_low = normed.astype(jnp.bfloat16)
    qkv = matmul(normed_low, w_qkv).astype(jnp.bfloat16)
    mixture, log_total = attention(qkv, allowed)
    mixture = mixture.astype(jnp.bfloat16)
    middle = hidden + matmul(mixture, w_out)
    normed_two, ffn_pull = jax.vjp(rms_norm, middle, gain_ffn)
    normed_two = normed_two.astype(jnp.bfloat16)
    inner_act, gelu_pull = jax.vjp(jax.nn.gelu, matmul(normed_two, w_up))
    activated = inner_act.astype(jnp.bfloat16)
    output = middle + matmul(activated, w_down)
    return (
        output,
        (att_pull, normed_low, qkv, mixture, log_total, ffn_pull, normed_two, gelu_pull, activated),
    )


def layer_backward(saved, w_qkv, w_out, w_up, w_down, allowed, upstream):
    att_pull, normed_low, qkv, mixture, log_total, ffn_pull, normed_two, gelu_pull, activated = (
        saved
    )
    dout = upstream.astype(jnp.bfloat16)
    grad_down = matmul_tn(dout, activated)
    dinner = gelu_pull(matmul_nt(dout, w_down))[0].astype(jnp.bfloat16)
    grad_up = matmul_tn(normed_two, dinner)
    dmiddle_norm, dgain_ffn = ffn_pull(matmul_nt(dinner, w_up))
    dmiddle = upstream + dmiddle_norm
    dattend = dmiddle.astype(jnp.bfloat16)
    grad_out = matmul_tn(mixture, dattend)
    dmixture = matmul_nt(dattend, w_out).astype(jnp.bfloat16)
    dqkv = attention_back(qkv, allowed, dmixture, log_total).astype(jnp.bfloat16)
    grad_qkv = matmul_tn(normed_low, dqkv)
    dhidden_norm, dgain_att = att_pull(matmul_nt(dqkv, w_qkv))
    return (dmiddle + dhidden_norm, (grad_qkv, grad_out, grad_up, grad_down), dgain_att, dgain_ffn)


def axis_bits(axis):
    return [1 << bit for bit in range(lax.axis_size(axis).bit_length() - 1)]


def swap(value, axis, bit):
    pairs = [(place, place ^ bit) for place in range(lax.axis_size(axis))]
    return lax.ppermute(value, axis, pairs)


def gather_pieces(piece):
    outer = lax.axis_size("dp").bit_length() - 1
    inner = lax.axis_size("fsdp").bit_length() - 1
    held = piece.reshape((1,) * (outer + inner) + piece.shape)
    order = [("dp", bit) for bit in reversed(range(outer))] + [
        ("fsdp", bit) for bit in reversed(range(inner))
    ]
    for place, (axis, bit) in enumerate(order):
        other = swap(held, axis, 1 << bit)
        upper = (lax.axis_index(axis) >> bit) & 1 == 1
        held = jnp.where(
            upper,
            jnp.concatenate([other, held], axis=place),
            jnp.concatenate([held, other], axis=place),
        )
    return held.reshape((lax.axis_size("dp"), lax.axis_size("fsdp")) + piece.shape)


def scatter_pieces(blocks):
    outer = lax.axis_size("dp").bit_length() - 1
    inner = lax.axis_size("fsdp").bit_length() - 1
    rows, columns = blocks.shape[2:]
    held = blocks.reshape((2,) * (outer + inner) + (rows, columns))
    order = [("dp", bit) for bit in reversed(range(outer))] + [
        ("fsdp", bit) for bit in reversed(range(inner))
    ]
    places = {item: place for place, item in enumerate(order)}
    for axis, bit in [("fsdp", bit) for bit in range(inner)] + [("dp", bit) for bit in range(outer)]:
        place = places[(axis, bit)]
        upper = (lax.axis_index(axis) >> bit) & 1 == 1
        low = lax.slice_in_dim(held, 0, 1, axis=place)
        high = lax.slice_in_dim(held, 1, 2, axis=place)
        other = swap(jnp.where(upper, low, high).astype(jnp.bfloat16), axis, 1 << bit)
        held = jnp.where(upper, high, low) + other.astype(jnp.float32)
    return held.reshape(rows, columns)


def sum_over(value, axis):
    terms = [value] + [swap(value, axis, step) for step in range(1, lax.axis_size(axis))]
    while len(terms) > 1:
        terms = [terms[at] + terms[at + 1] for at in range(0, len(terms), 2)]
    return terms[0]


def flat(items):
    return jnp.concatenate([item.reshape(-1) for item in items])


def unflat(vector, items):
    found, at = [], 0
    for item in items:
        found.append(vector[at : at + item.size].reshape(item.shape))
        at += item.size
    return found


def spread_columns(gathered, start, stop):
    part = gathered[:, :, :, start:stop]
    return part.transpose(1, 2, 0, 3).reshape(-1, part.shape[0] * (stop - start))


def block_columns(matrix):
    outer, inner = lax.axis_size("dp"), lax.axis_size("fsdp")
    return matrix.reshape(inner, matrix.shape[0] // inner, outer, -1).transpose(2, 0, 1, 3)


def shards(
    latents,
    targets,
    horizon,
    memory_valid,
    embed,
    qkv_weight,
    out_weight,
    up_weight,
    down_weight,
    head_weight,
    gains,
    embed_rows,
    embed_cols,
    qkv_rows,
    qkv_cols,
    out_rows,
    out_cols,
    up_rows,
    up_cols,
    down_rows,
    down_cols,
    head_rows,
    head_cols,
    gain_second,
):
    samples = latents.shape[0]
    layer_parts = [
        jnp.concatenate(
            [qkv_weight[at], out_weight[at], up_weight[at], down_weight[at].T], axis=1
        ).astype(jnp.bfloat16)
        for at in range(LAYERS)
    ]
    table_part = jnp.concatenate([embed.T, head_weight], axis=1).astype(jnp.bfloat16)
    widths = [qkv_weight.shape[2], out_weight.shape[2], up_weight.shape[2], down_weight.shape[1]]
    cuts = [0, widths[0], sum(widths[:2]), sum(widths[:3]), sum(widths)]
    table_cut = embed.shape[0]
    tables = gather_pieces(table_part)
    embed_full = spread_columns(tables, 0, table_cut).T
    head_full = spread_columns(tables, table_cut, 2 * table_cut)
    layer_weights = []
    for at in range(LAYERS):
        gathered = gather_pieces(layer_parts[at])
        pieces = [spread_columns(gathered, cuts[which], cuts[which + 1]) for which in range(4)]
        layer_weights.append((pieces[0], pieces[1], pieces[2], pieces[3].T))

    classes = jnp.arange(CLASSES, dtype=jnp.int32)
    one_hot = (latents[..., None] == classes).astype(jnp.bfloat16).reshape(samples * CTX, VOCAB)
    positions = jnp.arange(CTX, dtype=jnp.int32)
    causal = positions[None, :] <= positions[:, None]
    crosses = (positions[:, None] >= MEM) & (positions[None, :] < MEM)
    allowed = causal[None, None] & jnp.logical_not(
        crosses[None, None] & (memory_valid[:, None, None, None] == 0)
    )
    hidden = matmul(one_hot, embed_full)
    saved = []
    for layer_at in range(LAYERS):
        hidden, kept = layer_forward(
            hidden, *layer_weights[layer_at], gains[layer_at], gains[LAYERS + layer_at], allowed
        )
        saved.append(kept)
    latest = hidden.reshape(samples, CTX, D)[:, MEM:].reshape(samples * SEG, D)
    final, final_pull = jax.vjp(rms_norm, latest, gains[2 * LAYERS])
    final_low = final.astype(jnp.bfloat16)
    logits = matmul(final_low, head_full).reshape(samples, SEG, CATS, CLASSES)
    peak_logit = jnp.max(logits, axis=-1, keepdims=True)
    shifted = jnp.exp(logits - peak_logit)
    total = jnp.sum(shifted, axis=-1, keepdims=True)
    log_total = peak_logit[..., 0] + jnp.log(total[..., 0])
    target_hot = targets[..., None] == classes
    chosen = jnp.sum(jnp.where(target_hot, logits, 0.0), axis=-1)
    counted = jnp.arange(SEG, dtype=jnp.int32)[None, :] < horizon[:, None]
    per_position = jnp.sum(log_total - chosen, axis=-1)
    loss_local = jnp.sum(jnp.where(counted, per_position, 0.0))
    count_local = jnp.sum(horizon).astype(jnp.float32)
    dlogits = (shifted / total - target_hot.astype(jnp.float32)) * counted[:, :, None, None].astype(
        jnp.float32
    )
    dlogits = dlogits.reshape(samples * SEG, VOCAB).astype(jnp.bfloat16)
    head_term = matmul_tn(final_low, dlogits)
    dlatest, dgain_final = final_pull(matmul_nt(dlogits, head_full))
    upstream = jnp.concatenate(
        [jnp.zeros((samples, MEM, D), jnp.float32), dlatest.reshape(samples, SEG, D)], axis=1
    )
    upstream = upstream.reshape(samples * CTX, D)
    layer_raws = [None] * LAYERS
    att_terms = [None] * LAYERS
    ffn_terms = [None] * LAYERS
    for layer_at in reversed(range(LAYERS)):
        upstream, terms, att_terms[layer_at], ffn_terms[layer_at] = layer_backward(
            saved[layer_at], *layer_weights[layer_at], allowed, upstream
        )
        layer_raws[layer_at] = scatter_pieces(
            jnp.concatenate([block_columns(term) for term in terms], axis=3)
        )
    embed_term = matmul_tn(upstream.astype(jnp.bfloat16), one_hot)
    table_raw = scatter_pieces(
        jnp.concatenate([block_columns(embed_term), block_columns(head_term)], axis=3)
    )
    gain_local = jnp.stack(att_terms + ffn_terms + [dgain_final])

    raws = [jnp.stack([raw[:, cuts[at] : cuts[at + 1]] for raw in layer_raws]) for at in range(4)]
    raws = raws + [table_raw[:, :table_cut], table_raw[:, table_cut:]]
    masters = [
        qkv_weight,
        out_weight,
        up_weight,
        down_weight.transpose(0, 2, 1),
        embed.T,
        head_weight,
    ]
    inner_old = [qkv_rows, out_rows, up_rows, down_cols, embed_cols, head_rows]
    outer_old = [qkv_cols, out_cols, up_cols, down_rows, embed_rows, head_cols]
    inner_is_row = [True, True, True, False, False, True]
    inner_part = [jnp.sum(raw * raw, axis=-1) for raw in raws]
    outer_part = [jnp.sum(raw * raw, axis=-2) for raw in raws]
    weight_square = [jnp.sum(master * master, axis=(-2, -1)) for master in masters]
    outer_row_sums = [
        jnp.sum(outer_old[at], axis=-1) for at in range(6) if not inner_is_row[at]
    ]
    inner_row_sums = [jnp.sum(inner_old[at], axis=-1) for at in range(6) if inner_is_row[at]]
    scalars = [loss_local, jnp.sum(horizon).astype(jnp.float32)]
    first = inner_part + outer_row_sums + weight_square + scalars + [gain_local]
    first_sum = unflat(sum_over(flat(first), "dp"), first)
    inner_global, first_sum = first_sum[:6], first_sum[6:]
    outer_row_sums, first_sum = first_sum[:2], first_sum[2:]
    entry_square = [jnp.sum(part, axis=-1) for part in inner_global]
    second = outer_part + inner_row_sums + entry_square + first_sum
    second_sum = unflat(sum_over(flat(second), "fsdp"), second)
    outer_global, second_sum = second_sum[:6], second_sum[6:]
    inner_row_sums, second_sum = second_sum[:4], second_sum[4:]
    entry_square, second_sum = second_sum[:6], second_sum[6:]
    weight_total, second_sum = second_sum[:6], second_sum[6:]
    loss_total, count_total, gain_sum = second_sum
    row_sums = inner_row_sums[:3] + outer_row_sums + inner_row_sums[3:]

    square_total = jnp.sum(gain_sum * gain_sum)
    for part in entry_square:
        square_total = square_total + jnp.sum(part)
    norm_value = jnp.sqrt(square_total) / count_total
    scaling = jnp.minimum(1.0, clip_limit / norm_value) / count_total
    found = []
    for at in range(6):
        inner_length = masters[at].shape[-2] * lax.axis_size("fsdp")
        outer_length = masters[at].shape[-1] * lax.axis_size("dp")
        row_length = inner_length if inner_is_row[at] else outer_length
        entries = inner_length * outer_length
        square_scale = scaling * scaling
        inner_new = decay_two * inner_old[at] + (1 - decay_two) * (
            square_scale * inner_global[at] / outer_length + tiny_term
        )
        outer_new = decay_two * outer_old[at] + (1 - decay_two) * (
            square_scale * outer_global[at] / inner_length + tiny_term
        )
        mean_rows = decay_two * (row_sums[at] / row_length) + (1 - decay_two) * (
            square_scale * entry_square[at] / entries + tiny_term
        )
        spread = jnp.sqrt(weight_total[at] / entries)
        grad = raws[at] * scaling
        scale_of = (step_rate * spread * jnp.sqrt(mean_rows))[..., None, None]
        updated = masters[at] - scale_of * grad * (
            lax.rsqrt(inner_new)[..., :, None] * lax.rsqrt(outer_new)[..., None, :]
        )
        found.append((updated, grad, inner_new, outer_new))
    results = [loss_total, count_total, norm_value]
    for at in [4, 0, 1, 2, 3, 5]:
        updated, grad, inner_new, outer_new = found[at]
        if inner_is_row[at]:
            results = results + [updated, grad, inner_new, outer_new]
        else:
            turned = [jnp.swapaxes(item, -1, -2) for item in (updated, grad)]
            results = results + turned + [outer_new, inner_new]
    gain_grad = gain_sum * scaling
    gain_second_new = decay_two * gain_second + (1 - decay_two) * (
        gain_grad * gain_grad + tiny_term
    )
    gains_new = gains - step_rate * jnp.sqrt(
        jnp.mean(gains * gains, axis=-1, keepdims=True)
    ) * gain_grad * lax.rsqrt(gain_second_new)
    results = results + [gains_new, gain_grad, gain_second_new]
    return tuple(results)


def solution(mesh):
    return jax.shard_map(
        shards,
        mesh=mesh,
        in_specs=(
            P(("dp", "fsdp"), None, None),
            P(("dp", "fsdp"), None, None),
            P(("dp", "fsdp")),
            P(("dp", "fsdp")),
            P("dp", "fsdp"),
            P(None, "fsdp", "dp"),
            P(None, "fsdp", "dp"),
            P(None, "fsdp", "dp"),
            P(None, "dp", "fsdp"),
            P("fsdp", "dp"),
            P(),
            P("dp"),
            P("fsdp"),
            P(None, "fsdp"),
            P(None, "dp"),
            P(None, "fsdp"),
            P(None, "dp"),
            P(None, "fsdp"),
            P(None, "dp"),
            P(None, "dp"),
            P(None, "fsdp"),
            P("fsdp"),
            P("dp"),
            P(),
        ),
        out_specs=(
            P(),
            P(),
            P(),
            P("dp", "fsdp"),
            P("dp", "fsdp"),
            P("dp"),
            P("fsdp"),
            P(None, "fsdp", "dp"),
            P(None, "fsdp", "dp"),
            P(None, "fsdp"),
            P(None, "dp"),
            P(None, "fsdp", "dp"),
            P(None, "fsdp", "dp"),
            P(None, "fsdp"),
            P(None, "dp"),
            P(None, "fsdp", "dp"),
            P(None, "fsdp", "dp"),
            P(None, "fsdp"),
            P(None, "dp"),
            P(None, "dp", "fsdp"),
            P(None, "dp", "fsdp"),
            P(None, "dp"),
            P(None, "fsdp"),
            P("fsdp", "dp"),
            P("fsdp", "dp"),
            P("fsdp"),
            P("dp"),
            P(),
            P(),
            P(),
        ),
        check_vma=False,
    )
```

time: 2120 us -> 644 us (0.30)
  waiting for transfers between devices: 933 us -> 51.5 us
  blocking collectives: 621 us -> 0 us
  starting transfers between devices: 1.55 us -> 59.3 us
  matrix products: 185 us -> 138 us
  other arithmetic: 60.7 us -> 95.4 us
    all_gather x28 -> x0, blocking collectives: 495 us -> none  [the longest x3 97.3 us: fetch_layer(): lax.all_gather(piece_qkv, 'dp', axis=1, tiled=True)]
    reduce_scatter x14 -> x0, waiting for transfers between devices: 475 us -> none  [the longest x3 186 us: shards(): lax.psum_scatter(term_down.astype(jnp.bfloat16), 'dp', scatter_dimension=...]
    unnamed x42 -> x0, waiting for transfers between devices: 458 us -> none
    psum x4 -> x0, blocking collectives: 126 us -> none  [the longest x2 78.6 us: shards(): lax.psum((loss_local, count_local), ('dp', 'fsdp'))]
    ppermute x0 -> x50, starting transfers between devices: none -> 59.3 us  [swap(): return lax.ppermute(value, axis, pairs)]
    ppermute x0 -> x50, waiting for transfers between devices: none -> 51.5 us  [swap(): return lax.ppermute(value, axis, pairs)]
    unnamed x385 -> x364, local copies, waits for them, and re-layouts: 63.1 us -> 24.6 us
    transpose x0 -> x31, local copies, waits for them, and re-layouts: none -> 33.5 us  [the longest x24 24.9 us: spread_columns(): part.transpose(1, 2, 0, 3).reshape(-1, part.shape[0] * (stop - start))]
  transfers between devices with their start and end apart: 28 -> 50, of which waited for: 25 -> 20; matrix products, arithmetic and copies ran while one was open for 13% -> 16% of each run, Pallas kernels for 0% -> 0%
where the time goes in v1:
time: 644 us; the launch traced here: 635 us
  local copies, waits for them, and re-layouts  272 us (42%)
  matrix products  138 us (21%)
  other arithmetic  95.4 us (15%)
  starting transfers between devices  59.3 us (9%)
  waiting for transfers between devices  51.5 us (8%)
  between operations  16.7 us (3%)
    ppermute x50, starting transfers between devices, swap(): return lax.ppermute(value, axis, pairs)  59.3 us
    ppermute x50, waiting for transfers between devices, swap(): return lax.ppermute(value, axis, pairs)  51.5 us
    dot_general x13, matrix products, matmul_nt(): lax.dot_general(left, right, (((1,), (1,)), ((), ())), preferred_element_...  37.5 us
    dot_general x14, matrix products, matmul(): return jnp.dot(left, right, preferred_element_type=jnp.float32)  32.7 us
    dot_general x14, matrix products, matmul_tn(): lax.dot_general(left, right, (((0,), (0,)), ((), ())), preferred_element_...  30.9 us
    another operation x24, local copies, waits for them, and re-layouts  28 us
    transpose x24, local copies, waits for them, and re-layouts, spread_columns(): part.transpose(1, 2, 0, 3).reshape(-1, part.shape[0] * (stop - start))  24.9 us
    unnamed x364, local copies, waits for them, and re-layouts  24.6 us
  transfers between devices with their start and end apart: 50, of which 20 were waited for; matrix products, arithmetic and copies ran while one was open for 16% of the time, Pallas kernels for 0%

profile of v1, /device:TPU:0, one launch (start us, length us, event | category | flops | bytes accessed | tf_op | source)
XLA Modules:
  0.0 634.8 jit_solution(5445606282665248425)
XLA Ops:
  2.9 4.1 collective-permute-start
  10.6 3.0 collective-permute-start.10
  25.0 4.0 eq.50
  29.0 9.8 %eq.113 = s32[1536,1024]{0,1:T(8,128)} reshape(s32[16,96,32,32]{1,0,3,2:T(8,128)} %eq.50) | data formatting | bytes 12582912 | tf_op jit(solution)/shard_map/eq | solution.py:291
  39.1 4.3 broadcast_compare_fusion
  44.3 5.2 eq.53
  74.7 6.5 %collective-permute-done.8 = bf16[2,2,2,1,1,64,384]{6,5,4,3,2,1,0:T(8,128)(2,1)S(1)} collective-permute-done((bf16[2,2,2,1,1,64,384]{6,5,4,3,2,1,0:T(8,128)(2,1)S(1)}, bf16[2,2,2,1,1,64,384]{6,5,4,3,2,1,0:T(8,128)(2,1)S(1)}, u32[]{:S(2)}, u32[]{:S(2)}) %collective-permute-start.8) | collective-permute-done | bytes 393248 | tf_op jit(solution)/shard_map/ppermute | solution.py:175
  81.4 8.2 %collective-permute-done.13 = bf16[2,2,2,1,1,64,384]{6,5,0,1,2,4,3:T(8,128)(2,1)S(1)} collective-permute-done((bf16[2,2,2,1,1,64,384]{6,5,0,1,2,4,3:T(8,128)(2,1)S(1)}, bf16[2,2,2,1,1,64,384]{6,5,0,1,2,4,3:T(8,128)(2,1)S(1)}, u32[]{:S(2)}, u32[]{:S(2)}) %collective-permute-start.13) | collective-permute-done | bytes 393248 | tf_op jit(solution)/shard_map/ppermute | solution.py:175
  90.7 4.3 collective-permute-done.18
  129.6 8.0 %while.78 = (s32[]{:T(128)}, bf16[2,8,96,8,32]{2,4,3,1,0:T(8,128)(2,1)}, f32[2,8,8,96]{3,2,1,0:T(8,128)S(1)}, bf16[2,8,96,8,32]{2,4,3,1,0:T(8,128)(2,1)S(1)}, pr...) while((s32[]{:T(128)}, ...), condition=%wide.region_4.5_spmd, body=%wide.region_1.4_spmd.sunk | while | flops 82569216 | bytes 17172636 | solution.py:107
  137.6 3.7 copy.328
  141.3 3.1 convert_element_type.421
  166.9 8.4 %while.79 = (s32[]{:T(128)}, bf16[2,8,96,8,32]{2,4,3,1,0:T(8,128)(2,1)}, f32[2,8,8,96]{3,2,1,0:T(8,128)S(1)}, bf16[2,8,96,8,32]{2,4,3,1,0:T(8,128)(2,1)S(1)}, pr...) while((s32[]{:T(128)}, ...), condition=%wide.region_10.11_spmd, body=%wide.region_7.10_spmd.sunk | while | flops 82569216 | bytes 17172636 | solution.py:107
  175.3 3.7 copy.352
  179.0 3.0 convert_element_type.427
  204.6 8.2 %while.80 = (s32[]{:T(128)}, bf16[2,8,96,8,32]{2,4,3,1,0:T(8,128)(2,1)}, f32[2,8,8,96]{3,2,1,0:T(8,128)S(1)}, bf16[2,8,96,8,32]{2,4,3,1,0:T(8,128)(2,1)S(1)}, pr...) while((s32[]{:T(128)}, ...), condition=%wide.region_16.17_spmd, body=%wide.region_13.16_spmd.sunk | while | flops 82569216 | bytes 17172636 | solution.py:107
  215.7 3.0 convert_element_type.433
  222.4 4.9 fusion.158
  227.3 6.5 %copy.379 = f32[1536,1024]{1,0:T(8,128)} copy(f32[1536,1024]{0,1:T(8,128)} %get-tuple-element.881) | data formatting | bytes 12582912 | tf_op jit(solution)/shard_map/dot_general | solution.py:27
  236.0 6.8 %fusion.160 = f32[1536,256]{0,1:T(8,128)} fusion(f32[1536,256]{0,1:T(8,128)} %copy-done.30, f32[1536,1024]{1,0:T(8,128)} %copy.379, bf16[32,8,8,128]{3,2,1,0:T(8,128)(2,1)S(1)} %bitcast.1066), kind=kOutput, calls=%fused_computation.214 | convolution fusion | flops 819855360 | bytes 9961472 | tf_op jit(solution)/shard_map/dot_general | solution.py:27
  242.8 3.0 copy.382
  254.0 6.5 %select_reduce_fusion = (f32[16,48,32]{1,2,0:T(8,128)}, f32[16,48,32]{1,2,0:T(8,128)S(1)}) fusion(f32[16,48,32,32]{1,3,2,0:T(8,128)S(1)} %get-tuple-element.878, s32[16,48,32]{1,2,0:T(8,128)S(1)} %copy-done.106, f32[16,48,32]{1,2,0:T(8,128)S(1)} %get-tuple-element.877), kind=kLoop, calls=%fused_computation.166 | loop fusion | flops 3883008 | bytes 3538944 | tf_op jit(solution)/shard_map/reduce_sum | solution.py:314
  260.5 3.3 multiply_convert_fusion.3
  263.8 6.8 %copy.385 = bf16[16,48,32,32]{1,0,3,2:T(8,128)(2,1)} copy(bf16[16,48,32,32]{1,3,2,0:T(8,128)(2,1)S(1)} %multiply_convert_fusion.3) | data formatting | bytes 3145728 | tf_op jit(solution)/shard_map/convert_element_type | solution.py:322
  270.7 7.0 %convert_element_type.440 = bf16[768,1024]{0,1:T(8,128)(2,1)} reshape(bf16[16,48,32,32]{1,0,3,2:T(8,128)(2,1)} %copy.385) | data formatting | bytes 3145728 | tf_op jit(solution)/shard_map/convert_element_type | solution.py:322
  277.7 3.9 multiply_reduce_fusion.21
  282.6 7.0 %fusion.150 = bf16[1536,1024]{1,0:T(8,128)(2,1)S(1)} fusion(f32[1536,1024]{1,0:T(8,128)} %copy.379, bf16[1536,256]{1,0:T(8,128)(2,1)S(1)} %bitcast.1053, bf16[32,8,8,128]{3,2,1,0:T(8,128)(2,1)S(1)} %bitcast.1067), kind=kOutput, calls=%fused_computation.192 | convolution fusion | flops 836763648 | bytes 10747904 | tf_op jit(solution)/shard_map/dot_general | solution.py:37
  291.7 3.1 multiply_reduce_fusion.3
  297.0 3.1 copy.387
  300.8 4.0 fusion.339
  315.7 17.2 %while.81 = (s32[]{:T(128)}, bf16[2,8,96,8,32]{2,4,3,1,0:T(8,128)(2,1)}, bf16[2,8,96,8,32]{2,4,3,1,0:T(8,128)(2,1)}, bf16[2,8,96,8,32]{2,4,3,1,0:T(8,128)(2,1)},...) while((s32[]{:T(128)}, ...), condition=%wide.region_25.26_spmd, body=%wide.region_23.25_spmd.sunk | while | flops 194439168 | bytes 46124336 | solution.py:118
  348.2 3.5 fusion.318
  351.7 3.3 multiply_reduce_fusion.6
  355.5 3.3 convolution_bitcast_fusion.4
  358.8 5.0 fusion.143
  372.2 2.9 reshape_reshape.55
  378.7 17.5 %while.82 = (s32[]{:T(128)}, bf16[2,8,96,8,32]{2,4,3,1,0:T(8,128)(2,1)}, bf16[2,8,96,8,32]{2,4,3,1,0:T(8,128)(2,1)}, bf16[2,8,96,8,32]{2,4,3,1,0:T(8,128)(2,1)},...) while((s32[]{:T(128)}, ...), condition=%wide.region_30.31_spmd, body=%wide.region_28.30_spmd.sunk | while | flops 194439168 | bytes 46124336 | solution.py:118
  411.5 3.4 fusion.317
  418.2 3.3 convolution_bitcast_fusion.6
  421.5 5.0 fusion.136
  440.9 17.3 %while.83 = (s32[]{:T(128)}, bf16[2,8,96,8,32]{2,4,3,1,0:T(8,128)(2,1)}, bf16[2,8,96,8,32]{2,4,3,1,0:T(8,128)(2,1)}, bf16[2,8,96,8,32]{2,4,3,1,0:T(8,128)(2,1)},...) while((s32[]{:T(128)}, ...), condition=%wide.region_35.36_spmd, body=%wide.region_33.35_spmd.sunk | while | flops 194439168 | bytes 46124336 | solution.py:118
  473.3 3.6 fusion.316
  488.6 3.2 convolution_bitcast_fusion.2
  537.2 5.5 collective-permute-done.36
  560.4 6.7 %collective-permute-done.21 = bf16[2,2,2,1,1,64,384]{6,5,4,3,2,1,0:T(8,128)(2,1)S(1)} collective-permute-done((bf16[2,2,2,1,1,64,384]{6,5,4,3,2,1,0:T(8,128)(2,1)S(1)}, bf16[2,2,2,1,1,64,384]{6,5,4,3,2,1,0:T(8,128)(2,1)S(1)}, u32[]{:S(2)}, u32[]{:S(2)}) %collective-permute-start.21) | collective-permute-done | bytes 393248 | tf_op jit(solution)/shard_map/ppermute | solution.py:175
  570.2 3.1 collective-permute-done.22
  578.4 4.0 collective-permute-start.24
  592.9 3.3 collective-permute-start.44
  (997 shorter events, 425.2 us)
Async XLA Ops:
  2.9 48.5 %collective-permute-start = (bf16[1,1,1,1,1,64,256]{6,5,4,3,2,1,0:T(8,128)(2,1)S(1)}, bf16[1,1,1,1,1,64,256]{6,5,4,3,2,1,0:T(8,128)(2,1)S(1)}, u32[]{:S(2)}, u32[]{:S(2)}) collective-permute-start(bf16[1,1,1,1,1,64,256]{6,5,4,3,2,1,0:T(8,128)(2,1)S(1)} %pad_maximum_fusion.20), channel_id=1, source_target_pairs={{0,16},{4,20},{8,24},{12,28},{16,0},{20,4},{24,8},{28,12},{1,17},{... | collective-permute-start | bytes 98312 | tf_op jit(solution)/shard_map/ppermute | solution.py:175
  10.5 43.0 %collective-permute-start.5 = (bf16[1,1,1,1,1,64,384]{6,5,4,3,2,1,0:T(8,128)(2,1)S(1)}, bf16[1,1,1,1,1,64,384]{6,5,4,3,2,1,0:T(8,128)(2,1)S(1)}, u32[]{:S(2)}, u32[]{:S(2)}) collective-permute-start(bf16[1,1,1,1,1,64,384]{6,5,4,3,2,1,0:T(8,128)(2,1)S(1)} %pad_maximum_fusion.15), channel_id=1, source_target_pairs={{0,16},{4,20},{8,24},{12,28},{16,0},{20,4},{24,8},{28,12},{1,17},{... | collective-permute-start | bytes 147464 | tf_op jit(solution)/shard_map/ppermute | solution.py:175
  10.6 43.1 %collective-permute-start.10 = (bf16[1,1,1,1,1,64,384]{6,5,0,4,3,2,1:T(8,128)(2,1)S(1)}, bf16[1,1,1,1,1,64,384]{6,5,0,4,3,2,1:T(8,128)(2,1)S(1)}, u32[]{:S(2)}, u32[]{:S(2)}) collective-permute-start(bf16[1,1,1,1,1,64,384]{6,5,0,4,3,2,1:T(8,128)(2,1)S(1)} %maximum_bitcast_fusion.3), channel_id=1, source_target_pairs={{0,16},{4,20},{8,24},{12,28},{16,0},{20,4},{24,8},{28,12},{1,17},{... | collective-permute-start | bytes 147464 | tf_op jit(solution)/shard_map/ppermute | solution.py:175
  13.7 42.0 %collective-permute-start.15 = (bf16[1,1,1,1,1,64,384]{6,5,4,3,2,1,0:T(8,128)(2,1)S(1)}, bf16[1,1,1,1,1,64,384]{6,5,4,3,2,1,0:T(8,128)(2,1)S(1)}, u32[]{:S(2)}, u32[]{:S(2)}) collective-permute-start(bf16[1,1,1,1,1,64,384]{6,5,4,3,2,1,0:T(8,128)(2,1)S(1)} %pad_maximum_fusion.18), channel_id=1, source_target_pairs={{0,16},{4,20},{8,24},{12,28},{16,0},{20,4},{24,8},{28,12},{1,17},{... | collective-permute-start | bytes 147464 | tf_op jit(solution)/shard_map/ppermute | solution.py:175
  51.5 5.0 collective-permute-start.1
  53.5 5.8 collective-permute-start.6
  53.7 7.2 %collective-permute-start.11 = (bf16[2,1,1,1,1,64,384]{6,5,0,4,3,2,1:T(8,128)(2,1)S(1)}, bf16[2,1,1,1,1,64,384]{6,5,0,4,3,2,1:T(8,128)(2,1)S(1)}, u32[]{:S(2)}, u32[]{:S(2)}) collective-permute-start(bf16[2,1,1,1,1,64,384]{6,5,0,4,3,2,1:T(8,128)(2,1)S(1)} %bitcast_select_fusion.2), channel_id=1, source_target_pairs={{0,8},{4,12},{8,0},{12,4},{16,24},{20,28},{24,16},{28,20},{1,9},{5... | collective-permute-start | bytes 294920 | tf_op jit(solution)/shard_map/ppermute | solution.py:175
  55.7 6.4 %collective-permute-start.16 = (bf16[2,1,1,1,1,64,384]{6,5,4,3,2,1,0:T(8,128)(2,1)S(1)}, bf16[2,1,1,1,1,64,384]{6,5,4,3,2,1,0:T(8,128)(2,1)S(1)}, u32[]{:S(2)}, u32[]{:S(2)}) collective-permute-start(bf16[2,1,1,1,1,64,384]{6,5,4,3,2,1,0:T(8,128)(2,1)S(1)} %maximum_select_fusion.22), channel_id=1, source_target_pairs={{0,8},{4,12},{8,0},{12,4},{16,24},{20,28},{24,16},{28,20},{1,9},{5... | collective-permute-start | bytes 294920 | tf_op jit(solution)/shard_map/ppermute | solution.py:175
  56.5 6.9 %collective-permute-start.2 = (bf16[2,2,1,1,1,64,256]{6,5,1,0,4,3,2:T(8,128)(2,1)S(1)}, bf16[2,2,1,1,1,64,256]{6,5,1,0,4,3,2:T(8,128)(2,1)S(1)}, u32[]{:S(2)}, u32[]{:S(2)}) collective-permute-start(bf16[2,2,1,1,1,64,256]{6,5,1,0,4,3,2:T(8,128)(2,1)S(1)} %maximum_select_fusion.19), channel_id=1, source_target_pairs={{0,4},{4,0},{8,12},{12,8},{16,20},{20,16},{24,28},{28,24},{1,5},{5... | collective-permute-start | bytes 393224 | tf_op jit(solution)/shard_map/ppermute | solution.py:175
  59.3 7.9 %collective-permute-start.7 = (bf16[2,2,1,1,1,64,384]{6,5,1,0,4,3,2:T(8,128)(2,1)S(1)}, bf16[2,2,1,1,1,64,384]{6,5,1,0,4,3,2:T(8,128)(2,1)S(1)}, u32[]{:S(2)}, u32[]{:S(2)}) collective-permute-start(bf16[2,2,1,1,1,64,384]{6,5,1,0,4,3,2:T(8,128)(2,1)S(1)} %maximum_select_fusion.15), channel_id=1, source_target_pairs={{0,4},{4,0},{8,12},{12,8},{16,20},{20,16},{24,28},{28,24},{1,5},{5... | collective-permute-start | bytes 589832 | tf_op jit(solution)/shard_map/ppermute | solution.py:175
  60.9 10.1 %collective-permute-start.12 = (bf16[2,2,1,1,1,64,384]{6,5,0,4,3,2,1:T(8,128)(2,1)S(1)}, bf16[2,2,1,1,1,64,384]{6,5,0,4,3,2,1:T(8,128)(2,1)S(1)}, u32[]{:S(2)}, u32[]{:S(2)}) collective-permute-start(bf16[2,2,1,1,1,64,384]{6,5,0,4,3,2,1:T(8,128)(2,1)S(1)} %maximum_select_fusion.16), channel_id=1, source_target_pairs={{0,4},{4,0},{8,12},{12,8},{16,20},{20,16},{24,28},{28,24},{1,5},{5... | collective-permute-start | bytes 589832 | tf_op jit(solution)/shard_map/ppermute | solution.py:175
  62.2 10.9 %collective-permute-start.17 = (bf16[2,2,1,1,1,64,384]{6,5,0,4,3,2,1:T(8,128)(2,1)S(1)}, bf16[2,2,1,1,1,64,384]{6,5,0,4,3,2,1:T(8,128)(2,1)S(1)}, u32[]{:S(2)}, u32[]{:S(2)}) collective-permute-start(bf16[2,2,1,1,1,64,384]{6,5,0,4,3,2,1:T(8,128)(2,1)S(1)} %maximum_select_fusion.18), channel_id=1, source_target_pairs={{0,4},{4,0},{8,12},{12,8},{16,20},{20,16},{24,28},{28,24},{1,5},{5... | collective-permute-start | bytes 589832 | tf_op jit(solution)/shard_map/ppermute | solution.py:175
  63.5 11.1 %collective-permute-start.3 = (bf16[2,2,2,1,1,64,256]{6,5,4,3,2,1,0:T(8,128)(2,1)S(1)}, bf16[2,2,2,1,1,64,256]{6,5,4,3,2,1,0:T(8,128)(2,1)S(1)}, u32[]{:S(2)}, u32[]{:S(2)}) collective-permute-start(bf16[2,2,2,1,1,64,256]{6,5,4,3,2,1,0:T(8,128)(2,1)S(1)} %copy.305), channel_id=1, source_target_pairs={{0,2},{1,3},{2,0},{3,1},{4,6},{5,7},{6,4},{7,5},{8,10},{9,11},{10,... | collective-permute-start | bytes 786440 | tf_op jit(solution)/shard_map/ppermute | solution.py:175
  67.4 13.9 %collective-permute-start.8 = (bf16[2,2,2,1,1,64,384]{6,5,4,3,2,1,0:T(8,128)(2,1)S(1)}, bf16[2,2,2,1,1,64,384]{6,5,4,3,2,1,0:T(8,128)(2,1)S(1)}, u32[]{:S(2)}, u32[]{:S(2)}) collective-permute-start(bf16[2,2,2,1,1,64,384]{6,5,4,3,2,1,0:T(8,128)(2,1)S(1)} %copy.317), channel_id=1, source_target_pairs={{0,2},{1,3},{2,0},{3,1},{4,6},{5,7},{6,4},{7,5},{8,10},{9,11},{10,... | collective-permute-start | bytes 1179656 | tf_op jit(solution)/shard_map/ppermute | solution.py:175
  71.1 18.5 %collective-permute-start.13 = (bf16[2,2,2,1,1,64,384]{6,5,0,1,2,4,3:T(8,128)(2,1)S(1)}, bf16[2,2,2,1,1,64,384]{6,5,0,1,2,4,3:T(8,128)(2,1)S(1)}, u32[]{:S(2)}, u32[]{:S(2)}) collective-permute-start(bf16[2,2,2,1,1,64,384]{6,5,0,1,2,4,3:T(8,128)(2,1)S(1)} %copy.343), channel_id=1, source_target_pairs={{0,2},{1,3},{2,0},{3,1},{4,6},{5,7},{6,4},{7,5},{8,10},{9,11},{10,... | collective-permute-start | bytes 1179656 | tf_op jit(solution)/shard_map/ppermute | solution.py:175
  73.2 21.8 %collective-permute-start.18 = (bf16[2,2,2,1,1,64,384]{6,5,0,4,3,2,1:T(8,128)(2,1)S(1)}, bf16[2,2,2,1,1,64,384]{6,5,0,4,3,2,1:T(8,128)(2,1)S(1)}, u32[]{:S(2)}, u32[]{:S(2)}) collective-permute-start(bf16[2,2,2,1,1,64,384]{6,5,0,4,3,2,1:T(8,128)(2,1)S(1)} %maximum_select_fusion.12), channel_id=1, source_target_pairs={{0,2},{1,3},{2,0},{3,1},{4,6},{5,7},{6,4},{7,5},{8,10},{9,11},{10,... | collective-permute-start | bytes 1179656 | tf_op jit(solution)/shard_map/ppermute | solution.py:175
  74.7 20.6 %collective-permute-start.4 = (bf16[2,2,2,2,1,64,256]{6,5,4,3,2,1,0:T(8,128)(2,1)S(1)}, bf16[2,2,2,2,1,64,256]{6,5,4,3,2,1,0:T(8,128)(2,1)S(1)}, u32[]{:S(2)}, u32[]{:S(2)}) collective-permute-start(bf16[2,2,2,2,1,64,256]{6,5,4,3,2,1,0:T(8,128)(2,1)S(1)} %maximum_select_fusion.7), channel_id=1, source_target_pairs={{0,1},{1,0},{2,3},{3,2},{4,5},{5,4},{6,7},{7,6},{8,9},{9,8},{10,11... | collective-permute-start | bytes 1572872 | tf_op jit(solution)/shard_map/ppermute | solution.py:175
  81.3 20.3 %collective-permute-start.9 = (bf16[2,2,2,2,1,64,384]{6,5,4,3,2,1,0:T(8,128)(2,1)S(1)}, bf16[2,2,2,2,1,64,384]{6,5,4,3,2,1,0:T(8,128)(2,1)}, u32[]{:S(2)}, u32[]{:S(2)}) collective-permute-start(bf16[2,2,2,2,1,64,384]{6,5,4,3,2,1,0:T(8,128)(2,1)S(1)} %maximum_select_fusion.4), channel_id=1, source_target_pairs={{0,1},{1,0},{2,3},{3,2},{4,5},{5,4},{6,7},{7,6},{8,9},{9,8},{10,11... | collective-permute-start | bytes 2359304 | tf_op jit(solution)/shard_map/ppermute | solution.py:175
  90.7 14.3 %collective-permute-start.14 = (bf16[2,2,2,2,1,64,384]{6,5,0,1,2,4,3:T(8,128)(2,1)}, bf16[2,2,2,2,1,64,384]{6,5,0,1,2,4,3:T(8,128)(2,1)}, u32[]{:S(2)}, u32[]{:S(2)}) collective-permute-start(bf16[2,2,2,2,1,64,384]{6,5,0,1,2,4,3:T(8,128)(2,1)} %maximum_select_fusion.5), channel_id=1, source_target_pairs={{0,1},{1,0},{2,3},{3,2},{4,5},{5,4},{6,7},{7,6},{8,9},{9,8},{10,11... | collective-permute-start | bytes 2359304 | tf_op jit(solution)/shard_map/ppermute | solution.py:175
  95.1 16.7 %collective-permute-start.19 = (bf16[2,2,2,2,1,64,384]{6,5,0,1,2,4,3:T(8,128)(2,1)S(1)}, bf16[2,2,2,2,1,64,384]{6,5,0,1,2,4,3:T(8,128)(2,1)}, u32[]{:S(2)}, u32[]{:S(2)}) collective-permute-start(bf16[2,2,2,2,1,64,384]{6,5,0,1,2,4,3:T(8,128)(2,1)S(1)} %maximum_select_fusion.6), channel_id=1, source_target_pairs={{0,1},{1,0},{2,3},{3,2},{4,5},{5,4},{6,7},{7,6},{8,9},{9,8},{10,11... | collective-permute-start | bytes 2359304 | tf_op jit(solution)/shard_map/ppermute | solution.py:175
  493.8 41.3 %collective-permute-start.30 = (bf16[2,2,2,2,1,64,384]{6,5,4,3,2,1,0:T(8,128)(2,1)}, bf16[2,2,2,2,1,64,384]{6,5,4,3,2,1,0:T(8,128)(2,1)}, u32[]{:S(2)}, u32[]{:S(2)}) collective-permute-start(bf16[2,2,2,2,1,64,384]{6,5,4,3,2,1,0:T(8,128)(2,1)} %select_convert_fusion), channel_id=1, source_target_pairs={{0,1},{1,0},{2,3},{3,2},{4,5},{5,4},{6,7},{7,6},{8,9},{9,8},{10,11... | collective-permute-start | bytes 2359304 | tf_op jit(solution)/shard_map/ppermute | solution.py:175
  505.8 37.7 %collective-permute-start.25 = (bf16[2,2,2,2,1,64,384]{6,5,4,3,2,1,0:T(8,128)(2,1)}, bf16[2,2,2,2,1,64,384]{6,5,4,3,2,1,0:T(8,128)(2,1)}, u32[]{:S(2)}, u32[]{:S(2)}) collective-permute-start(bf16[2,2,2,2,1,64,384]{6,5,4,3,2,1,0:T(8,128)(2,1)} %select_convert_fusion.1), channel_id=1, source_target_pairs={{0,1},{1,0},{2,3},{3,2},{4,5},{5,4},{6,7},{7,6},{8,9},{9,8},{10,11... | collective-permute-start | bytes 2359304 | tf_op jit(solution)/shard_map/ppermute | solution.py:175
  526.2 5.1 collective-permute-start.35
  528.9 19.6 %collective-permute-start.20 = (bf16[2,2,2,2,1,64,384]{6,5,4,3,2,1,0:T(8,128)(2,1)}, bf16[2,2,2,2,1,64,384]{6,5,4,3,2,1,0:T(8,128)(2,1)}, u32[]{:S(2)}, u32[]{:S(2)}) collective-permute-start(bf16[2,2,2,2,1,64,384]{6,5,4,3,2,1,0:T(8,128)(2,1)} %select_convert_fusion.2), channel_id=1, source_target_pairs={{0,1},{1,0},{2,3},{3,2},{4,5},{5,4},{6,7},{7,6},{8,9},{9,8},{10,11... | collective-permute-start | bytes 2359304 | tf_op jit(solution)/shard_map/ppermute | solution.py:175
  533.5 9.2 %collective-permute-start.36 = (bf16[2,2,2,1,1,64,256]{6,5,4,3,2,1,0:T(8,128)(2,1)S(1)}, bf16[2,2,2,1,1,64,256]{6,5,4,3,2,1,0:T(8,128)(2,1)S(1)}, u32[]{:S(2)}, u32[]{:S(2)}) collective-permute-start(bf16[2,2,2,1,1,64,256]{6,5,4,3,2,1,0:T(8,128)(2,1)S(1)} %select_convert_fusion.7), channel_id=1, source_target_pairs={{0,2},{1,3},{2,0},{3,1},{4,6},{5,7},{6,4},{7,5},{8,10},{9,11},{10,... | collective-permute-start | bytes 786440 | tf_op jit(solution)/shard_map/ppermute | solution.py:175
  536.7 20.9 %collective-permute-start.31 = (bf16[2,2,2,1,1,64,384]{6,5,4,3,2,1,0:T(8,128)(2,1)S(1)}, bf16[2,2,2,1,1,64,384]{6,5,4,3,2,1,0:T(8,128)(2,1)S(1)}, u32[]{:S(2)}, u32[]{:S(2)}) collective-permute-start(bf16[2,2,2,1,1,64,384]{6,5,4,3,2,1,0:T(8,128)(2,1)S(1)} %select_convert_fusion.4), channel_id=1, source_target_pairs={{0,2},{1,3},{2,0},{3,1},{4,6},{5,7},{6,4},{7,5},{8,10},{9,11},{10,... | collective-permute-start | bytes 1179656 | tf_op jit(solution)/shard_map/ppermute | solution.py:175
  542.9 5.0 collective-permute-start.37
  545.0 14.6 %collective-permute-start.26 = (bf16[2,2,2,1,1,64,384]{6,5,4,3,2,1,0:T(8,128)(2,1)S(1)}, bf16[2,2,2,1,1,64,384]{6,5,4,3,2,1,0:T(8,128)(2,1)S(1)}, u32[]{:S(2)}, u32[]{:S(2)}) collective-permute-start(bf16[2,2,2,1,1,64,384]{6,5,4,3,2,1,0:T(8,128)(2,1)S(1)} %select_convert_fusion.5), channel_id=1, source_target_pairs={{0,2},{1,3},{2,0},{3,1},{4,6},{5,7},{6,4},{7,5},{8,10},{9,11},{10,... | collective-permute-start | bytes 1179656 | tf_op jit(solution)/shard_map/ppermute | solution.py:175
  548.0 4.3 collective-permute-start.38
  552.4 5.1 collective-permute-start.39
  555.1 12.0 %collective-permute-start.21 = (bf16[2,2,2,1,1,64,384]{6,5,4,3,2,1,0:T(8,128)(2,1)S(1)}, bf16[2,2,2,1,1,64,384]{6,5,4,3,2,1,0:T(8,128)(2,1)S(1)}, u32[]{:S(2)}, u32[]{:S(2)}) collective-permute-start(bf16[2,2,2,1,1,64,384]{6,5,4,3,2,1,0:T(8,128)(2,1)S(1)} %select_convert_fusion.6), channel_id=1, source_target_pairs={{0,2},{1,3},{2,0},{3,1},{4,6},{5,7},{6,4},{7,5},{8,10},{9,11},{10,... | collective-permute-start | bytes 1179656 | tf_op jit(solution)/shard_map/ppermute | solution.py:175
  557.7 10.1 %collective-permute-start.32 = (bf16[2,2,1,1,1,64,384]{6,5,4,3,2,1,0:T(8,128)(2,1)S(1)}, bf16[2,2,1,1,1,64,384]{6,5,4,3,2,1,0:T(8,128)(2,1)S(1)}, u32[]{:S(2)}, u32[]{:S(2)}) collective-permute-start(bf16[2,2,1,1,1,64,384]{6,5,4,3,2,1,0:T(8,128)(2,1)S(1)} %select_convert_fusion.8), channel_id=1, source_target_pairs={{0,4},{4,0},{8,12},{12,8},{16,20},{20,16},{24,28},{28,24},{1,5},{5... | collective-permute-start | bytes 589832 | tf_op jit(solution)/shard_map/ppermute | solution.py:175
  559.8 8.8 %collective-permute-start.27 = (bf16[2,2,1,1,1,64,384]{6,5,4,3,2,1,0:T(8,128)(2,1)S(1)}, bf16[2,2,1,1,1,64,384]{6,5,4,3,2,1,0:T(8,128)(2,1)S(1)}, u32[]{:S(2)}, u32[]{:S(2)}) collective-permute-start(bf16[2,2,1,1,1,64,384]{6,5,4,3,2,1,0:T(8,128)(2,1)S(1)} %select_convert_fusion.9), channel_id=1, source_target_pairs={{0,4},{4,0},{8,12},{12,8},{16,20},{20,16},{24,28},{28,24},{1,5},{5... | collective-permute-start | bytes 589832 | tf_op jit(solution)/shard_map/ppermute | solution.py:175
  567.3 6.1 collective-permute-start.22
  568.0 6.1 collective-permute-start.33
  568.6 8.2 %collective-permute-start.28 = (bf16[2,1,1,1,1,64,384]{6,5,4,3,2,1,0:T(8,128)(2,1)S(1)}, bf16[2,1,1,1,1,64,384]{6,5,4,3,2,1,0:T(8,128)(2,1)S(1)}, u32[]{:S(2)}, u32[]{:S(2)}) collective-permute-start(bf16[2,1,1,1,1,64,384]{6,5,4,3,2,1,0:T(8,128)(2,1)S(1)} %select_convert_fusion.13), channel_id=1, source_target_pairs={{0,8},{4,12},{8,0},{12,4},{16,24},{20,28},{24,16},{28,20},{1,9},{5... | collective-permute-start | bytes 294920 | tf_op jit(solution)/shard_map/ppermute | solution.py:175
  573.6 4.7 collective-permute-start.23
  574.2 8.1 %collective-permute-start.34 = (bf16[1,1,1,1,1,64,384]{6,5,4,3,2,1,0:T(8,128)(2,1)S(1)}, bf16[1,1,1,1,1,64,384]{6,5,4,3,2,1,0:T(8,128)(2,1)S(1)}, u32[]{:S(2)}, u32[]{:S(2)}) collective-permute-start(bf16[1,1,1,1,1,64,384]{6,5,4,3,2,1,0:T(8,128)(2,1)S(1)} %select_convert_fusion.16), channel_id=1, source_target_pairs={{0,16},{4,20},{8,24},{12,28},{16,0},{20,4},{24,8},{28,12},{1,17},{... | collective-permute-start | bytes 147464 | tf_op jit(solution)/shard_map/ppermute | solution.py:175
  577.0 5.5 collective-permute-start.29
  578.4 6.5 %collective-permute-start.24 = (bf16[1,1,1,1,1,64,384]{6,5,4,3,2,1,0:T(8,128)(2,1)S(1)}, bf16[1,1,1,1,1,64,384]{6,5,4,3,2,1,0:T(8,128)(2,1)S(1)}, u32[]{:S(2)}, u32[]{:S(2)}) collective-permute-start(bf16[1,1,1,1,1,64,384]{6,5,4,3,2,1,0:T(8,128)(2,1)S(1)} %select_convert_fusion.18), channel_id=1, source_target_pairs={{0,16},{4,20},{8,24},{12,28},{16,0},{20,4},{24,8},{28,12},{1,17},{... | collective-permute-start | bytes 147464 | tf_op jit(solution)/shard_map/ppermute | solution.py:175
  588.5 7.7 %collective-permute-start.45 = (f32[2708]{0:T(1024)S(1)}, f32[2708]{0:T(1024)S(1)}, u32[]{:S(2)}, u32[]{:S(2)}) collective-permute-start(f32[2708]{0:T(1024)S(1)} %concatenate.1427), channel_id=1, source_target_pairs={{0,24},{4,28},{8,16},{12,20},{16,8},{20,12},{24,0},{28,4},{1,25},{... | collective-permute-start | bytes 32504 | tf_op jit(solution)/shard_map/ppermute | solution.py:175
  590.7 7.5 %collective-permute-start.46 = (f32[2708]{0:T(1024)S(1)}, f32[2708]{0:T(1024)S(1)}, u32[]{:S(2)}, u32[]{:S(2)}) collective-permute-start(f32[2708]{0:T(1024)S(1)} %concatenate.1427), channel_id=1, source_target_pairs={{0,28},{4,24},{8,20},{12,16},{16,12},{20,8},{24,4},{28,0},{1,29},{... | collective-permute-start | bytes 32504 | tf_op jit(solution)/shard_map/ppermute | solution.py:175
  592.3 8.6 %collective-permute-start.43 = (f32[2708]{0:T(1024)S(1)}, f32[2708]{0:T(1024)S(1)}, u32[]{:S(2)}, u32[]{:S(2)}) collective-permute-start(f32[2708]{0:T(1024)S(1)} %concatenate.1427), channel_id=1, source_target_pairs={{0,16},{4,20},{8,24},{12,28},{16,0},{20,4},{24,8},{28,12},{1,17},{... | collective-permute-start | bytes 32504 | tf_op jit(solution)/shard_map/ppermute | solution.py:175
  592.9 8.0 %collective-permute-start.44 = (f32[2708]{0:T(1024)S(1)}, f32[2708]{0:T(1024)S(1)}, u32[]{:S(2)}, u32[]{:S(2)}) collective-permute-start(f32[2708]{0:T(1024)S(1)} %concatenate.1427), channel_id=1, source_target_pairs={{0,20},{4,16},{8,28},{12,24},{16,4},{20,0},{24,12},{28,8},{1,21},{... | collective-permute-start | bytes 32504 | tf_op jit(solution)/shard_map/ppermute | solution.py:175
  596.2 4.8 collective-permute-start.41
  596.2 4.8 collective-permute-start.42
  598.2 3.7 collective-permute-start.40
  605.6 3.8 collective-permute-start.48
  (224 other events, 2483.5 us)

commit v2 on v1

v2 whole, which is shorter than its diff:
```python
import functools

import jax
import jax.numpy as jnp
from jax import lax
from jax.experimental import pallas as pl
from jax.experimental.pallas import tpu as pltpu
from jax.sharding import PartitionSpec as P

D = 256
HEADS = 8
HEAD = D // HEADS
FF = 1024
CATS = 32
CLASSES = 32
LAYERS = 3
SEG = 48
MEM = 48
CTX = 96
VOCAB = 1024
GROUP = 4
ROWS = GROUP * CTX
SPREAD = HEADS * CTX
WIDE = 3 * D + D + FF + FF
CUT = [0, 3 * D, 4 * D, 4 * D + FF, WIDE]
VMEM_BYTES = 56 * 1024 * 1024

decay_two = 0.9
step_rate = 0.3
clip_limit = 0.05
tiny_term = 1e-30
norm_eps = 1e-06
masked_score = -1e30
log2_e = 1.4426950408889634
score_scale = HEAD ** (-0.5)
gelu_one = 0.7978845608028654
gelu_two = 0.044715


def dot_nn(left, right):
    return lax.dot_general(
        left, right, (((1,), (0,)), ((), ())), preferred_element_type=jnp.float32
    )


def dot_nt(left, right):
    return lax.dot_general(
        left, right, (((1,), (1,)), ((), ())), preferred_element_type=jnp.float32
    )


def dot_tn(left, right):
    return lax.dot_general(
        left, right, (((0,), (0,)), ((), ())), preferred_element_type=jnp.float32
    )


def inverse_rms(values):
    return lax.rsqrt(jnp.mean(values * values, axis=-1, keepdims=True) + norm_eps)


def rms_back(values, inverse, gain_row, upstream):
    normed = values * inverse
    scaled = upstream * gain_row
    inner = jnp.mean(scaled * normed, axis=-1, keepdims=True)
    return (
        inverse * (scaled - normed * inner),
        jnp.sum(upstream * normed, axis=0, keepdims=True),
    )


def head_masks():
    lane = lax.broadcasted_iota(jnp.int32, (1, D // 2), 1) // HEAD
    return [lane == head for head in range(HEADS // 2)]


def expand_heads(rows, masks):
    half = D // 2
    nothing = jnp.zeros((CTX, half), rows.dtype)
    pieces = []
    for head in range(HEADS):
        side, at = divmod(head, HEADS // 2)
        kept = rows[:, side * half : (side + 1) * half] * masks[at].astype(rows.dtype)
        pair = [kept, nothing] if side == 0 else [nothing, kept]
        pieces.append(jnp.concatenate(pair, axis=1))
    return jnp.concatenate(pieces, axis=0)


def collapse_heads(spread, rows, masks):
    half, span = D // 2, SPREAD // 2
    sides = []
    for side in range(2):
        product = dot_tn(
            spread[:, side * span : (side + 1) * span], rows[:, side * half : (side + 1) * half]
        )
        taken = product[(HEADS // 2 - 1) * CTX :]
        for at in range(HEADS // 2 - 1):
            taken = jnp.where(masks[at], product[at * CTX : (at + 1) * CTX], taken)
        sides.append(taken)
    return jnp.concatenate(sides, axis=1)


def fill_bias(bias_ref):
    key_at = lax.broadcasted_iota(jnp.int32, (CTX, SPREAD), 0)
    query_at = lax.broadcasted_iota(jnp.int32, (CTX, SPREAD), 1) % CTX
    later = key_at > query_at
    crosses = (query_at >= MEM) & (key_at < MEM)
    bias_ref[0] = jnp.where(later | crosses, masked_score, 0.0)
    bias_ref[1] = jnp.where(later, masked_score, 0.0)


def unpack_weights(gathered_ref, widths, start=0):
    count = gathered_ref.shape[0]
    found = []
    for width in widths:
        found.append(
            jnp.concatenate(
                [gathered_ref[at, :, start : start + width] for at in range(count)], axis=1
            )
        )
        start += width
    return found


def one_hot_rows(latent_rows):
    spot = lax.broadcasted_iota(jnp.int32, (CATS, VOCAB), 1) // CLASSES
    group = lax.broadcasted_iota(jnp.int32, (CATS, VOCAB), 0)
    spreader = jnp.where(spot == group, 1.0, 0.0).astype(jnp.bfloat16)
    classes = (lax.broadcasted_iota(jnp.int32, (1, VOCAB), 1) % CLASSES).astype(jnp.float32)
    drawn = dot_nn(latent_rows, spreader)
    return jnp.where(drawn == classes, 1.0, 0.0).astype(jnp.bfloat16)


def forward_kernel(layer, widths, first, *refs):
    if first:
        (latent_ref, gathered_ref, gains_ref, valid_ref, entry_ref) = refs[:5]
        refs = refs[5:]
    else:
        (entry_ref, gathered_ref, gains_ref, valid_ref) = refs[:4]
        refs = refs[4:]
    output_ref, middle_ref, qkv_ref, mix_ref, lse_ref, weight_ref, bias_ref, inner_ref = refs[:8]
    step = pl.program_id(0)

    @pl.when(step == 0)
    def _():
        fill_bias(bias_ref)
        pieces = unpack_weights(gathered_ref, widths)
        for at in range(4):
            weight_ref[:, CUT[at] : CUT[at + 1]] = pieces[at]
        if first:
            embed_ref = refs[8]
            span = gathered_ref.shape[2] - sum(widths)
            embed_ref[...] = unpack_weights(gathered_ref, [span], sum(widths))[0]

    if first:
        hidden = dot_nt(one_hot_rows(latent_ref[...]), refs[8][...])
        entry_ref[...] = hidden
    else:
        hidden = entry_ref[...]
    masks = head_masks()
    gain_att = gains_ref[layer : layer + 1, :]
    gain_ffn = gains_ref[LAYERS + layer : LAYERS + layer + 1, :]
    normed = (hidden * inverse_rms(hidden) * gain_att).astype(jnp.bfloat16)
    qkv_ref[...] = dot_nn(normed, weight_ref[:, CUT[0] : CUT[1]]).astype(jnp.bfloat16)
    for sample in range(GROUP):
        rows = slice(sample * CTX, (sample + 1) * CTX)
        queries = qkv_ref[rows, 0:D]
        keys = qkv_ref[rows, D : 2 * D]
        values = qkv_ref[rows, 2 * D : 3 * D]
        scores = dot_nt(keys, expand_heads(queries, masks))
        scores = scores + bias_ref[valid_ref[step * GROUP + sample]]
        peak = jnp.max(scores, axis=0, keepdims=True)
        exponent = jnp.exp2((scores - peak) * (score_scale * log2_e))
        total = jnp.sum(exponent, axis=0, keepdims=True)
        chance = (exponent * (1.0 / total)).astype(jnp.bfloat16)
        mix_ref[rows, :] = collapse_heads(chance, values, masks).astype(jnp.bfloat16)
        lse_ref[sample] = peak * (score_scale * log2_e) + jnp.log2(total)
    middle = hidden + dot_nn(mix_ref[...], weight_ref[:, CUT[1] : CUT[2]])
    middle_ref[...] = middle
    normed_two = (middle * inverse_rms(middle) * gain_ffn).astype(jnp.bfloat16)
    for part in range(FF // D):
        columns = slice(part * D, (part + 1) * D)
        inner = dot_nn(normed_two, weight_ref[:, CUT[2] + part * D : CUT[2] + (part + 1) * D])
        for sample in range(GROUP):
            rows = slice(sample * CTX, (sample + 1) * CTX)
            value = inner[rows]
            bend = jnp.tanh(value * (gelu_one + (gelu_one * gelu_two) * (value * value)))
            inner_ref[rows, columns] = ((0.5 * value) * (1.0 + bend)).astype(jnp.bfloat16)
    output_ref[...] = middle + dot_nt(inner_ref[...], weight_ref[:, CUT[3] : CUT[4]])


def row_spec(width):
    return pl.BlockSpec((ROWS, width), lambda step: (step, 0))


def whole_spec(shape):
    return pl.BlockSpec(shape, lambda step: (0,) * len(shape))


def smem_spec():
    return pl.BlockSpec(memory_space=pltpu.SMEM)


def run_forward(layer, widths, source, gathered, gains, valid):
    first = layer == 0
    tokens = source.shape[0]
    f32, b16 = jnp.float32, jnp.bfloat16
    shape = jax.ShapeDtypeStruct
    common = [whole_spec(gathered.shape), whole_spec(gains.shape), smem_spec()]
    outs = [
        (shape((tokens, D), f32), row_spec(D)),
        (shape((tokens, D), f32), row_spec(D)),
        (shape((tokens, 3 * D), b16), row_spec(3 * D)),
        (shape((tokens, D), b16), row_spec(D)),
        (
            shape((tokens // CTX, 1, SPREAD), f32),
            pl.BlockSpec((GROUP, 1, SPREAD), lambda step: (step, 0, 0)),
        ),
        (shape((D, WIDE), b16), whole_spec((D, WIDE))),
    ]
    scratch = [pltpu.VMEM((2, CTX, SPREAD), f32), pltpu.VMEM((ROWS, FF), b16)]
    if first:
        in_specs = [row_spec(CATS)] + common
        operands = (source, gathered, gains, valid)
        outs = [(shape((tokens, D), f32), row_spec(D))] + outs
        scratch = scratch + [pltpu.VMEM((D, VOCAB), b16)]
    else:
        in_specs = [row_spec(D)] + common
        operands = (source, gathered, gains, valid)
    found = pl.pallas_call(
        functools.partial(forward_kernel, layer, widths, first),
        grid=(tokens // ROWS,),
        in_specs=in_specs,
        out_specs=[spec for _, spec in outs],
        out_shape=[item for item, _ in outs],
        scratch_shapes=scratch,
        compiler_params=pltpu.CompilerParams(vmem_limit_bytes=VMEM_BYTES),
        cost_estimate=pl.CostEstimate(
            flops=2 * tokens * D * WIDE * (2 if first else 1),
            bytes_accessed=tokens * D * 16 + D * WIDE * 4,
            transcendentals=tokens * (FF + SPREAD),
        ),
        name="layer_forward",
    )(*operands)
    if first:
        return found[0], found[1:]
    return source, found


def head_kernel(start, hidden_ref, table_ref, targets_ref, counted_ref, gains_ref, *refs):
    dhidden_ref, head_grad_ref, gain_ref, loss_ref, turned_ref, final_ref, dlogits_ref = refs
    samples = hidden_ref.shape[0] // CTX
    count = table_ref.shape[0]
    width = head_grad_ref.shape[2]
    tokens = samples * SEG
    gain_row = gains_ref[2 * LAYERS : 2 * LAYERS + 1, :]
    head = unpack_weights(table_ref, [width], start)[0]
    turned_ref[...] = head.T
    for sample in range(samples):
        latest = hidden_ref[sample * CTX + MEM : (sample + 1) * CTX, :]
        final_ref[sample * SEG : (sample + 1) * SEG, :] = (
            latest * inverse_rms(latest) * gain_row
        ).astype(jnp.bfloat16)
    block = D
    loss = jnp.zeros((1, block), jnp.float32)
    spots = lax.broadcasted_iota(jnp.int32, (CLASSES, block), 0)
    for part in range(tokens // block):
        columns = slice(part * block, (part + 1) * block)
        counted = counted_ref[0:1, columns]
        final = final_ref[columns, :]
        for quarter in range(VOCAB // D):
            logits = dot_nt(turned_ref[quarter * D : (quarter + 1) * D, :], final)
            for inside in range(D // CLASSES):
                group = quarter * (D // CLASSES) + inside
                values = logits[inside * CLASSES : (inside + 1) * CLASSES]
                peak = jnp.max(values, axis=0, keepdims=True)
                shifted = values - peak
                exponent = jnp.exp2(shifted * log2_e)
                total = jnp.sum(exponent, axis=0, keepdims=True)
                hot = spots == targets_ref[group : group + 1, columns]
                chosen = jnp.sum(jnp.where(hot, shifted, 0.0), axis=0, keepdims=True)
                loss = loss + counted * (jnp.log(total) - chosen)
                chance = exponent * (1.0 / total)
                slope = (chance - jnp.where(hot, 1.0, 0.0)) * counted
                dlogits_ref[group * CLASSES : (group + 1) * CLASSES, columns] = slope.astype(
                    jnp.bfloat16
                )
    loss_ref[...] = jnp.sum(loss, axis=1, keepdims=True)
    head_grad = dot_nt(final_ref[...].T, dlogits_ref[...])
    for at in range(count):
        head_grad_ref[at] = head_grad[:, at * width : (at + 1) * width]
    dfinal = dot_nn(head, dlogits_ref[...]).T
    gain_sum = jnp.zeros((1, D), jnp.float32)
    for sample in range(samples):
        latest = hidden_ref[sample * CTX + MEM : (sample + 1) * CTX, :]
        slope, gain_part = rms_back(
            latest,
            inverse_rms(latest),
            gain_row,
            dfinal[sample * SEG : (sample + 1) * SEG, :],
        )
        gain_sum = gain_sum + gain_part
        dhidden_ref[sample * CTX : sample * CTX + MEM, :] = jnp.zeros((MEM, D), jnp.float32)
        dhidden_ref[sample * CTX + MEM : (sample + 1) * CTX, :] = slope
    gain_ref[...] = gain_sum


def run_head(hidden, table, start, targets, counted, gains):
    tokens = hidden.shape[0]
    counts = targets.shape[1]
    f32, b16 = jnp.float32, jnp.bfloat16
    shape = jax.ShapeDtypeStruct
    vmem = pl.BlockSpec(memory_space=pltpu.VMEM)
    return pl.pallas_call(
        functools.partial(head_kernel, start),
        in_specs=[vmem] * 5,
        out_specs=[vmem] * 4,
        out_shape=[
            shape((tokens, D), f32),
            shape(table.shape[:2] + (table.shape[2] - start,), f32),
            shape((1, D), f32),
            shape((1, 1), f32),
        ],
        scratch_shapes=[
            pltpu.VMEM((VOCAB, D), b16),
            pltpu.VMEM((counts, D), b16),
            pltpu.VMEM((VOCAB, counts), b16),
        ],
        compiler_params=pltpu.CompilerParams(vmem_limit_bytes=VMEM_BYTES),
        cost_estimate=pl.CostEstimate(
            flops=6 * counts * D * VOCAB,
            bytes_accessed=tokens * D * 8 + D * VOCAB * 6,
            transcendentals=counts * VOCAB,
        ),
        name="head_and_loss",
    )(hidden, table, targets, counted, gains)


def backward_kernel(layer, widths, first, *refs):
    (entry_ref, middle_ref, qkv_ref, mix_ref, lse_ref, up_ref, weight_ref, gains_ref, valid_ref) = (
        refs[:9]
    )
    refs = refs[9:]
    if first:
        latent_ref = refs[0]
        refs = refs[1:]
        grad_ref, gain_ref = refs[:2]
        refs = refs[2:]
    else:
        dentry_ref, grad_ref, gain_ref = refs[:3]
        refs = refs[3:]
    (
        bias_ref,
        normed_ref,
        normed_two_ref,
        inner_ref,
        dinner_ref,
        dout_ref,
        dmiddle_ref,
        dqkv_ref,
        mixes_ref,
    ) = refs[:9]
    step = pl.program_id(0)
    last = pl.num_programs(0) - 1
    here = pl.ds(pl.multiple_of(step * ROWS, ROWS), ROWS)

    @pl.when(step == 0)
    def _():
        fill_bias(bias_ref)
        gain_ref[...] = jnp.zeros_like(gain_ref)

    masks = head_masks()
    gain_att = gains_ref[layer : layer + 1, :]
    gain_ffn = gains_ref[LAYERS + layer : LAYERS + layer + 1, :]
    upstream = up_ref[...]
    dout = upstream.astype(jnp.bfloat16)
    dout_ref[here, :] = dout
    mixes_ref[here, :] = mix_ref[...]
    middle = middle_ref[...]
    inverse_two = inverse_rms(middle)
    normed_two = (middle * inverse_two * gain_ffn).astype(jnp.bfloat16)
    normed_two_ref[here, :] = normed_two
    for part in range(FF // D):
        columns = slice(part * D, (part + 1) * D)
        inner = dot_nn(normed_two, weight_ref[:, CUT[2] + part * D : CUT[2] + (part + 1) * D])
        dact = dot_nn(dout, weight_ref[:, CUT[3] + part * D : CUT[3] + (part + 1) * D])
        for sample in range(GROUP):
            rows = slice(sample * CTX, (sample + 1) * CTX)
            there = pl.ds(pl.multiple_of(step * ROWS + sample * CTX, CTX), CTX)
            value = inner[rows]
            square = value * value
            bend = jnp.tanh(value * (gelu_one + (gelu_one * gelu_two) * square))
            half_value = 0.5 * value
            inner_ref[there, columns] = (half_value * (1.0 + bend)).astype(jnp.bfloat16)
            slope = (0.5 + 0.5 * bend) + (half_value * (1.0 - bend * bend)) * (
                gelu_one + (3.0 * gelu_one * gelu_two) * square
            )
            dinner_ref[there, columns] = (dact[rows] * slope).astype(jnp.bfloat16)
    dnormed_two = dot_nt(dinner_ref[here, :], weight_ref[:, CUT[2] : CUT[3]])
    through, gain_part = rms_back(middle, inverse_two, gain_ffn, dnormed_two)
    gain_ref[1:2, :] += gain_part
    dmiddle = upstream + through
    dattend = dmiddle.astype(jnp.bfloat16)
    dmiddle_ref[here, :] = dattend
    dmix = dot_nt(dattend, weight_ref[:, CUT[1] : CUT[2]]).astype(jnp.bfloat16)
    for sample in range(GROUP):
        rows = slice(sample * CTX, (sample + 1) * CTX)
        there = pl.ds(pl.multiple_of(step * ROWS + sample * CTX, CTX), CTX)
        queries = expand_heads(qkv_ref[rows, 0:D], masks)
        keys = qkv_ref[rows, D : 2 * D]
        values = qkv_ref[rows, 2 * D : 3 * D]
        slopes = expand_heads(dmix[rows], masks)
        scores = dot_nt(keys, queries) + bias_ref[valid_ref[step * GROUP + sample]]
        chance = jnp.exp2(scores * (score_scale * log2_e) - lse_ref[sample])
        dchance = dot_nt(values, slopes)
        weighed = chance * dchance
        dscore = (weighed - chance * jnp.sum(weighed, axis=0, keepdims=True)).astype(jnp.bfloat16)
        dvalues = dot_nn(chance.astype(jnp.bfloat16), slopes)
        dkeys = dot_nn(dscore, queries) * score_scale
        dqueries = collapse_heads(dscore, keys, masks) * score_scale
        dqkv_ref[there, 0:D] = dqueries.astype(jnp.bfloat16)
        dqkv_ref[there, D : 2 * D] = dkeys.astype(jnp.bfloat16)
        dqkv_ref[there, 2 * D : 3 * D] = dvalues.astype(jnp.bfloat16)
    hidden = entry_ref[...]
    inverse = inverse_rms(hidden)
    normed_ref[here, :] = (hidden * inverse * gain_att).astype(jnp.bfloat16)
    dnormed = dot_nt(dqkv_ref[here, :], weight_ref[:, CUT[0] : CUT[1]])
    through, gain_part = rms_back(hidden, inverse, gain_att, dnormed)
    gain_ref[0:1, :] += gain_part
    dentry = dmiddle + through
    if first:
        dlow_ref, hot_ref = refs[9:11]
        dlow_ref[here, :] = dentry.astype(jnp.bfloat16)
        hot_ref[here, :] = one_hot_rows(latent_ref[...])
    else:
        dentry_ref[...] = dentry

    @pl.when(step == last)
    def _():
        count = grad_ref.shape[0]
        cuts = [0]
        for width in widths:
            cuts.append(cuts[-1] + width)
        pairs = [
            (normed_ref, dqkv_ref),
            (mixes_ref, dmiddle_ref),
            (normed_two_ref, dinner_ref),
            (dout_ref, inner_ref),
        ]
        for which, (left, right) in enumerate(pairs):
            turned = left[...].T
            grad = dot_nn(turned, right[...])
            for at in range(count):
                grad_ref[at, :, cuts[which] : cuts[which + 1]] = grad[
                    :, at * widths[which] : (at + 1) * widths[which]
                ]
        if first:
            grad = dot_nn(refs[9][...].T, refs[10][...])
            span = grad_ref.shape[2] - cuts[-1]
            for at in range(count):
                grad_ref[at, :, cuts[-1] :] = grad[:, at * span : (at + 1) * span]


def run_backward(layer, widths, count, saved, upstream, gains, valid, latents=None, span=0):
    first = layer == 0
    entry, (output, middle, qkv, mix, lse, weights) = saved
    tokens = upstream.shape[0]
    f32, b16 = jnp.float32, jnp.bfloat16
    shape = jax.ShapeDtypeStruct
    in_specs = [
        row_spec(D),
        row_spec(D),
        row_spec(3 * D),
        row_spec(D),
        pl.BlockSpec((GROUP, 1, SPREAD), lambda step: (step, 0, 0)),
        row_spec(D),
        whole_spec(weights.shape),
        whole_spec(gains.shape),
        smem_spec(),
    ]
    operands = [entry, middle, qkv, mix, lse, upstream, weights, gains, valid]
    across = sum(widths) + span
    outs = [
        (shape((count, D, across), f32), whole_spec((count, D, across))),
        (shape((2, D), f32), whole_spec((2, D))),
    ]
    scratch = [
        pltpu.VMEM((2, CTX, SPREAD), f32),
        pltpu.VMEM((tokens, D), b16),
        pltpu.VMEM((tokens, D), b16),
        pltpu.VMEM((tokens, FF), b16),
        pltpu.VMEM((tokens, FF), b16),
        pltpu.VMEM((tokens, D), b16),
        pltpu.VMEM((tokens, D), b16),
        pltpu.VMEM((tokens, 3 * D), b16),
        pltpu.VMEM((tokens, D), b16),
    ]
    if first:
        in_specs.append(row_spec(CATS))
        operands.append(latents)
        scratch = scratch + [pltpu.VMEM((tokens, D), b16), pltpu.VMEM((tokens, VOCAB), b16)]
    else:
        outs.insert(0, (shape((tokens, D), f32), row_spec(D)))
    return pl.pallas_call(
        functools.partial(backward_kernel, layer, widths, first),
        grid=(tokens // ROWS,),
        in_specs=in_specs,
        out_specs=[spec for _, spec in outs],
        out_shape=[item for item, _ in outs],
        scratch_shapes=scratch,
        compiler_params=pltpu.CompilerParams(vmem_limit_bytes=VMEM_BYTES),
        cost_estimate=pl.CostEstimate(
            flops=6 * tokens * D * WIDE,
            bytes_accessed=tokens * D * 24 + D * WIDE * 6,
            transcendentals=tokens * (FF + SPREAD),
        ),
        name="layer_backward",
    )(*operands)


def swap(value, axis, bit):
    pairs = [(place, place ^ bit) for place in range(lax.axis_size(axis))]
    return lax.ppermute(value, axis, pairs)


def gather_pieces(pieces):
    outer = lax.axis_size("dp").bit_length() - 1
    inner = lax.axis_size("fsdp").bit_length() - 1
    order = [("dp", bit) for bit in reversed(range(outer))] + [
        ("fsdp", bit) for bit in reversed(range(inner))
    ]
    done = [None] * len(order)
    found = []
    for piece in pieces:
        held = piece.reshape((1,) * (outer + inner) + piece.shape)
        for place, (axis, bit) in enumerate(order):
            if done[place] is not None:
                held, _ = lax.optimization_barrier((held, done[place]))
            other = swap(held, axis, 1 << bit)
            done[place] = other
            upper = (lax.axis_index(axis) >> bit) & 1 == 1
            held = jnp.where(
                upper,
                jnp.concatenate([other, held], axis=place),
                jnp.concatenate([held, other], axis=place),
            )
        found.append(
            held.reshape(lax.axis_size("dp"), lax.axis_size("fsdp") * piece.shape[0], piece.shape[1])
        )
    return found


def scatter_pieces(blocks):
    outer = lax.axis_size("dp").bit_length() - 1
    inner = lax.axis_size("fsdp").bit_length() - 1
    rows, columns = blocks.shape[1] >> inner, blocks.shape[2]
    held = blocks.reshape((2,) * (outer + inner) + (rows, columns))
    order = [("dp", bit) for bit in reversed(range(outer))] + [
        ("fsdp", bit) for bit in reversed(range(inner))
    ]
    places = {item: place for place, item in enumerate(order)}
    for axis, bit in [("fsdp", bit) for bit in range(inner)] + [("dp", bit) for bit in range(outer)]:
        place = places[(axis, bit)]
        upper = (lax.axis_index(axis) >> bit) & 1 == 1
        low = lax.slice_in_dim(held, 0, 1, axis=place)
        high = lax.slice_in_dim(held, 1, 2, axis=place)
        other = swap(jnp.where(upper, low, high).astype(jnp.bfloat16), axis, 1 << bit)
        held = jnp.where(upper, high, low) + other.astype(jnp.float32)
    return held.reshape(rows, columns)


def sum_over(value, axis):
    terms = [value] + [swap(value, axis, step) for step in range(1, lax.axis_size(axis))]
    while len(terms) > 1:
        terms = [terms[at] + terms[at + 1] for at in range(0, len(terms), 2)]
    return terms[0]


def flat(items):
    return jnp.concatenate([item.reshape(-1) for item in items])


def unflat(vector, items):
    found, at = [], 0
    for item in items:
        found.append(vector[at : at + item.size].reshape(item.shape))
        at += item.size
    return found


def shards(
    latents,
    targets,
    horizon,
    memory_valid,
    embed,
    qkv_weight,
    out_weight,
    up_weight,
    down_weight,
    head_weight,
    gains,
    embed_rows,
    embed_cols,
    qkv_rows,
    qkv_cols,
    out_rows,
    out_cols,
    up_rows,
    up_cols,
    down_rows,
    down_cols,
    head_rows,
    head_cols,
    gain_second,
):
    samples = latents.shape[0]
    count = lax.axis_size("dp")
    layer_parts = [
        jnp.concatenate(
            [qkv_weight[at], out_weight[at], up_weight[at], down_weight[at].T], axis=1
        ).astype(jnp.bfloat16)
        for at in range(LAYERS)
    ]
    widths = [qkv_weight.shape[2], out_weight.shape[2], up_weight.shape[2], down_weight.shape[1]]
    cuts = [0, widths[0], sum(widths[:2]), sum(widths[:3]), sum(widths)]
    span = embed.shape[0]
    layer_parts[0] = jnp.concatenate([layer_parts[0], embed.T.astype(jnp.bfloat16)], axis=1)
    layer_parts[-1] = jnp.concatenate([layer_parts[-1], head_weight.astype(jnp.bfloat16)], axis=1)
    gathered = gather_pieces(layer_parts)

    latent_rows = latents.astype(jnp.bfloat16).reshape(samples * CTX, CATS)
    target_rows = targets.transpose(2, 0, 1).reshape(CATS, samples * SEG)
    counted = jnp.arange(SEG, dtype=jnp.int32)[None, :] < horizon[:, None]
    counted = counted.astype(jnp.float32).reshape(1, samples * SEG)
    current = latent_rows
    saved = []
    for at in range(LAYERS):
        saved.append(run_forward(at, widths, current, gathered[at], gains, memory_valid))
        current = saved[-1][1][0]
    upstream, head_term, dgain_final, loss_local = run_head(
        current, gathered[-1], cuts[-1], target_rows, counted, gains
    )
    loss_local = loss_local[0, 0]
    head_raw = scatter_pieces(head_term)
    layer_raws = [None] * LAYERS
    att_terms = [None] * LAYERS
    ffn_terms = [None] * LAYERS
    for at in reversed(range(LAYERS)):
        found = run_backward(
            at,
            widths,
            count,
            saved[at],
            upstream,
            gains,
            memory_valid,
            latent_rows if at == 0 else None,
            span if at == 0 else 0,
        )
        if at:
            upstream = found[0]
        layer_raws[at] = scatter_pieces(found[-2])
        att_terms[at], ffn_terms[at] = found[-1][0], found[-1][1]
    embed_raw = layer_raws[0][:, cuts[-1] :]
    gain_local = jnp.stack(att_terms + ffn_terms + [dgain_final[0]])

    raws = [jnp.stack([raw[:, cuts[at] : cuts[at + 1]] for raw in layer_raws]) for at in range(4)]
    raws = raws + [embed_raw, head_raw]
    masters = [
        qkv_weight,
        out_weight,
        up_weight,
        down_weight.transpose(0, 2, 1),
        embed.T,
        head_weight,
    ]
    inner_old = [qkv_rows, out_rows, up_rows, down_cols, embed_cols, head_rows]
    outer_old = [qkv_cols, out_cols, up_cols, down_rows, embed_rows, head_cols]
    inner_is_row = [True, True, True, False, False, True]
    inner_part = [jnp.sum(raw * raw, axis=-1) for raw in raws]
    outer_part = [jnp.sum(raw * raw, axis=-2) for raw in raws]
    weight_square = [jnp.sum(master * master, axis=(-2, -1)) for master in masters]
    outer_row_sums = [
        jnp.sum(outer_old[at], axis=-1) for at in range(6) if not inner_is_row[at]
    ]
    inner_row_sums = [jnp.sum(inner_old[at], axis=-1) for at in range(6) if inner_is_row[at]]
    scalars = [loss_local, jnp.sum(horizon).astype(jnp.float32)]
    first = inner_part + outer_row_sums + weight_square + scalars + [gain_local]
    first_sum = unflat(sum_over(flat(first), "dp"), first)
    inner_global, first_sum = first_sum[:6], first_sum[6:]
    outer_row_sums, first_sum = first_sum[:2], first_sum[2:]
    entry_square = [jnp.sum(part, axis=-1) for part in inner_global]
    second = outer_part + inner_row_sums + entry_square + first_sum
    second_sum = unflat(sum_over(flat(second), "fsdp"), second)
    outer_global, second_sum = second_sum[:6], second_sum[6:]
    inner_row_sums, second_sum = second_sum[:4], second_sum[4:]
    entry_square, second_sum = second_sum[:6], second_sum[6:]
    weight_total, second_sum = second_sum[:6], second_sum[6:]
    loss_total, count_total, gain_sum = second_sum
    row_sums = inner_row_sums[:3] + outer_row_sums + inner_row_sums[3:]

    square_total = jnp.sum(gain_sum * gain_sum)
    for part in entry_square:
        square_total = square_total + jnp.sum(part)
    norm_value = jnp.sqrt(square_total) / count_total
    scaling = jnp.minimum(1.0, clip_limit / norm_value) / count_total
    found = []
    for at in range(6):
        inner_length = masters[at].shape[-2] * lax.axis_size("fsdp")
        outer_length = masters[at].shape[-1] * lax.axis_size("dp")
        row_length = inner_length if inner_is_row[at] else outer_length
        entries = inner_length * outer_length
        square_scale = scaling * scaling
        inner_new = decay_two * inner_old[at] + (1 - decay_two) * (
            square_scale * inner_global[at] / outer_length + tiny_term
        )
        outer_new = decay_two * outer_old[at] + (1 - decay_two) * (
            square_scale * outer_global[at] / inner_length + tiny_term
        )
        mean_rows = decay_two * (row_sums[at] / row_length) + (1 - decay_two) * (
            square_scale * entry_square[at] / entries + tiny_term
        )
        spread = jnp.sqrt(weight_total[at] / entries)
        grad = raws[at] * scaling
        scale_of = (step_rate * spread * jnp.sqrt(mean_rows))[..., None, None]
        updated = masters[at] - scale_of * grad * (
            lax.rsqrt(inner_new)[..., :, None] * lax.rsqrt(outer_new)[..., None, :]
        )
        found.append((updated, grad, inner_new, outer_new))
    results = [loss_total, count_total, norm_value]
    for at in [4, 0, 1, 2, 3, 5]:
        updated, grad, inner_new, outer_new = found[at]
        if inner_is_row[at]:
            results = results + [updated, grad, inner_new, outer_new]
        else:
            turned = [jnp.swapaxes(item, -1, -2) for item in (updated, grad)]
            results = results + turned + [outer_new, inner_new]
    gain_grad = gain_sum * scaling
    gain_second_new = decay_two * gain_second + (1 - decay_two) * (
        gain_grad * gain_grad + tiny_term
    )
    gains_new = gains - step_rate * jnp.sqrt(
        jnp.mean(gains * gains, axis=-1, keepdims=True)
    ) * gain_grad * lax.rsqrt(gain_second_new)
    results = results + [gains_new, gain_grad, gain_second_new]
    return tuple(results)


def solution(mesh):
    return jax.shard_map(
        shards,
        mesh=mesh,
        in_specs=(
            P(("dp", "fsdp"), None, None),
            P(("dp", "fsdp"), None, None),
            P(("dp", "fsdp")),
            P(("dp", "fsdp")),
            P("dp", "fsdp"),
            P(None, "fsdp", "dp"),
            P(None, "fsdp", "dp"),
            P(None, "fsdp", "dp"),
            P(None, "dp", "fsdp"),
            P("fsdp", "dp"),
            P(),
            P("dp"),
            P("fsdp"),
            P(None, "fsdp"),
            P(None, "dp"),
            P(None, "fsdp"),
            P(None, "dp"),
            P(None, "fsdp"),
            P(None, "dp"),
            P(None, "dp"),
            P(None, "fsdp"),
            P("fsdp"),
            P("dp"),
            P(),
        ),
        out_specs=(
            P(),
            P(),
            P(),
            P("dp", "fsdp"),
            P("dp", "fsdp"),
            P("dp"),
            P("fsdp"),
            P(None, "fsdp", "dp"),
            P(None, "fsdp", "dp"),
            P(None, "fsdp"),
            P(None, "dp"),
            P(None, "fsdp", "dp"),
            P(None, "fsdp", "dp"),
            P(None, "fsdp"),
            P(None, "dp"),
            P(None, "fsdp", "dp"),
            P(None, "fsdp", "dp"),
            P(None, "fsdp"),
            P(None, "dp"),
            P(None, "dp", "fsdp"),
            P(None, "dp", "fsdp"),
            P(None, "dp"),
            P(None, "fsdp"),
            P("fsdp", "dp"),
            P("fsdp", "dp"),
            P("fsdp"),
            P("dp"),
            P(),
            P(),
            P(),
        ),
        check_vma=False,
    )
```

time: 644 us -> 349 us (0.54)
  local copies, waits for them, and re-layouts: 272 us -> 17.6 us
  matrix products: 138 us -> 0 us
  Pallas kernels: 0 us -> 130 us
  other arithmetic: 95.4 us -> 42 us
  waiting for transfers between devices: 51.5 us -> 75.7 us
    dot_general x83 -> x0, matrix products: 138 us -> none  [the longest x13 37.5 us: matmul_nt(): lax.dot_general(left, right, (((1,), (1,)), ((), ())), preferred_element_...]
    pallas_call x0 -> x7, Pallas kernels: none -> 130 us  [the longest x3 74.9 us: run_backward(): pl.pallas_call(functools.partial(backward_kernel, layer, widths, first),...]
    another operation x37 -> x1, local copies, waits for them, and re-layouts: 47.4 us -> 0.76 us  [shards(): gain_local = jnp.stack(att_terms + ffn_terms + [dgain_final[0]])]
    convert_element_type x12 -> x2, local copies, waits for them, and re-layouts: 37.8 us -> 1.6 us  [the longest x1 0.94 us: shards(): latent_rows = latents.astype(jnp.bfloat16).reshape(samples * CTX, CATS)]
    transpose x31 -> x2, local copies, waits for them, and re-layouts: 33.5 us -> 0.16 us  [the longest x1 0.16 us: shards(): target_rows = targets.transpose(2, 0, 1).reshape(CATS, samples * SEG)]
    reshape x21 -> x1, local copies, waits for them, and re-layouts: 28.6 us -> 0.78 us  [shards(): target_rows = targets.transpose(2, 0, 1).reshape(CATS, samples * SEG)]
    while x105 -> x0, local copies, waits for them, and re-layouts: 26.1 us -> none
    ppermute x50 -> x45, waiting for transfers between devices: 51.5 us -> 75.7 us  [swap(): return lax.ppermute(value, axis, pairs)]
  transfers between devices with their start and end apart: 50 -> 45, of which waited for: 20 -> 26; matrix products, arithmetic and copies ran while one was open for 16% -> 9% of each run, Pallas kernels for 0% -> 31%
where the time goes in v2:
time: 349 us; the launch traced here: 344 us
  Pallas kernels  130 us (37%)
  waiting for transfers between devices  75.7 us (22%)
  starting transfers between devices  65.2 us (19%)
  other arithmetic  42 us (12%)
  local copies, waits for them, and re-layouts  17.6 us (5%)
  between operations  14.3 us (4%)
    ppermute x45, waiting for transfers between devices, swap(): return lax.ppermute(value, axis, pairs)  75.7 us
    pallas_call x3, Pallas kernels, run_backward(): pl.pallas_call(functools.partial(backward_kernel, layer, widths, first),...  74.9 us
    ppermute x45, starting transfers between devices, swap(): return lax.ppermute(value, axis, pairs)  65.2 us
    pallas_call x3, Pallas kernels, run_forward(): pl.pallas_call(functools.partial(forward_kernel, layer, widths, first), g...  48.2 us
    reduce_sum x6, other arithmetic, shards(): jnp.sum(master * master, axis=(-2, -1))  8.09 us
    select_n x15, other arithmetic, gather_pieces(): jnp.where(upper, jnp.concatenate([other, held], axis=place), jnp.concaten...  7.9 us
    convert_element_type x20, other arithmetic, scatter_pieces(): jnp.where(upper, low, high).astype(jnp.bfloat16)  7.68 us
  transfers between devices with their start and end apart: 45, of which 26 were waited for; matrix products, arithmetic and copies ran while one was open for 9% of the time, Pallas kernels for 31%

profile of v2, /device:TPU:0, one launch (start us, length us, event | category | flops | bytes accessed | tf_op | source)
XLA Modules:
  0.0 344.4 jit_solution(7144204216420993909)
XLA Ops:
  1.6 1.6 multiply_reduce_fusion
  3.2 1.6 multiply_reduce_fusion.1
  6.6 4.1 %collective-permute-start = (bf16[1,1,1,1,1,64,512]{6,5,0,1,2,4,3:T(8,128)(2,1)S(1)}, bf16[1,1,1,1,1,64,512]{6,5,0,1,2,4,3:T(8,128)(2,1)S(1)}, u32[]{:S(2)}, u32[]{:S(2)}) collective-permute-start(bf16[1,1,1,1,1,64,512]{6,5,0,1,2,4,3:T(8,128)(2,1)S(1)} %bitcast.154), channel_id=1, source_target_pairs={{0,16},{4,20},{8,24},{12,28},{16,0},{20,4},{24,8},{28,12},{1,17},{... | collective-permute-start | bytes 196616 | tf_op jit(solution)/shard_map/ppermute | solution.py:523
  10.7 3.6 %collective-permute-done = bf16[1,1,1,1,1,64,512]{6,5,0,1,2,4,3:T(8,128)(2,1)S(1)} collective-permute-done((bf16[1,1,1,1,1,64,512]{6,5,0,1,2,4,3:T(8,128)(2,1)S(1)}, bf16[1,1,1,1,1,64,512]{6,5,0,1,2,4,3:T(8,128)(2,1)S(1)}, u32[]{:S(2)}, u32[]{:S(2)}) %collective-permute-start) | collective-permute-done | bytes 65568 | tf_op jit(solution)/shard_map/ppermute | solution.py:523
  15.0 4.4 %collective-permute-done.1 = bf16[2,1,1,1,1,64,512]{6,5,0,1,2,4,3:T(8,128)(2,1)S(1)} collective-permute-done((bf16[2,1,1,1,1,64,512]{6,5,0,1,2,4,3:T(8,128)(2,1)S(1)}, bf16[2,1,1,1,1,64,512]{6,5,0,1,2,4,3:T(8,128)(2,1)S(1)}, u32[]{:S(2)}, u32[]{:S(2)}) %collective-permute-start.1) | collective-permute-done | bytes 131104 | tf_op jit(solution)/shard_map/ppermute | solution.py:523
  19.4 1.8 collective-permute-start.2
  21.2 4.6 %collective-permute-done.2 = bf16[2,2,1,1,1,64,512]{6,5,0,1,2,4,3:T(8,128)(2,1)S(1)} collective-permute-done((bf16[2,2,1,1,1,64,512]{6,5,0,1,2,4,3:T(8,128)(2,1)S(1)}, bf16[2,2,1,1,1,64,512]{6,5,0,1,2,4,3:T(8,128)(2,1)S(1)}, u32[]{:S(2)}, u32[]{:S(2)}) %collective-permute-start.2) | collective-permute-done | bytes 262176 | tf_op jit(solution)/shard_map/ppermute | solution.py:523
  25.9 1.8 collective-permute-start.3
  27.8 3.1 collective-permute-start.5
  30.9 2.1 collective-permute-done.5
  40.0 3.9 %collective-permute-start.10 = (bf16[1,1,1,1,1,64,512]{6,5,0,1,2,4,3:T(8,128)(2,1)S(1)}, bf16[1,1,1,1,1,64,512]{6,5,0,1,2,4,3:T(8,128)(2,1)S(1)}, u32[]{:S(2)}, u32[]{:S(2)}) collective-permute-start(bf16[1,1,1,1,1,64,512]{6,5,0,1,2,4,3:T(8,128)(2,1)S(1)} %bitcast.161), channel_id=1, source_target_pairs={{0,16},{4,20},{8,24},{12,28},{16,0},{20,4},{24,8},{28,12},{1,17},{... | collective-permute-start | bytes 196616 | tf_op jit(solution)/shard_map/ppermute | solution.py:523
  45.5 2.2 collective-permute-done.10
  48.2 4.7 %collective-permute-done.11 = bf16[2,1,1,1,1,64,512]{6,5,0,1,2,4,3:T(8,128)(2,1)S(1)} collective-permute-done((bf16[2,1,1,1,1,64,512]{6,5,0,1,2,4,3:T(8,128)(2,1)S(1)}, bf16[2,1,1,1,1,64,512]{6,5,0,1,2,4,3:T(8,128)(2,1)S(1)}, u32[]{:S(2)}, u32[]{:S(2)}) %collective-permute-start.11) | collective-permute-done | bytes 131104 | tf_op jit(solution)/shard_map/ppermute | solution.py:523
  57.5 2.8 collective-permute-done.12
  61.6 1.6 collective-permute-start.13
  70.1 3.5 %collective-permute-done.13 = bf16[2,2,2,1,1,64,512]{6,5,0,1,2,4,3:T(8,128)(2,1)} collective-permute-done((bf16[2,2,2,1,1,64,512]{6,5,0,1,2,4,3:T(8,128)(2,1)S(1)}, bf16[2,2,2,1,1,64,512]{6,5,0,1,2,4,3:T(8,128)(2,1)}, u32[]{:S(2)}, u32[]{:S(2)}) %collective-permute-start.13) | collective-permute-done | bytes 524320 | tf_op jit(solution)/shard_map/ppermute | solution.py:523
  77.0 18.6 %layer_forward.3 = (f32[1536,256]{1,0:T(8,128)}, f32[1536,256]{1,0:T(8,128)}, f32[1536,256]{1,0:T(8,128)}, bf16[1536,768]{1,0:T(8,128)(2,1)}, bf16[1536,256]{1,0...) custom-call(bf16[1536,32]{1,0:T(8,128)(2,1)} %bitcast.158, bf16[8,256,512]{2,1,0:T(8,128)(2,1)} %bitcast.151, ...), custom_call_target="tpu_custom_call" | custom-call | flops 4831838208 | bytes 9437184 | tf_op jit(solution)/shard_map/layer_forward/pallas_call | solution.py:230
  95.7 2.8 maximum_select_fusion.2
  98.4 14.6 %layer_forward.4 = (f32[1536,256]{1,0:T(8,128)}, f32[1536,256]{1,0:T(8,128)}, bf16[1536,768]{1,0:T(8,128)(2,1)}, bf16[1536,256]{1,0:T(8,128)(2,1)}, f32[16,1,768]{2,1,0:T(1,128)}, /*index=5*/bf16[256,3072]{1,0:T(8,128)(2,1)}) custom-call(f32[1536,256]{1,0:T(8,128)} %get-tuple-element.76.refs_0_, bf16[8,256,384]{2,1,0:T(8,128)(2,1)} %bitcast.152, ...), custom_call_target="tpu_custom_call" | custom-call | flops 2415919104 | bytes 9437184 | tf_op jit(solution)/shard_map/layer_forward/pallas_call | solution.py:230
  114.9 15.0 %layer_forward.5 = (f32[1536,256]{1,0:T(8,128)}, f32[1536,256]{1,0:T(8,128)}, bf16[1536,768]{1,0:T(8,128)(2,1)}, bf16[1536,256]{1,0:T(8,128)(2,1)}, f32[16,1,768]{2,1,0:T(1,128)}, /*index=5*/bf16[256,3072]{1,0:T(8,128)(2,1)}) custom-call(f32[1536,256]{1,0:T(8,128)} %get-tuple-element.86.refs_0_, bf16[8,256,512]{2,1,0:T(8,128)(2,1)} %bitcast.149, ...), custom_call_target="tpu_custom_call" | custom-call | flops 2415919104 | bytes 9437184 | tf_op jit(solution)/shard_map/layer_forward/pallas_call | solution.py:230
  129.9 6.5 %head_and_loss.1 = (f32[1536,256]{1,0:T(8,128)}, f32[8,256,128]{2,1,0:T(8,128)}, f32[1,256]{1,0:T(1,128)}, f32[1,1]{1,0:T(1,128)}) custom-call(f32[1536,256]{1,0:T(8,128)} %get-tuple-element.96.hidden_ref, bf16[8,256,512]{2,1,0:T(8,128)(2,1)} %bitcast.150, s32[32,768]{1,0:T(8,128)} %reshape.1477.targets_ref, f32[1,768]{1,0:T(1,128)} %reshape.1509.counted_ref, ...), custom_call_target="tpu_custom_call" | custom-call | flops 1207959552 | bytes 4718592 | tf_op jit(solution)/shard_map/head_and_loss/pallas_call | solution.py:314
  138.2 24.2 %layer_backward.3 = (f32[1536,256]{1,0:T(8,128)}, f32[8,256,384]{2,1,0:T(8,128)}, f32[2,256]{1,0:T(2,128)}) custom-call(f32[1536,256]{1,0:T(8,128)} %get-tuple-element.86.refs_0_, f32[1536,256]{1,0:T(8,128)} %get-tuple-element.92.refs_1_, bf16[1536,768]{1,0:T(8,128)(2,1)} %get-tuple-element.93.refs_2_, bf16[1536,256]{1,0:T(8,128)(2,1)} %get-tuple-element.94.refs_3_, ...), custom_call_target="tpu_custom_call" | custom-call | flops 7247757312 | bytes 14155776 | tf_op jit(solution)/shard_map/layer_backward/pallas_call | solution.py:504
  162.4 24.5 %layer_backward.4 = (f32[1536,256]{1,0:T(8,128)}, f32[8,256,384]{2,1,0:T(8,128)}, f32[2,256]{1,0:T(2,128)}) custom-call(f32[1536,256]{1,0:T(8,128)} %get-tuple-element.76.refs_0_, f32[1536,256]{1,0:T(8,128)} %get-tuple-element.82.refs_1_, bf16[1536,768]{1,0:T(8,128)(2,1)} %get-tuple-element.83.refs_2_, bf16[1536,256]{1,0:T(8,128)(2,1)} %get-tuple-element.84.refs_3_, ...), custom_call_target="tpu_custom_call" | custom-call | flops 7247757312 | bytes 14155776 | tf_op jit(solution)/shard_map/layer_backward/pallas_call | solution.py:504
  187.0 26.2 %layer_backward.5 = (f32[8,256,512]{2,1,0:T(8,128)}, f32[2,256]{1,0:T(2,128)}) custom-call(f32[1536,256]{1,0:T(8,128)} %get-tuple-element.71.refs_0_, f32[1536,256]{1,0:T(8,128)} %get-tuple-element.72.refs_1_, bf16[1536,768]{1,0:T(8,128)(2,1)} %get-tuple-element.73.refs_2_, bf16[1536,256]{1,0:T(8,128)(2,1)} %get-tuple-element.74.refs_3_, ...), custom_call_target="tpu_custom_call" | custom-call | flops 7247757312 | bytes 14155776 | tf_op jit(solution)/shard_map/layer_backward/pallas_call | solution.py:504
  213.2 3.5 %select_convert_fusion = bf16[2,2,2,2,1,64,512]{6,5,4,3,2,1,0:T(8,128)(2,1)} fusion(f32[2,2,2,2,2,64,512]{6,5,4,3,2,1,0:T(8,128)} %bitcast.141, pred[]{:T(512)S(6)} %eq.14), kind=kLoop, calls=%fused_computation.3 | loop fusion | flops 524288 | bytes 3145729 | tf_op jit(solution)/shard_map/convert_element_type | solution.py:567
  219.1 3.3 collective-permute-done.31
  225.2 1.7 collective-permute-done.32
  227.1 2.2 select_convert_fusion.2
  230.9 3.5 %collective-permute-start.34 = (bf16[1,1,1,1,1,64,128]{6,5,4,3,2,1,0:T(8,128)(2,1)S(1)}, bf16[1,1,1,1,1,64,128]{6,5,4,3,2,1,0:T(8,128)(2,1)S(1)}, u32[]{:S(2)}, u32[]{:S(2)}) collective-permute-start(bf16[1,1,1,1,1,64,128]{6,5,4,3,2,1,0:T(8,128)(2,1)S(1)} %select_convert_fusion.19), channel_id=1, source_target_pairs={{0,16},{4,20},{8,24},{12,28},{16,0},{20,4},{24,8},{28,12},{1,17},{... | collective-permute-start | bytes 49160 | tf_op jit(solution)/shard_map/ppermute | solution.py:523
  241.5 7.2 %collective-permute-done.21 = bf16[2,2,2,1,1,64,384]{6,5,4,3,2,1,0:T(8,128)(2,1)S(1)} collective-permute-done((bf16[2,2,2,1,1,64,384]{6,5,4,3,2,1,0:T(8,128)(2,1)S(1)}, bf16[2,2,2,1,1,64,384]{6,5,4,3,2,1,0:T(8,128)(2,1)S(1)}, u32[]{:S(2)}, u32[]{:S(2)}) %collective-permute-start.21) | collective-permute-done | bytes 393248 | tf_op jit(solution)/shard_map/ppermute | solution.py:523
  250.5 6.7 %collective-permute-done.26 = bf16[2,2,2,1,1,64,384]{6,5,4,3,2,1,0:T(8,128)(2,1)S(1)} collective-permute-done((bf16[2,2,2,1,1,64,384]{6,5,4,3,2,1,0:T(8,128)(2,1)S(1)}, bf16[2,2,2,1,1,64,384]{6,5,4,3,2,1,0:T(8,128)(2,1)S(1)}, u32[]{:S(2)}, u32[]{:S(2)}) %collective-permute-start.26) | collective-permute-done | bytes 393248 | tf_op jit(solution)/shard_map/ppermute | solution.py:523
  260.1 3.0 collective-permute-done.27
  264.4 3.0 collective-permute-start.24
  267.9 3.0 collective-permute-start.29
  271.0 2.0 collective-permute-done.29
  273.3 2.3 collective-permute-start.17
  275.8 4.1 %collective-permute-done.17 = bf16[2,2,1,1,1,64,512]{6,5,4,3,2,1,0:T(8,128)(2,1)S(1)} collective-permute-done((bf16[2,2,1,1,1,64,512]{6,5,4,3,2,1,0:T(8,128)(2,1)S(1)}, bf16[2,2,1,1,1,64,512]{6,5,4,3,2,1,0:T(8,128)(2,1)S(1)}, u32[]{:S(2)}, u32[]{:S(2)}) %collective-permute-start.17) | collective-permute-done | bytes 262176 | tf_op jit(solution)/shard_map/ppermute | solution.py:523
  281.2 4.1 %collective-permute-done.18 = bf16[2,1,1,1,1,64,512]{6,5,4,3,2,1,0:T(8,128)(2,1)S(1)} collective-permute-done((bf16[2,1,1,1,1,64,512]{6,5,4,3,2,1,0:T(8,128)(2,1)S(1)}, bf16[2,1,1,1,1,64,512]{6,5,4,3,2,1,0:T(8,128)(2,1)S(1)}, u32[]{:S(2)}, u32[]{:S(2)}) %collective-permute-start.18) | collective-permute-done | bytes 131104 | tf_op jit(solution)/shard_map/ppermute | solution.py:523
  285.4 2.9 collective-permute-start.19
  288.3 2.5 collective-permute-done.19
  291.8 2.7 concatenate.540
  294.5 2.7 collective-permute-start.35
  298.7 2.5 collective-permute-start.38
  301.2 1.8 collective-permute-start.39
  303.0 3.5 %collective-permute-start.40 = (f32[2708]{0:T(1024)S(1)}, f32[2708]{0:T(1024)S(1)}, u32[]{:S(2)}, u32[]{:S(2)}) collective-permute-start(f32[2708]{0:T(1024)S(1)} %concatenate.540), channel_id=1, source_target_pairs={{0,24},{4,28},{8,16},{12,20},{16,8},{20,12},{24,0},{28,4},{1,25},{... | collective-permute-start | bytes 32504 | tf_op jit(solution)/shard_map/ppermute | solution.py:523
  308.5 4.4 %collective-permute-done.41 = f32[2708]{0:T(1024)S(1)} collective-permute-done((f32[2708]{0:T(1024)S(1)}, f32[2708]{0:T(1024)S(1)}, u32[]{:S(2)}, u32[]{:S(2)}) %collective-permute-start.41) | collective-permute-done | bytes 10864 | tf_op jit(solution)/shard_map/ppermute | solution.py:523
  314.6 2.0 concatenate.541
  316.7 1.7 collective-permute-start.43
  (288 shorter events, 74.2 us)
Async XLA Ops:
  6.6 7.7 %collective-permute-start = (bf16[1,1,1,1,1,64,512]{6,5,0,1,2,4,3:T(8,128)(2,1)S(1)}, bf16[1,1,1,1,1,64,512]{6,5,0,1,2,4,3:T(8,128)(2,1)S(1)}, u32[]{:S(2)}, u32[]{:S(2)}) collective-permute-start(bf16[1,1,1,1,1,64,512]{6,5,0,1,2,4,3:T(8,128)(2,1)S(1)} %bitcast.154), channel_id=1, source_target_pairs={{0,16},{4,20},{8,24},{12,28},{16,0},{20,4},{24,8},{28,12},{1,17},{... | collective-permute-start | bytes 196616 | tf_op jit(solution)/shard_map/ppermute | solution.py:523
  14.3 5.0 %collective-permute-start.1 = (bf16[2,1,1,1,1,64,512]{6,5,0,1,2,4,3:T(8,128)(2,1)S(1)}, bf16[2,1,1,1,1,64,512]{6,5,0,1,2,4,3:T(8,128)(2,1)S(1)}, u32[]{:S(2)}, u32[]{:S(2)}) collective-permute-start(bf16[2,1,1,1,1,64,512]{6,5,0,1,2,4,3:T(8,128)(2,1)S(1)} %maximum_select_fusion.14), channel_id=1, source_target_pairs={{0,8},{4,12},{8,0},{12,4},{16,24},{20,28},{24,16},{28,20},{1,9},{5... | collective-permute-start | bytes 393224 | tf_op jit(solution)/shard_map/ppermute | solution.py:523
  19.4 6.4 %collective-permute-start.2 = (bf16[2,2,1,1,1,64,512]{6,5,0,1,2,4,3:T(8,128)(2,1)S(1)}, bf16[2,2,1,1,1,64,512]{6,5,0,1,2,4,3:T(8,128)(2,1)S(1)}, u32[]{:S(2)}, u32[]{:S(2)}) collective-permute-start(bf16[2,2,1,1,1,64,512]{6,5,0,1,2,4,3:T(8,128)(2,1)S(1)} %maximum_select_fusion.10), channel_id=1, source_target_pairs={{0,4},{4,0},{8,12},{12,8},{16,20},{20,16},{24,28},{28,24},{1,5},{5... | collective-permute-start | bytes 786440 | tf_op jit(solution)/shard_map/ppermute | solution.py:523
  25.9 9.9 %collective-permute-start.3 = (bf16[2,2,2,1,1,64,512]{6,5,0,1,2,4,3:T(8,128)(2,1)S(1)}, bf16[2,2,2,1,1,64,512]{6,5,0,1,2,4,3:T(8,128)(2,1)S(1)}, u32[]{:S(2)}, u32[]{:S(2)}) collective-permute-start(bf16[2,2,2,1,1,64,512]{6,5,0,1,2,4,3:T(8,128)(2,1)S(1)} %maximum_select_fusion.6), channel_id=1, source_target_pairs={{0,2},{1,3},{2,0},{3,1},{4,6},{5,7},{6,4},{7,5},{8,10},{9,11},{10,... | collective-permute-start | bytes 1572872 | tf_op jit(solution)/shard_map/ppermute | solution.py:523
  27.8 5.2 %collective-permute-start.5 = (bf16[1,1,1,1,1,64,384]{6,5,4,3,2,1,0:T(8,128)(2,1)S(1)}, bf16[1,1,1,1,1,64,384]{6,5,4,3,2,1,0:T(8,128)(2,1)S(1)}, u32[]{:S(2)}, u32[]{:S(2)}) collective-permute-start(bf16[1,1,1,1,1,64,384]{6,5,4,3,2,1,0:T(8,128)(2,1)S(1)} %pad_maximum_fusion.4), channel_id=1, source_target_pairs={{0,16},{4,20},{8,24},{12,28},{16,0},{20,4},{24,8},{28,12},{1,17},{... | collective-permute-start | bytes 147464 | tf_op jit(solution)/shard_map/ppermute | solution.py:523
  33.0 4.7 %collective-permute-start.6 = (bf16[2,1,1,1,1,64,384]{6,5,4,3,2,1,0:T(8,128)(2,1)S(1)}, bf16[2,1,1,1,1,64,384]{6,5,4,3,2,1,0:T(8,128)(2,1)S(1)}, u32[]{:S(2)}, u32[]{:S(2)}) collective-permute-start(bf16[2,1,1,1,1,64,384]{6,5,4,3,2,1,0:T(8,128)(2,1)S(1)} %maximum_select_fusion.17), channel_id=1, source_target_pairs={{0,8},{4,12},{8,0},{12,4},{16,24},{20,28},{24,16},{28,20},{1,9},{5... | collective-permute-start | bytes 294920 | tf_op jit(solution)/shard_map/ppermute | solution.py:523
  36.1 21.3 %collective-permute-start.4 = (bf16[2,2,2,2,1,64,512]{6,5,0,1,2,4,3:T(8,128)(2,1)S(1)}, bf16[2,2,2,2,1,64,512]{6,5,0,1,2,4,3:T(8,128)(2,1)S(1)}, u32[]{:S(2)}, u32[]{:S(2)}) collective-permute-start(bf16[2,2,2,2,1,64,512]{6,5,0,1,2,4,3:T(8,128)(2,1)S(1)} %maximum_select_fusion.3), channel_id=1, source_target_pairs={{0,1},{1,0},{2,3},{3,2},{4,5},{5,4},{6,7},{7,6},{8,9},{9,8},{10,11... | collective-permute-start | bytes 3145736 | tf_op jit(solution)/shard_map/ppermute | solution.py:523
  37.7 6.1 %collective-permute-start.7 = (bf16[2,2,1,1,1,64,384]{6,5,4,3,2,1,0:T(8,128)(2,1)S(1)}, bf16[2,2,1,1,1,64,384]{6,5,4,3,2,1,0:T(8,128)(2,1)S(1)}, u32[]{:S(2)}, u32[]{:S(2)}) collective-permute-start(bf16[2,2,1,1,1,64,384]{6,5,4,3,2,1,0:T(8,128)(2,1)S(1)} %maximum_select_fusion.13), channel_id=1, source_target_pairs={{0,4},{4,0},{8,12},{12,8},{16,20},{20,16},{24,28},{28,24},{1,5},{5... | collective-permute-start | bytes 589832 | tf_op jit(solution)/shard_map/ppermute | solution.py:523
  40.0 7.7 %collective-permute-start.10 = (bf16[1,1,1,1,1,64,512]{6,5,0,1,2,4,3:T(8,128)(2,1)S(1)}, bf16[1,1,1,1,1,64,512]{6,5,0,1,2,4,3:T(8,128)(2,1)S(1)}, u32[]{:S(2)}, u32[]{:S(2)}) collective-permute-start(bf16[1,1,1,1,1,64,512]{6,5,0,1,2,4,3:T(8,128)(2,1)S(1)} %bitcast.161), channel_id=1, source_target_pairs={{0,16},{4,20},{8,24},{12,28},{16,0},{20,4},{24,8},{28,12},{1,17},{... | collective-permute-start | bytes 196616 | tf_op jit(solution)/shard_map/ppermute | solution.py:523
  43.9 12.2 %collective-permute-start.8 = (bf16[2,2,2,1,1,64,384]{6,5,4,3,2,1,0:T(8,128)(2,1)S(1)}, bf16[2,2,2,1,1,64,384]{6,5,4,3,2,1,0:T(8,128)(2,1)}, u32[]{:S(2)}, u32[]{:S(2)}) collective-permute-start(bf16[2,2,2,1,1,64,384]{6,5,4,3,2,1,0:T(8,128)(2,1)S(1)} %maximum_select_fusion.9), channel_id=1, source_target_pairs={{0,2},{1,3},{2,0},{3,1},{4,6},{5,7},{6,4},{7,5},{8,10},{9,11},{10,... | collective-permute-start | bytes 1179656 | tf_op jit(solution)/shard_map/ppermute | solution.py:523
  47.7 5.2 %collective-permute-start.11 = (bf16[2,1,1,1,1,64,512]{6,5,0,1,2,4,3:T(8,128)(2,1)S(1)}, bf16[2,1,1,1,1,64,512]{6,5,0,1,2,4,3:T(8,128)(2,1)S(1)}, u32[]{:S(2)}, u32[]{:S(2)}) collective-permute-start(bf16[2,1,1,1,1,64,512]{6,5,0,1,2,4,3:T(8,128)(2,1)S(1)} %maximum_select_fusion.16), channel_id=1, source_target_pairs={{0,8},{4,12},{8,0},{12,4},{16,24},{20,28},{24,16},{28,20},{1,9},{5... | collective-permute-start | bytes 393224 | tf_op jit(solution)/shard_map/ppermute | solution.py:523
  52.9 7.3 %collective-permute-start.12 = (bf16[2,2,1,1,1,64,512]{6,5,0,1,2,4,3:T(8,128)(2,1)S(1)}, bf16[2,2,1,1,1,64,512]{6,5,0,1,2,4,3:T(8,128)(2,1)}, u32[]{:S(2)}, u32[]{:S(2)}) collective-permute-start(bf16[2,2,1,1,1,64,512]{6,5,0,1,2,4,3:T(8,128)(2,1)S(1)} %maximum_select_fusion.12), channel_id=1, source_target_pairs={{0,4},{4,0},{8,12},{12,8},{16,20},{20,16},{24,28},{28,24},{1,5},{5... | collective-permute-start | bytes 786440 | tf_op jit(solution)/shard_map/ppermute | solution.py:523
  57.4 17.7 %collective-permute-start.9 = (bf16[2,2,2,2,1,64,384]{6,5,4,3,2,1,0:T(8,128)(2,1)S(1)}, bf16[2,2,2,2,1,64,384]{6,5,4,3,2,1,0:T(8,128)(2,1)}, u32[]{:S(2)}, u32[]{:S(2)}) collective-permute-start(bf16[2,2,2,2,1,64,384]{6,5,4,3,2,1,0:T(8,128)(2,1)S(1)} %maximum_select_fusion.5), channel_id=1, source_target_pairs={{0,1},{1,0},{2,3},{3,2},{4,5},{5,4},{6,7},{7,6},{8,9},{9,8},{10,11... | collective-permute-start | bytes 2359304 | tf_op jit(solution)/shard_map/ppermute | solution.py:523
  61.6 12.0 %collective-permute-start.13 = (bf16[2,2,2,1,1,64,512]{6,5,0,1,2,4,3:T(8,128)(2,1)S(1)}, bf16[2,2,2,1,1,64,512]{6,5,0,1,2,4,3:T(8,128)(2,1)}, u32[]{:S(2)}, u32[]{:S(2)}) collective-permute-start(bf16[2,2,2,1,1,64,512]{6,5,0,1,2,4,3:T(8,128)(2,1)S(1)} %maximum_select_fusion.8), channel_id=1, source_target_pairs={{0,2},{1,3},{2,0},{3,1},{4,6},{5,7},{6,4},{7,5},{8,10},{9,11},{10,... | collective-permute-start | bytes 1572872 | tf_op jit(solution)/shard_map/ppermute | solution.py:523
  75.0 38.0 %collective-permute-start.14 = (bf16[2,2,2,2,1,64,512]{6,5,0,1,2,4,3:T(8,128)(2,1)S(1)}, bf16[2,2,2,2,1,64,512]{6,5,0,1,2,4,3:T(8,128)(2,1)S(1)}, u32[]{:S(2)}, u32[]{:S(2)}) collective-permute-start(bf16[2,2,2,2,1,64,512]{6,5,0,1,2,4,3:T(8,128)(2,1)S(1)} %maximum_select_fusion.4), channel_id=1, source_target_pairs={{0,1},{1,0},{2,3},{3,2},{4,5},{5,4},{6,7},{7,6},{8,9},{9,8},{10,11... | collective-permute-start | bytes 3145736 | tf_op jit(solution)/shard_map/ppermute | solution.py:523
  137.7 79.1 %collective-permute-start.30 = (bf16[2,2,2,2,1,64,128]{6,5,4,3,2,1,0:T(8,128)(2,1)S(1)}, bf16[2,2,2,2,1,64,128]{6,5,4,3,2,1,0:T(8,128)(2,1)S(1)}, u32[]{:S(2)}, u32[]{:S(2)}) collective-permute-start(bf16[2,2,2,2,1,64,128]{6,5,4,3,2,1,0:T(8,128)(2,1)S(1)} %select_convert_fusion.6), channel_id=1, source_target_pairs={{0,1},{1,0},{2,3},{3,2},{4,5},{5,4},{6,7},{7,6},{8,9},{9,8},{10,11... | collective-permute-start | bytes 786440 | tf_op jit(solution)/shard_map/ppermute | solution.py:523
  216.9 5.5 %collective-permute-start.31 = (bf16[2,2,2,1,1,64,128]{6,5,4,3,2,1,0:T(8,128)(2,1)S(1)}, bf16[2,2,2,1,1,64,128]{6,5,4,3,2,1,0:T(8,128)(2,1)S(1)}, u32[]{:S(2)}, u32[]{:S(2)}) collective-permute-start(bf16[2,2,2,1,1,64,128]{6,5,4,3,2,1,0:T(8,128)(2,1)S(1)} %select_convert_fusion.10), channel_id=1, source_target_pairs={{0,2},{1,3},{2,0},{3,1},{4,6},{5,7},{6,4},{7,5},{8,10},{9,11},{10,... | collective-permute-start | bytes 393224 | tf_op jit(solution)/shard_map/ppermute | solution.py:523
  222.5 4.3 %collective-permute-start.32 = (bf16[2,2,1,1,1,64,128]{6,5,4,3,2,1,0:T(8,128)(2,1)S(1)}, bf16[2,2,1,1,1,64,128]{6,5,4,3,2,1,0:T(8,128)(2,1)S(1)}, u32[]{:S(2)}, u32[]{:S(2)}) collective-permute-start(bf16[2,2,1,1,1,64,128]{6,5,4,3,2,1,0:T(8,128)(2,1)S(1)} %select_convert_fusion.14), channel_id=1, source_target_pairs={{0,4},{4,0},{8,12},{12,8},{16,20},{20,16},{24,28},{28,24},{1,5},{5... | collective-permute-start | bytes 196616 | tf_op jit(solution)/shard_map/ppermute | solution.py:523
  225.1 14.1 %collective-permute-start.15 = (bf16[2,2,2,2,1,64,512]{6,5,4,3,2,1,0:T(8,128)(2,1)}, bf16[2,2,2,2,1,64,512]{6,5,4,3,2,1,0:T(8,128)(2,1)S(1)}, u32[]{:S(2)}, u32[]{:S(2)}) collective-permute-start(bf16[2,2,2,2,1,64,512]{6,5,4,3,2,1,0:T(8,128)(2,1)} %select_convert_fusion), channel_id=1, source_target_pairs={{0,1},{1,0},{2,3},{3,2},{4,5},{5,4},{6,7},{7,6},{8,9},{9,8},{10,11... | collective-permute-start | bytes 3145736 | tf_op jit(solution)/shard_map/ppermute | solution.py:523
  226.9 4.0 %collective-permute-start.33 = (bf16[2,1,1,1,1,64,128]{6,5,4,3,2,1,0:T(8,128)(2,1)S(1)}, bf16[2,1,1,1,1,64,128]{6,5,4,3,2,1,0:T(8,128)(2,1)S(1)}, u32[]{:S(2)}, u32[]{:S(2)}) collective-permute-start(bf16[2,1,1,1,1,64,128]{6,5,4,3,2,1,0:T(8,128)(2,1)S(1)} %select_convert_fusion.18), channel_id=1, source_target_pairs={{0,8},{4,12},{8,0},{12,4},{16,24},{20,28},{24,16},{28,20},{1,9},{5... | collective-permute-start | bytes 98312 | tf_op jit(solution)/shard_map/ppermute | solution.py:523
  229.3 6.9 %collective-permute-start.20 = (bf16[2,2,2,2,1,64,384]{6,5,4,3,2,1,0:T(8,128)(2,1)S(1)}, bf16[2,2,2,2,1,64,384]{6,5,4,3,2,1,0:T(8,128)(2,1)S(1)}, u32[]{:S(2)}, u32[]{:S(2)}) collective-permute-start(bf16[2,2,2,2,1,64,384]{6,5,4,3,2,1,0:T(8,128)(2,1)S(1)} %select_convert_fusion.2), channel_id=1, source_target_pairs={{0,1},{1,0},{2,3},{3,2},{4,5},{5,4},{6,7},{7,6},{8,9},{9,8},{10,11... | collective-permute-start | bytes 2359304 | tf_op jit(solution)/shard_map/ppermute | solution.py:523
  230.9 5.2 %collective-permute-start.34 = (bf16[1,1,1,1,1,64,128]{6,5,4,3,2,1,0:T(8,128)(2,1)S(1)}, bf16[1,1,1,1,1,64,128]{6,5,4,3,2,1,0:T(8,128)(2,1)S(1)}, u32[]{:S(2)}, u32[]{:S(2)}) collective-permute-start(bf16[1,1,1,1,1,64,128]{6,5,4,3,2,1,0:T(8,128)(2,1)S(1)} %select_convert_fusion.19), channel_id=1, source_target_pairs={{0,16},{4,20},{8,24},{12,28},{16,0},{20,4},{24,8},{28,12},{1,17},{... | collective-permute-start | bytes 49160 | tf_op jit(solution)/shard_map/ppermute | solution.py:523
  234.5 3.7 %collective-permute-start.25 = (bf16[2,2,2,2,1,64,384]{6,5,4,3,2,1,0:T(8,128)(2,1)S(1)}, bf16[2,2,2,2,1,64,384]{6,5,4,3,2,1,0:T(8,128)(2,1)S(1)}, u32[]{:S(2)}, u32[]{:S(2)}) collective-permute-start(bf16[2,2,2,2,1,64,384]{6,5,4,3,2,1,0:T(8,128)(2,1)S(1)} %select_convert_fusion.1), channel_id=1, source_target_pairs={{0,1},{1,0},{2,3},{3,2},{4,5},{5,4},{6,7},{7,6},{8,9},{9,8},{10,11... | collective-permute-start | bytes 2359304 | tf_op jit(solution)/shard_map/ppermute | solution.py:523
  236.6 12.1 %collective-permute-start.21 = (bf16[2,2,2,1,1,64,384]{6,5,4,3,2,1,0:T(8,128)(2,1)S(1)}, bf16[2,2,2,1,1,64,384]{6,5,4,3,2,1,0:T(8,128)(2,1)S(1)}, u32[]{:S(2)}, u32[]{:S(2)}) collective-permute-start(bf16[2,2,2,1,1,64,384]{6,5,4,3,2,1,0:T(8,128)(2,1)S(1)} %select_convert_fusion.5), channel_id=1, source_target_pairs={{0,2},{1,3},{2,0},{3,1},{4,6},{5,7},{6,4},{7,5},{8,10},{9,11},{10,... | collective-permute-start | bytes 1179656 | tf_op jit(solution)/shard_map/ppermute | solution.py:523
  238.6 18.6 %collective-permute-start.26 = (bf16[2,2,2,1,1,64,384]{6,5,4,3,2,1,0:T(8,128)(2,1)S(1)}, bf16[2,2,2,1,1,64,384]{6,5,4,3,2,1,0:T(8,128)(2,1)S(1)}, u32[]{:S(2)}, u32[]{:S(2)}) collective-permute-start(bf16[2,2,2,1,1,64,384]{6,5,4,3,2,1,0:T(8,128)(2,1)S(1)} %select_convert_fusion.4), channel_id=1, source_target_pairs={{0,2},{1,3},{2,0},{3,1},{4,6},{5,7},{6,4},{7,5},{8,10},{9,11},{10,... | collective-permute-start | bytes 1179656 | tf_op jit(solution)/shard_map/ppermute | solution.py:523
  239.9 33.1 %collective-permute-start.16 = (bf16[2,2,2,1,1,64,512]{6,5,4,3,2,1,0:T(8,128)(2,1)S(1)}, bf16[2,2,2,1,1,64,512]{6,5,4,3,2,1,0:T(8,128)(2,1)S(1)}, u32[]{:S(2)}, u32[]{:S(2)}) collective-permute-start(bf16[2,2,2,1,1,64,512]{6,5,4,3,2,1,0:T(8,128)(2,1)S(1)} %select_convert_fusion.3), channel_id=1, source_target_pairs={{0,2},{1,3},{2,0},{3,1},{4,6},{5,7},{6,4},{7,5},{8,10},{9,11},{10,... | collective-permute-start | bytes 1572872 | tf_op jit(solution)/shard_map/ppermute | solution.py:523
  248.9 10.0 %collective-permute-start.22 = (bf16[2,2,1,1,1,64,384]{6,5,4,3,2,1,0:T(8,128)(2,1)S(1)}, bf16[2,2,1,1,1,64,384]{6,5,4,3,2,1,0:T(8,128)(2,1)S(1)}, u32[]{:S(2)}, u32[]{:S(2)}) collective-permute-start(bf16[2,2,1,1,1,64,384]{6,5,4,3,2,1,0:T(8,128)(2,1)S(1)} %select_convert_fusion.9), channel_id=1, source_target_pairs={{0,4},{4,0},{8,12},{12,8},{16,20},{20,16},{24,28},{28,24},{1,5},{5... | collective-permute-start | bytes 589832 | tf_op jit(solution)/shard_map/ppermute | solution.py:523
  257.3 5.7 %collective-permute-start.27 = (bf16[2,2,1,1,1,64,384]{6,5,4,3,2,1,0:T(8,128)(2,1)S(1)}, bf16[2,2,1,1,1,64,384]{6,5,4,3,2,1,0:T(8,128)(2,1)S(1)}, u32[]{:S(2)}, u32[]{:S(2)}) collective-permute-start(bf16[2,2,1,1,1,64,384]{6,5,4,3,2,1,0:T(8,128)(2,1)S(1)} %select_convert_fusion.8), channel_id=1, source_target_pairs={{0,4},{4,0},{8,12},{12,8},{16,20},{20,16},{24,28},{28,24},{1,5},{5... | collective-permute-start | bytes 589832 | tf_op jit(solution)/shard_map/ppermute | solution.py:523
  259.0 5.3 %collective-permute-start.23 = (bf16[2,1,1,1,1,64,384]{6,5,4,3,2,1,0:T(8,128)(2,1)S(1)}, bf16[2,1,1,1,1,64,384]{6,5,4,3,2,1,0:T(8,128)(2,1)S(1)}, u32[]{:S(2)}, u32[]{:S(2)}) collective-permute-start(bf16[2,1,1,1,1,64,384]{6,5,4,3,2,1,0:T(8,128)(2,1)S(1)} %select_convert_fusion.13), channel_id=1, source_target_pairs={{0,8},{4,12},{8,0},{12,4},{16,24},{20,28},{24,16},{28,20},{1,9},{5... | collective-permute-start | bytes 294920 | tf_op jit(solution)/shard_map/ppermute | solution.py:523
  263.2 4.7 %collective-permute-start.28 = (bf16[2,1,1,1,1,64,384]{6,5,4,3,2,1,0:T(8,128)(2,1)S(1)}, bf16[2,1,1,1,1,64,384]{6,5,4,3,2,1,0:T(8,128)(2,1)S(1)}, u32[]{:S(2)}, u32[]{:S(2)}) collective-permute-start(bf16[2,1,1,1,1,64,384]{6,5,4,3,2,1,0:T(8,128)(2,1)S(1)} %select_convert_fusion.12), channel_id=1, source_target_pairs={{0,8},{4,12},{8,0},{12,4},{16,24},{20,28},{24,16},{28,20},{1,9},{5... | collective-permute-start | bytes 294920 | tf_op jit(solution)/shard_map/ppermute | solution.py:523
  264.4 6.5 %collective-permute-start.24 = (bf16[1,1,1,1,1,64,384]{6,5,4,3,2,1,0:T(8,128)(2,1)S(1)}, bf16[1,1,1,1,1,64,384]{6,5,4,3,2,1,0:T(8,128)(2,1)S(1)}, u32[]{:S(2)}, u32[]{:S(2)}) collective-permute-start(bf16[1,1,1,1,1,64,384]{6,5,4,3,2,1,0:T(8,128)(2,1)S(1)} %select_convert_fusion.17), channel_id=1, source_target_pairs={{0,16},{4,20},{8,24},{12,28},{16,0},{20,4},{24,8},{28,12},{1,17},{... | collective-permute-start | bytes 147464 | tf_op jit(solution)/shard_map/ppermute | solution.py:523
  267.9 5.1 %collective-permute-start.29 = (bf16[1,1,1,1,1,64,384]{6,5,4,3,2,1,0:T(8,128)(2,1)S(1)}, bf16[1,1,1,1,1,64,384]{6,5,4,3,2,1,0:T(8,128)(2,1)S(1)}, u32[]{:S(2)}, u32[]{:S(2)}) collective-permute-start(bf16[1,1,1,1,1,64,384]{6,5,4,3,2,1,0:T(8,128)(2,1)S(1)} %select_convert_fusion.16), channel_id=1, source_target_pairs={{0,16},{4,20},{8,24},{12,28},{16,0},{20,4},{24,8},{28,12},{1,17},{... | collective-permute-start | bytes 147464 | tf_op jit(solution)/shard_map/ppermute | solution.py:523
  273.3 6.6 %collective-permute-start.17 = (bf16[2,2,1,1,1,64,512]{6,5,4,3,2,1,0:T(8,128)(2,1)S(1)}, bf16[2,2,1,1,1,64,512]{6,5,4,3,2,1,0:T(8,128)(2,1)S(1)}, u32[]{:S(2)}, u32[]{:S(2)}) collective-permute-start(bf16[2,2,1,1,1,64,512]{6,5,4,3,2,1,0:T(8,128)(2,1)S(1)} %select_convert_fusion.7), channel_id=1, source_target_pairs={{0,4},{4,0},{8,12},{12,8},{16,20},{20,16},{24,28},{28,24},{1,5},{5... | collective-permute-start | bytes 786440 | tf_op jit(solution)/shard_map/ppermute | solution.py:523
  280.2 60.6 %copy-start.8 = (f32[3,64,96]{2,1,0:T(8,128)S(1)}, f32[3,64,96]{2,1,0:T(8,128)}, u32[]{:S(2)}) copy-start(f32[3,64,96]{2,1,0:T(8,128)} %param.29) | copy-start | bytes 221188
  280.3 5.0 %collective-permute-start.18 = (bf16[2,1,1,1,1,64,512]{6,5,4,3,2,1,0:T(8,128)(2,1)S(1)}, bf16[2,1,1,1,1,64,512]{6,5,4,3,2,1,0:T(8,128)(2,1)S(1)}, u32[]{:S(2)}, u32[]{:S(2)}) collective-permute-start(bf16[2,1,1,1,1,64,512]{6,5,4,3,2,1,0:T(8,128)(2,1)S(1)} %select_convert_fusion.11), channel_id=1, source_target_pairs={{0,8},{4,12},{8,0},{12,4},{16,24},{20,28},{24,16},{28,20},{1,9},{5... | collective-permute-start | bytes 393224 | tf_op jit(solution)/shard_map/ppermute | solution.py:523
  281.2 60.3 %copy-start.7 = (f32[3,128,64]{1,2,0:T(8,128)S(1)}, f32[3,128,64]{1,2,0:T(8,128)}, u32[]{:S(2)}) copy-start(f32[3,128,64]{1,2,0:T(8,128)} %param.32) | copy-start | bytes 294916
  281.2 60.3 %copy-start.9 = (f32[3,64,128]{2,1,0:T(8,128)S(1)}, f32[3,64,128]{2,1,0:T(8,128)}, u32[]{:S(2)}) copy-start(f32[3,64,128]{2,1,0:T(8,128)} %param.31) | copy-start | bytes 294916
  285.4 5.3 %collective-permute-start.19 = (bf16[1,1,1,1,1,64,512]{6,5,4,3,2,1,0:T(8,128)(2,1)S(1)}, bf16[1,1,1,1,1,64,512]{6,5,4,3,2,1,0:T(8,128)(2,1)S(1)}, u32[]{:S(2)}, u32[]{:S(2)}) collective-permute-start(bf16[1,1,1,1,1,64,512]{6,5,4,3,2,1,0:T(8,128)(2,1)S(1)} %select_convert_fusion.15), channel_id=1, source_target_pairs={{0,16},{4,20},{8,24},{12,28},{16,0},{20,4},{24,8},{28,12},{1,17},{... | collective-permute-start | bytes 196616 | tf_op jit(solution)/shard_map/ppermute | solution.py:523
  294.5 8.5 %collective-permute-start.35 = (f32[2708]{0:T(1024)S(1)}, f32[2708]{0:T(1024)S(1)}, u32[]{:S(2)}, u32[]{:S(2)}) collective-permute-start(f32[2708]{0:T(1024)S(1)} %concatenate.540), channel_id=1, source_target_pairs={{0,4},{4,0},{8,12},{12,8},{16,20},{20,16},{24,28},{28,24},{1,5},{5... | collective-permute-start | bytes 32504 | tf_op jit(solution)/shard_map/ppermute | solution.py:523
  297.2 9.3 %collective-permute-start.36 = (f32[2708]{0:T(1024)S(1)}, f32[2708]{0:T(1024)S(1)}, u32[]{:S(2)}, u32[]{:S(2)}) collective-permute-start(f32[2708]{0:T(1024)S(1)} %concatenate.540), channel_id=1, source_target_pairs={{0,8},{4,12},{8,0},{12,4},{16,24},{20,28},{24,16},{28,20},{1,9},{5... | collective-permute-start | bytes 32504 | tf_op jit(solution)/shard_map/ppermute | solution.py:523
  297.9 9.9 %collective-permute-start.37 = (f32[2708]{0:T(1024)S(1)}, f32[2708]{0:T(1024)S(1)}, u32[]{:S(2)}, u32[]{:S(2)}) collective-permute-start(f32[2708]{0:T(1024)S(1)} %concatenate.540), channel_id=1, source_target_pairs={{0,12},{4,8},{8,4},{12,0},{16,28},{20,24},{24,20},{28,16},{1,13},{... | collective-permute-start | bytes 32504 | tf_op jit(solution)/shard_map/ppermute | solution.py:523
  298.7 9.1 %collective-permute-start.38 = (f32[2708]{0:T(1024)S(1)}, f32[2708]{0:T(1024)S(1)}, u32[]{:S(2)}, u32[]{:S(2)}) collective-permute-start(f32[2708]{0:T(1024)S(1)} %concatenate.540), channel_id=1, source_target_pairs={{0,16},{4,20},{8,24},{12,28},{16,0},{20,4},{24,8},{28,12},{1,17},{... | collective-permute-start | bytes 32504 | tf_op jit(solution)/shard_map/ppermute | solution.py:523
  301.2 6.6 %collective-permute-start.39 = (f32[2708]{0:T(1024)S(1)}, f32[2708]{0:T(1024)S(1)}, u32[]{:S(2)}, u32[]{:S(2)}) collective-permute-start(f32[2708]{0:T(1024)S(1)} %concatenate.540), channel_id=1, source_target_pairs={{0,20},{4,16},{8,28},{12,24},{16,4},{20,0},{24,12},{28,8},{1,21},{... | collective-permute-start | bytes 32504 | tf_op jit(solution)/shard_map/ppermute | solution.py:523
  303.0 5.5 %collective-permute-start.40 = (f32[2708]{0:T(1024)S(1)}, f32[2708]{0:T(1024)S(1)}, u32[]{:S(2)}, u32[]{:S(2)}) collective-permute-start(f32[2708]{0:T(1024)S(1)} %concatenate.540), channel_id=1, source_target_pairs={{0,24},{4,28},{8,16},{12,20},{16,8},{20,12},{24,0},{28,4},{1,25},{... | collective-permute-start | bytes 32504 | tf_op jit(solution)/shard_map/ppermute | solution.py:523
  306.5 6.4 %collective-permute-start.41 = (f32[2708]{0:T(1024)S(1)}, f32[2708]{0:T(1024)S(1)}, u32[]{:S(2)}, u32[]{:S(2)}) collective-permute-start(f32[2708]{0:T(1024)S(1)} %concatenate.540), channel_id=1, source_target_pairs={{0,28},{4,24},{8,20},{12,16},{16,12},{20,8},{24,4},{28,0},{1,29},{... | collective-permute-start | bytes 32504 | tf_op jit(solution)/shard_map/ppermute | solution.py:523
  316.6 3.2 collective-permute-start.42
  316.7 3.8 %collective-permute-start.43 = (f32[3240]{0:T(1024)S(1)}, f32[3240]{0:T(1024)S(1)}, u32[]{:S(2)}, u32[]{:S(2)}) collective-permute-start(f32[3240]{0:T(1024)S(1)} %concatenate.541), channel_id=1, source_target_pairs={{0,2},{1,3},{2,0},{3,1},{4,6},{5,7},{6,4},{7,5},{8,10},{9,11},{10,... | collective-permute-start | bytes 38888 | tf_op jit(solution)/shard_map/ppermute | solution.py:523
  318.3 3.2 collective-permute-start.44
  (38 other events, 1087.1 us)

commit v3 on v1

v3 whole, which is shorter than its diff:
```python
import functools

import jax
import jax.numpy as jnp
from jax import lax
from jax.experimental import pallas as pl
from jax.experimental.pallas import tpu as pltpu
from jax.sharding import PartitionSpec as P

D = 256
HEADS = 8
HEAD = D // HEADS
FF = 1024
CATS = 32
CLASSES = 32
LAYERS = 3
SEG = 48
MEM = 48
CTX = 96
VOCAB = 1024
GROUP = 4
ROWS = GROUP * CTX
SPREAD = HEADS * CTX
PARTS = [3 * D, D, FF, FF]
VMEM_BYTES = 56 * 1024 * 1024

decay_two = 0.9
step_rate = 0.3
clip_limit = 0.05
tiny_term = 1e-30
norm_eps = 1e-06
masked_score = -1e30
log2_e = 1.4426950408889634
score_scale = HEAD ** (-0.5)
gelu_one = 0.7978845608028654
gelu_two = 0.044715


def dot_nn(left, right):
    return lax.dot_general(
        left, right, (((1,), (0,)), ((), ())), preferred_element_type=jnp.float32
    )


def dot_nt(left, right):
    return lax.dot_general(
        left, right, (((1,), (1,)), ((), ())), preferred_element_type=jnp.float32
    )


def dot_tn(left, right):
    return lax.dot_general(
        left, right, (((0,), (0,)), ((), ())), preferred_element_type=jnp.float32
    )


def inverse_rms(values):
    return lax.rsqrt(jnp.mean(values * values, axis=-1, keepdims=True) + norm_eps)


def rms_back(values, inverse, gain_row, upstream):
    normed = values * inverse
    scaled = upstream * gain_row
    inner = jnp.mean(scaled * normed, axis=-1, keepdims=True)
    return (
        inverse * (scaled - normed * inner),
        jnp.sum(upstream * normed, axis=0, keepdims=True),
    )


def head_masks():
    lane = lax.broadcasted_iota(jnp.int32, (1, D // 2), 1) // HEAD
    return [lane == head for head in range(HEADS // 2)]


def expand_heads(rows, masks):
    half = D // 2
    nothing = jnp.zeros((rows.shape[0], half), rows.dtype)
    pieces = []
    for head in range(HEADS):
        side, at = divmod(head, HEADS // 2)
        kept = rows[:, side * half : (side + 1) * half] * masks[at].astype(rows.dtype)
        pair = [kept, nothing] if side == 0 else [nothing, kept]
        pieces.append(jnp.concatenate(pair, axis=1))
    return jnp.concatenate(pieces, axis=0)


def collapse_heads(spread, rows, masks):
    half, span = D // 2, spread.shape[1] // 2
    queries = span // (HEADS // 2)
    sides = []
    for side in range(2):
        product = dot_tn(
            spread[:, side * span : (side + 1) * span], rows[:, side * half : (side + 1) * half]
        )
        taken = product[(HEADS // 2 - 1) * queries :]
        for at in range(HEADS // 2 - 1):
            taken = jnp.where(masks[at], product[at * queries : (at + 1) * queries], taken)
        sides.append(taken)
    return jnp.concatenate(sides, axis=1)


def fill_bias(bias_ref):
    spread = bias_ref.shape[2]
    queries = spread // HEADS
    key_at = lax.broadcasted_iota(jnp.int32, (CTX, spread), 0)
    query_at = lax.broadcasted_iota(jnp.int32, (CTX, spread), 1) % queries + (CTX - queries)
    later = key_at > query_at
    crosses = (query_at >= MEM) & (key_at < MEM)
    bias_ref[0] = jnp.where(later | crosses, masked_score, 0.0)
    bias_ref[1] = jnp.where(later, masked_score, 0.0)


def block_place(outer_at, inner_high, outer_bits, inner_bits):
    place = 0
    for bit in range(outer_bits):
        place |= ((outer_at >> bit) & 1) << (outer_bits - 1 - bit)
    for bit in range(inner_bits - 1):
        place |= ((inner_high >> bit) & 1) << (outer_bits + inner_bits - 2 - bit)
    return place


def place_weights(targets, own_ref, other_ref, core, widths, bits, start=0):
    outer_bits, inner_bits = bits
    rows = own_ref.shape[1]
    for high in range(1 << (inner_bits - 1)):
        for source, side in ((own_ref, core), (other_ref, 1 - core)):
            here = pl.ds(pl.multiple_of((2 * high + side) * rows, rows), rows)
            at = start
            for (target, column), width in zip(targets, widths):
                block = [
                    source[block_place(outer, high, outer_bits, inner_bits), :, at : at + width]
                    for outer in range(1 << outer_bits)
                ]
                target[here, column : column + (width << outer_bits)] = jnp.concatenate(
                    block, axis=1
                )
                at += width


def write_blocks(send_ref, keep_ref, sum_ref, core, widths, bits):
    outer_bits, inner_bits = bits
    rows = keep_ref.shape[1]
    for high in range(1 << (inner_bits - 1)):
        for target, side in ((keep_ref, core), (send_ref, 1 - core)):
            here = pl.ds(pl.multiple_of((2 * high + side) * rows, rows), rows)
            taken = sum_ref[here, :]
            for outer in range(1 << outer_bits):
                block, column = [], 0
                for width in widths:
                    block.append(taken[:, column + outer * width : column + (outer + 1) * width])
                    column += width << outer_bits
                target[block_place(outer, high, outer_bits, inner_bits)] = jnp.concatenate(
                    block, axis=1
                ).astype(target.dtype)


def one_hot_rows(latent_rows):
    spot = lax.broadcasted_iota(jnp.int32, (CATS, VOCAB), 1) // CLASSES
    group = lax.broadcasted_iota(jnp.int32, (CATS, VOCAB), 0)
    spreader = jnp.where(spot == group, 1.0, 0.0).astype(jnp.bfloat16)
    classes = (lax.broadcasted_iota(jnp.int32, (1, VOCAB), 1) % CLASSES).astype(jnp.float32)
    drawn = dot_nn(latent_rows, spreader)
    return jnp.where(drawn == classes, 1.0, 0.0).astype(jnp.bfloat16)


def tail_rows(values, queries):
    if queries == CTX:
        return values
    return jnp.concatenate(
        [
            values[(sample + 1) * CTX - queries : (sample + 1) * CTX]
            for sample in range(values.shape[0] // CTX)
        ],
        axis=0,
    )


def attend_forward(step, hidden, gain_row, weight_ref, valid_ref, bias_ref, masks, refs):
    middle_ref, qkv_ref, mix_ref, lse_ref = refs
    queries = lse_ref.shape[2] // HEADS
    normed = (hidden * inverse_rms(hidden) * gain_row).astype(jnp.bfloat16)
    qkv_ref[...] = dot_nn(normed, weight_ref[:, 0 : 3 * D]).astype(jnp.bfloat16)
    for sample in range(GROUP):
        rows = slice(sample * CTX, (sample + 1) * CTX)
        spread = expand_heads(qkv_ref[(sample + 1) * CTX - queries : (sample + 1) * CTX, 0:D], masks)
        scores = dot_nt(qkv_ref[rows, D : 2 * D], spread)
        scores = scores + bias_ref[valid_ref[step * GROUP + sample]]
        peak = jnp.max(scores, axis=0, keepdims=True)
        exponent = jnp.exp2((scores - peak) * (score_scale * log2_e))
        total = jnp.sum(exponent, axis=0, keepdims=True)
        chance = (exponent * (1.0 / total)).astype(jnp.bfloat16)
        mix_ref[sample * queries : (sample + 1) * queries, :] = collapse_heads(
            chance, qkv_ref[rows, 2 * D : 3 * D], masks
        ).astype(jnp.bfloat16)
        lse_ref[sample] = peak * (score_scale * log2_e) + jnp.log2(total)
    middle_ref[...] = tail_rows(hidden, queries) + dot_nn(
        mix_ref[...], weight_ref[:, 3 * D : 4 * D]
    )


def gelu_bend(value, square):
    return jnp.tanh(value * (gelu_one + (gelu_one * gelu_two) * square))


def gelu_slope(half_value, bend, square):
    return (0.5 + 0.5 * bend) + (half_value * (1.0 - bend * bend)) * (
        gelu_one + (3.0 * gelu_one * gelu_two) * square
    )


def feed_forward(middle, gain_row, weight_ref, inner_ref):
    normed = (middle * inverse_rms(middle) * gain_row).astype(jnp.bfloat16)
    for part in range(FF // D):
        columns = slice(part * D, (part + 1) * D)
        inner = dot_nn(normed, weight_ref[:, columns])
        for sample in range(GROUP):
            rows = slice(sample * CTX, (sample + 1) * CTX)
            value = inner[rows]
            bend = gelu_bend(value, value * value)
            inner_ref[rows, columns] = ((0.5 * value) * (1.0 + bend)).astype(jnp.bfloat16)
    return middle + dot_nt(inner_ref[...], weight_ref[:, FF : 2 * FF])


def feed_back(here, upstream, middle, gain_row, weight_ref, refs):
    normed_ref, inner_ref, dinner_ref, dout_ref = refs
    dout = upstream.astype(jnp.bfloat16)
    dout_ref[here(0, ROWS), :] = dout
    inverse = inverse_rms(middle)
    normed = (middle * inverse * gain_row).astype(jnp.bfloat16)
    normed_ref[here(0, ROWS), :] = normed
    for part in range(FF // D):
        columns = slice(part * D, (part + 1) * D)
        inner = dot_nn(normed, weight_ref[:, columns])
        dact = dot_nn(dout, weight_ref[:, FF + part * D : FF + (part + 1) * D])
        for sample in range(GROUP):
            rows = slice(sample * CTX, (sample + 1) * CTX)
            there = here(sample * CTX, CTX)
            value = inner[rows]
            square = value * value
            bend = gelu_bend(value, square)
            half_value = 0.5 * value
            inner_ref[there, columns] = (half_value * (1.0 + bend)).astype(jnp.bfloat16)
            dinner_ref[there, columns] = (
                dact[rows] * gelu_slope(half_value, bend, square)
            ).astype(jnp.bfloat16)
    dnormed = dot_nt(dinner_ref[here(0, ROWS), :], weight_ref[:, 0:FF])
    through, gain_part = rms_back(middle, inverse, gain_row, dnormed)
    return upstream + through, gain_part


def attend_back(step, here, saved, dmiddle, gain_row, weight_ref, valid_ref, bias_ref, masks, refs):
    hidden, qkv_ref, mix_ref, lse_ref = saved
    normed_ref, dmiddle_ref, dqkv_ref, mixes_ref = refs
    queries = lse_ref.shape[2] // HEADS
    short = here(0, GROUP * queries, queries)
    dattend = dmiddle.astype(jnp.bfloat16)
    dmiddle_ref[short, :] = dattend
    mixes_ref[short, :] = mix_ref[...]
    dmix = dot_nt(dattend, weight_ref[:, 3 * D : 4 * D]).astype(jnp.bfloat16)
    for sample in range(GROUP):
        rows = slice(sample * CTX, (sample + 1) * CTX)
        there = here(sample * CTX, CTX)
        spread = expand_heads(qkv_ref[(sample + 1) * CTX - queries : (sample + 1) * CTX, 0:D], masks)
        keys = qkv_ref[rows, D : 2 * D]
        slopes = expand_heads(dmix[sample * queries : (sample + 1) * queries], masks)
        scores = dot_nt(keys, spread) + bias_ref[valid_ref[step * GROUP + sample]]
        chance = jnp.exp2(scores * (score_scale * log2_e) - lse_ref[sample])
        dchance = dot_nt(qkv_ref[rows, 2 * D : 3 * D], slopes)
        weighed = chance * dchance
        dscore = (weighed - chance * jnp.sum(weighed, axis=0, keepdims=True)).astype(jnp.bfloat16)
        dvalues = dot_nn(chance.astype(jnp.bfloat16), slopes)
        dkeys = dot_nn(dscore, spread) * score_scale
        dqueries = (collapse_heads(dscore, keys, masks) * score_scale).astype(jnp.bfloat16)
        if queries < CTX:
            nothing = jnp.zeros((CTX - queries, D), jnp.bfloat16)
            dqueries = jnp.concatenate([nothing, dqueries], axis=0)
        dqkv_ref[there, 0:D] = dqueries
        dqkv_ref[there, D : 2 * D] = dkeys.astype(jnp.bfloat16)
        dqkv_ref[there, 2 * D : 3 * D] = dvalues.astype(jnp.bfloat16)
    inverse = inverse_rms(hidden)
    normed_ref[here(0, ROWS), :] = (hidden * inverse * gain_row).astype(jnp.bfloat16)
    dnormed = dot_nt(dqkv_ref[here(0, ROWS), :], weight_ref[:, 0 : 3 * D])
    through, gain_part = rms_back(hidden, inverse, gain_row, dnormed)
    if queries < CTX:
        nothing = jnp.zeros((CTX - queries, D), jnp.float32)
        pieces = []
        for sample in range(GROUP):
            pieces = pieces + [nothing, dmiddle[sample * queries : (sample + 1) * queries]]
        dmiddle = jnp.concatenate(pieces, axis=0)
    return dmiddle + through, gain_part


def row_spec(width, rows=ROWS):
    return pl.BlockSpec((rows, width), lambda step: (step, 0))


def lse_spec(queries):
    return pl.BlockSpec((GROUP, 1, HEADS * queries), lambda step: (step, 0, 0))


def whole_spec(shape):
    return pl.BlockSpec(shape, lambda step: (0,) * len(shape))


def smem_spec():
    return pl.BlockSpec(memory_space=pltpu.SMEM)


def forward_kernel(layer, widths, bits, source_ref, own_ref, other_ref, gains_ref, valid_ref, core_ref, *refs):
    entry_ref, att_ref, before_ref, bias_ref = refs[0], refs[5], refs[6], refs[7]
    step = pl.program_id(0)

    @pl.when(step == 0)
    def _():
        fill_bias(bias_ref)
        att = [(att_ref, 0), (att_ref, 3 * D)]
        before = [(before_ref, 0)] if layer == 0 else [(before_ref, 0), (before_ref, FF)]
        targets = att + before if layer == 0 else before + att
        place_weights(targets, own_ref, other_ref, core_ref[0], widths[: len(targets)], bits)

    if layer == 0:
        hidden = dot_nt(one_hot_rows(source_ref[...]), before_ref[...])
    else:
        gain_ffn = gains_ref[LAYERS + layer - 1 : LAYERS + layer, :]
        hidden = feed_forward(source_ref[...], gain_ffn, before_ref, refs[8])
    entry_ref[...] = hidden
    attend_forward(
        step,
        hidden,
        gains_ref[layer : layer + 1, :],
        att_ref,
        valid_ref,
        bias_ref,
        head_masks(),
        refs[1:5],
    )


def run_forward(layer, widths, bits, source, own, other, gains, valid, core):
    tokens = source.shape[0]
    queries = SEG if layer == LAYERS - 1 else CTX
    f32, b16 = jnp.float32, jnp.bfloat16
    shape = jax.ShapeDtypeStruct
    short = tokens // CTX * queries
    outs = [
        (shape((tokens, D), f32), row_spec(D)),
        (shape((short, D), f32), row_spec(D, GROUP * queries)),
        (shape((tokens, 3 * D), b16), row_spec(3 * D)),
        (shape((short, D), b16), row_spec(D, GROUP * queries)),
        (shape((tokens // CTX, 1, HEADS * queries), f32), lse_spec(queries)),
        (shape((D, 4 * D), b16), whole_spec((D, 4 * D))),
    ]
    scratch = [pltpu.VMEM((2, CTX, HEADS * queries), f32)]
    if layer == 0:
        scratch = [pltpu.VMEM((D, VOCAB), b16)] + scratch
    else:
        outs.append((shape((D, 2 * FF), b16), whole_spec((D, 2 * FF))))
        scratch.append(pltpu.VMEM((ROWS, FF), b16))
    return pl.pallas_call(
        functools.partial(forward_kernel, layer, widths, bits),
        grid=(tokens // ROWS,),
        in_specs=[
            row_spec(source.shape[1]),
            whole_spec(own.shape),
            whole_spec(other.shape),
            whole_spec(gains.shape),
            smem_spec(),
            smem_spec(),
        ],
        out_specs=[spec for _, spec in outs],
        out_shape=[item for item, _ in outs],
        scratch_shapes=scratch,
        compiler_params=pltpu.CompilerParams(vmem_limit_bytes=VMEM_BYTES),
        cost_estimate=pl.CostEstimate(
            flops=2 * tokens * D * 12 * D,
            bytes_accessed=tokens * D * 16 + D * 12 * D * 4,
            transcendentals=tokens * (FF + HEADS * CTX),
        ),
        name="forward_part",
    )(source, own, other, gains, valid, core)


def top_kernel(widths, bits, start, middle_ref, own_ref, other_ref, targets_ref, counted_ref, gains_ref, core_ref, *refs):
    dmiddle_ref, send_ref, keep_ref, gain_ref, loss_ref = refs[:5]
    weight_ref, head_ref, turned_ref, final_ref, dlogits_ref = refs[5:10]
    normed_ref, inner_ref, slope_ref, dinner_ref, dout_ref, last_ref, sum_ref = refs[10:]
    tokens = middle_ref.shape[0]
    gain_final = gains_ref[2 * LAYERS : 2 * LAYERS + 1, :]
    gain_ffn = gains_ref[2 * LAYERS - 1 : 2 * LAYERS, :]
    place_weights(
        [(weight_ref, 0), (weight_ref, FF), (head_ref, 0)],
        own_ref,
        other_ref,
        core_ref[0],
        widths,
        bits,
        start,
    )
    turned_ref[...] = head_ref[...].T
    for block in range(tokens // ROWS):
        rows = slice(block * ROWS, (block + 1) * ROWS)
        middle = middle_ref[rows, :]
        normed = (middle * inverse_rms(middle) * gain_ffn).astype(jnp.bfloat16)
        normed_ref[rows, :] = normed
        for part in range(FF // D):
            columns = slice(part * D, (part + 1) * D)
            inner = dot_nn(normed, weight_ref[:, columns])
            for piece in range(GROUP):
                value = inner[piece * CTX : (piece + 1) * CTX]
                there = slice(block * ROWS + piece * CTX, block * ROWS + (piece + 1) * CTX)
                square = value * value
                bend = gelu_bend(value, square)
                half_value = 0.5 * value
                inner_ref[there, columns] = (half_value * (1.0 + bend)).astype(jnp.bfloat16)
                slope_ref[there, columns] = gelu_slope(half_value, bend, square)
        last = middle + dot_nt(inner_ref[rows, :], weight_ref[:, FF : 2 * FF])
        last_ref[rows, :] = last
        final_ref[rows, :] = (last * inverse_rms(last) * gain_final).astype(jnp.bfloat16)
    span = D
    loss = jnp.zeros((1, span), jnp.float32)
    spots = lax.broadcasted_iota(jnp.int32, (CLASSES, span), 0)
    for part in range(tokens // span):
        columns = slice(part * span, (part + 1) * span)
        counted = counted_ref[0:1, columns]
        final = final_ref[columns, :]
        for quarter in range(VOCAB // D):
            logits = dot_nt(turned_ref[quarter * D : (quarter + 1) * D, :], final)
            for inside in range(D // CLASSES):
                group = quarter * (D // CLASSES) + inside
                values = logits[inside * CLASSES : (inside + 1) * CLASSES]
                shifted = values - jnp.max(values, axis=0, keepdims=True)
                exponent = jnp.exp2(shifted * log2_e)
                total = jnp.sum(exponent, axis=0, keepdims=True)
                hot = spots == targets_ref[group : group + 1, columns]
                chosen = jnp.sum(jnp.where(hot, shifted, 0.0), axis=0, keepdims=True)
                loss = loss + counted * (jnp.log(total) - chosen)
                chance = exponent * (1.0 / total)
                slope = (chance - jnp.where(hot, 1.0, 0.0)) * counted
                dlogits_ref[group * CLASSES : (group + 1) * CLASSES, columns] = slope.astype(
                    jnp.bfloat16
                )
    loss_ref[...] = jnp.sum(loss, axis=1, keepdims=True)
    sum_ref[:, 2 * FF :] = dot_nt(final_ref[...].T, dlogits_ref[...])
    dfinal = dot_nn(head_ref[...], dlogits_ref[...]).T
    last = last_ref[...]
    dlast, gain_part = rms_back(last, inverse_rms(last), gain_final, dfinal)
    gain_ref[1:2, :] = gain_part
    last_ref[...] = dlast
    gain_sum = jnp.zeros((1, D), jnp.float32)
    for block in range(tokens // ROWS):
        rows = slice(block * ROWS, (block + 1) * ROWS)
        upstream = last_ref[rows, :]
        dout = upstream.astype(jnp.bfloat16)
        dout_ref[rows, :] = dout
        for part in range(FF // D):
            columns = slice(part * D, (part + 1) * D)
            dact = dot_nn(dout, weight_ref[:, FF + part * D : FF + (part + 1) * D])
            dinner_ref[rows, columns] = (dact * slope_ref[rows, columns]).astype(jnp.bfloat16)
        dnormed = dot_nt(dinner_ref[rows, :], weight_ref[:, 0:FF])
        middle = middle_ref[rows, :]
        through, gain_part = rms_back(middle, inverse_rms(middle), gain_ffn, dnormed)
        gain_sum = gain_sum + gain_part
        dmiddle_ref[rows, :] = upstream + through
    gain_ref[0:1, :] = gain_sum
    sum_ref[:, 0:FF] = dot_nn(normed_ref[...].T, dinner_ref[...])
    sum_ref[:, FF : 2 * FF] = dot_nn(dout_ref[...].T, inner_ref[...])
    write_blocks(send_ref, keep_ref, sum_ref, core_ref[0], widths, bits)


def block_outs(own, widths):
    shape = jax.ShapeDtypeStruct
    blocks = own.shape[:2] + (sum(widths),)
    return [shape(blocks, jnp.bfloat16), shape(blocks, jnp.float32)]


def run_top(widths, bits, start, middle, own, other, targets, counted, gains, core):
    tokens = middle.shape[0]
    f32, b16 = jnp.float32, jnp.bfloat16
    shape = jax.ShapeDtypeStruct
    vmem = pl.BlockSpec(memory_space=pltpu.VMEM)
    return pl.pallas_call(
        functools.partial(top_kernel, widths, bits, start),
        in_specs=[vmem] * 6 + [smem_spec()],
        out_specs=[vmem] * 5,
        out_shape=[shape((tokens, D), f32)]
        + block_outs(own, widths)
        + [shape((2, D), f32), shape((1, 1), f32)],
        scratch_shapes=[
            pltpu.VMEM((D, 2 * FF), b16),
            pltpu.VMEM((D, VOCAB), b16),
            pltpu.VMEM((VOCAB, D), b16),
            pltpu.VMEM((tokens, D), b16),
            pltpu.VMEM((VOCAB, tokens), b16),
            pltpu.VMEM((tokens, D), b16),
            pltpu.VMEM((tokens, FF), b16),
            pltpu.VMEM((tokens, FF), f32),
            pltpu.VMEM((tokens, FF), b16),
            pltpu.VMEM((tokens, D), b16),
            pltpu.VMEM((tokens, D), f32),
            pltpu.VMEM((D, 2 * FF + VOCAB), f32),
        ],
        compiler_params=pltpu.CompilerParams(vmem_limit_bytes=VMEM_BYTES),
        cost_estimate=pl.CostEstimate(
            flops=6 * tokens * D * 3 * FF,
            bytes_accessed=tokens * D * 8 + D * 3 * FF * 10,
            transcendentals=tokens * (FF + VOCAB),
        ),
        name="loss_part",
    )(middle, own, other, targets, counted, gains, core)


def backward_kernel(layer, widths, bits, *refs):
    entry_ref, qkv_ref, mix_ref, lse_ref, dmiddle_ref, att_ref = refs[:6]
    gains_ref, valid_ref, core_ref = refs[6:9]
    if layer == 0:
        latent_ref, send_ref, keep_ref, gain_ref, bias_ref = refs[9:14]
        att_kept, before_kept, sum_ref = refs[14:18], refs[18:20], refs[20]
    else:
        before_ref, ffn_ref, out_ref, send_ref, keep_ref, gain_ref, bias_ref = refs[9:16]
        att_kept, before_kept, sum_ref = refs[16:20], refs[20:24], refs[24]
    step = pl.program_id(0)

    def here(start, length, unit=CTX):
        base = step * (GROUP * unit)
        return pl.ds(pl.multiple_of(base + start, 16), length)

    @pl.when(step == 0)
    def _():
        fill_bias(bias_ref)
        gain_ref[...] = jnp.zeros_like(gain_ref)

    dentry, gain_part = attend_back(
        step,
        here,
        (entry_ref[...], qkv_ref, mix_ref, lse_ref),
        dmiddle_ref[...],
        gains_ref[layer : layer + 1, :],
        att_ref,
        valid_ref,
        bias_ref,
        head_masks(),
        att_kept,
    )
    gain_ref[0:1, :] += gain_part
    if layer == 0:
        before_kept[0][here(0, ROWS), :] = dentry.astype(jnp.bfloat16)
        before_kept[1][here(0, ROWS), :] = one_hot_rows(latent_ref[...])
    else:
        dbefore, gain_part = feed_back(
            here,
            dentry,
            before_ref[...],
            gains_ref[LAYERS + layer - 1 : LAYERS + layer, :],
            ffn_ref,
            before_kept,
        )
        out_ref[...] = dbefore
        gain_ref[1:2, :] += gain_part

    @pl.when(step == pl.num_programs(0) - 1)
    def _():
        normed_ref, dattend_ref, dqkv_ref, mixes_ref = att_kept
        att = [(normed_ref, dqkv_ref), (mixes_ref, dattend_ref)]
        if layer == 0:
            pairs = att + [(before_kept[0], before_kept[1])]
        else:
            normed_two_ref, inner_ref, dinner_ref, dout_ref = before_kept
            pairs = [(normed_two_ref, dinner_ref), (dout_ref, inner_ref)] + att
        column = 0
        for left, right in pairs:
            wide = right.shape[1]
            sum_ref[:, column : column + wide] = dot_nn(left[...].T, right[...])
            column += wide
        write_blocks(send_ref, keep_ref, sum_ref, core_ref[0], widths, bits)


def run_backward(layer, widths, bits, blocks_like, saved, dmiddle, gains, valid, core, before):
    entry, _, qkv, mix, lse, weights = saved[:6]
    tokens = entry.shape[0]
    queries = lse.shape[2] // HEADS
    short = tokens // CTX * queries
    f32, b16 = jnp.float32, jnp.bfloat16
    shape = jax.ShapeDtypeStruct
    in_specs = [
        row_spec(D),
        row_spec(3 * D),
        row_spec(D, GROUP * queries),
        lse_spec(queries),
        row_spec(D, GROUP * queries),
        whole_spec(weights.shape),
        whole_spec(gains.shape),
        smem_spec(),
        smem_spec(),
    ]
    operands = [entry, qkv, mix, lse, dmiddle, weights, gains, valid, core]
    blocks = block_outs(blocks_like, widths)
    outs = [(item, whole_spec(item.shape)) for item in blocks]
    outs.append((shape((2, D), f32), whole_spec((2, D))))
    scratch = [
        pltpu.VMEM((2, CTX, HEADS * queries), f32),
        pltpu.VMEM((tokens, D), b16),
        pltpu.VMEM((short, D), b16),
        pltpu.VMEM((tokens, 3 * D), b16),
        pltpu.VMEM((short, D), b16),
    ]
    if layer == 0:
        in_specs.append(row_spec(CATS))
        operands.append(before)
        scratch = scratch + [pltpu.VMEM((tokens, D), b16), pltpu.VMEM((tokens, VOCAB), b16)]
        wide = 4 * D + VOCAB
    else:
        in_specs = in_specs + [row_spec(D), whole_spec(before[1].shape)]
        operands = operands + list(before)
        outs.insert(0, (shape((tokens, D), f32), row_spec(D)))
        scratch = scratch + [
            pltpu.VMEM((tokens, D), b16),
            pltpu.VMEM((tokens, FF), b16),
            pltpu.VMEM((tokens, FF), b16),
            pltpu.VMEM((tokens, D), b16),
        ]
        wide = 4 * D + 2 * FF
    return pl.pallas_call(
        functools.partial(backward_kernel, layer, widths, bits),
        grid=(tokens // ROWS,),
        in_specs=in_specs,
        out_specs=[spec for _, spec in outs],
        out_shape=[item for item, _ in outs],
        scratch_shapes=scratch + [pltpu.VMEM((D, wide), f32)],
        compiler_params=pltpu.CompilerParams(vmem_limit_bytes=VMEM_BYTES),
        cost_estimate=pl.CostEstimate(
            flops=6 * tokens * D * wide,
            bytes_accessed=tokens * D * 24 + D * wide * 6,
            transcendentals=tokens * (FF + HEADS * CTX),
        ),
        name="backward_part",
    )(*operands)


def matrix_plan(widths):
    order = [
        (2, 2), (3, 2), (5, 0), (2, 1), (3, 1), (0, 2), (1, 2),
        (2, 0), (3, 0), (0, 1), (1, 1), (0, 0), (1, 0), (4, 0),
    ]
    plan, column = {}, 0
    for which, layer in order:
        plan[(which, layer)] = (column, widths[which])
        column += widths[which]
    return plan, column


def matrix_list():
    return [(which, layer) for which in range(4) for layer in range(LAYERS)] + [(4, 0), (5, 0)]


MATRICES = 4 * LAYERS + 2
LANES = 128
INNER_ROWS = 16
COMMON_ROWS = 16
ROW_IS_INNER = [True, True, True, False, False, True]


def master_of(masters, which, layer):
    if which == 1:
        return masters[1][layer].T
    return masters[which][layer] if which < 4 else masters[which][...]


def old_row(refs, which, layer):
    return refs[which][layer : layer + 1, :] if which < 4 else refs[which][...]


def stats_kernel(widths, *refs):
    raw_early, raw_late, masters, row_refs = refs[0], refs[1], refs[2:8], refs[8:14]
    gains_at, loss_ref, counted_ref, packet_ref = refs[14:18], refs[18], refs[19], refs[20]
    plan, total = matrix_plan(widths)
    square = jnp.concatenate([raw_early[...] * raw_early[...], raw_late[...] * raw_late[...]], axis=1)
    rows = square.shape[0]
    one = lambda value: jnp.sum(jnp.sum(value, axis=1, keepdims=True), axis=0, keepdims=True)
    inner, weights, entries, row_sums = [], [], [], []
    for which, layer in matrix_list():
        column, width = plan[(which, layer)]
        inner.append(jnp.sum(square[:, column : column + width], axis=1, keepdims=True))
        entries.append(jnp.sum(inner[-1], axis=0, keepdims=True))
        master = master_of(masters, which, layer)
        weights.append(one(master * master))
        row_sums.append(one(old_row(row_refs, which, layer)))
    packet_ref[...] = jnp.zeros_like(packet_ref)
    inner.append(jnp.zeros((rows, LANES - MATRICES), jnp.float32))
    packet_ref[0:INNER_ROWS, 0:rows] = jnp.concatenate(inner, axis=1).T[0:INNER_ROWS, :]
    top, two, one_at, zero = [ref[...] for ref in gains_at]
    gain = jnp.concatenate(
        [zero[0:1], one_at[0:1], two[0:1], one_at[1:2], two[1:2], top[0:1], top[1:2]], axis=0
    )
    scalars = [loss_ref[...], one(counted_ref[...])] + weights + entries + row_sums
    scalars.append(jnp.zeros((1, LANES - len(scalars)), jnp.float32))
    at = INNER_ROWS
    packet_ref[at : at + 7, :] = gain[:, 0:LANES]
    packet_ref[at + 7 : at + 8, :] = jnp.concatenate(scalars, axis=1)
    packet_ref[at + 8 : at + 15, :] = gain[:, LANES:]
    outer = jnp.sum(square, axis=0, keepdims=True)
    at = INNER_ROWS + COMMON_ROWS
    for row, start in enumerate(range(0, total, LANES)):
        stop = min(start + LANES, total)
        packet_ref[at + row : at + row + 1, 0 : stop - start] = outer[:, start:stop]


def outer_rows(widths):
    _, total = matrix_plan(widths)
    return -(-total // (8 * LANES)) * 8


def run_stats(widths, raw_early, raw_late, masters, rows, gain_parts, loss, counted):
    vmem = pl.BlockSpec(memory_space=pltpu.VMEM)
    operands = [raw_early, raw_late] + masters + rows + gain_parts + [loss, counted]
    packet = (INNER_ROWS + COMMON_ROWS + outer_rows(widths), LANES)
    return pl.pallas_call(
        functools.partial(stats_kernel, widths),
        in_specs=[vmem] * len(operands),
        out_specs=vmem,
        out_shape=jax.ShapeDtypeStruct(packet, jnp.float32),
        name="statistics",
    )(*operands)


def update_kernel(widths, sizes, *refs):
    across_ref, along_ref, raw_early, raw_late = refs[:4]
    masters, inner_refs, outer_refs = refs[4:10], refs[10:16], refs[16:22]
    gains_ref, second_ref = refs[22:24]
    outs = refs[24:]
    outer_count, inner_count = sizes
    plan, total = matrix_plan(widths)
    rows = raw_early.shape[0]
    scalars = along_ref[7:8, :]
    pick = lambda at: scalars[:, at : at + 1]
    gain_sum = jnp.concatenate([along_ref[0:7, :], along_ref[8:15, :]], axis=1)
    gain_square = jnp.sum(jnp.sum(gain_sum * gain_sum, axis=1, keepdims=True), axis=0, keepdims=True)
    square_total = gain_square
    for at in range(MATRICES):
        square_total = square_total + pick(2 + MATRICES + at)
    count_total = pick(1)
    norm_value = jnp.sqrt(square_total) / count_total
    scaling = jnp.minimum(1.0, clip_limit / norm_value) / count_total
    square_scale = scaling * scaling
    outer_total = jnp.concatenate(
        [
            along_ref[COMMON_ROWS + row : COMMON_ROWS + row + 1, 0 : min(LANES, total - row * LANES)]
            for row in range(-(-total // LANES))
        ],
        axis=1,
    )
    inner_new = []
    for at, (which, layer) in enumerate(matrix_list()):
        outer_length = widths[which] * outer_count
        inner_new.append(
            decay_two * old_row(inner_refs, which, layer)
            + (1 - decay_two)
            * (square_scale * across_ref[at : at + 1, 0:rows] / outer_length + tiny_term)
        )
    stacked = jnp.concatenate(inner_new, axis=0)
    stacked = jnp.concatenate([stacked, jnp.ones((LANES - MATRICES, rows), jnp.float32)], axis=0)
    if rows < LANES:
        stacked = jnp.concatenate([stacked, jnp.ones((LANES, LANES - rows), jnp.float32)], axis=1)
    turned = lax.rsqrt(stacked).T
    outs[0][...] = pick(0)
    outs[1][...] = count_total
    outs[2][...] = norm_value
    first_out = {4: 3, 0: 7, 1: 11, 2: 15, 3: 19, 5: 23}
    for at, (which, layer) in enumerate(matrix_list()):
        column, width = plan[(which, layer)]
        outer_length, inner_length = width * outer_count, rows * inner_count
        row_length = inner_length if ROW_IS_INNER[which] else outer_length
        copies = outer_count if ROW_IS_INNER[which] else inner_count
        entries = outer_length * inner_length
        early = raw_early.shape[1]
        if column < early:
            raw = raw_early[:, column : column + width]
        else:
            raw = raw_late[:, column - early : column - early + width]
        outer_new = decay_two * old_row(outer_refs, which, layer) + (1 - decay_two) * (
            square_scale * outer_total[:, column : column + width] / inner_length + tiny_term
        )
        mean_rows = decay_two * (pick(2 + 2 * MATRICES + at) / (copies * row_length)) + (
            1 - decay_two
        ) * (square_scale * pick(2 + MATRICES + at) / entries + tiny_term)
        factor = step_rate * jnp.sqrt(pick(2 + at) / entries) * jnp.sqrt(mean_rows)
        grad = raw * scaling
        updated = master_of(masters, which, layer) - grad * (
            turned[0:rows, at : at + 1] * (factor * lax.rsqrt(outer_new))
        )
        first = first_out[which]
        row_new, column_new = (
            (inner_new[at], outer_new) if ROW_IS_INNER[which] else (outer_new, inner_new[at])
        )
        if which < 4:
            if which == 1:
                updated, grad = updated.T, grad.T
            outs[first][layer] = updated
            outs[first + 1][layer] = grad
            outs[first + 2][layer : layer + 1, :] = row_new
            outs[first + 3][layer : layer + 1, :] = column_new
        else:
            outs[first][...] = updated
            outs[first + 1][...] = grad
            outs[first + 2][...] = row_new
            outs[first + 3][...] = column_new
    gain_grad = gain_sum * scaling
    second_new = decay_two * second_ref[...] + (1 - decay_two) * (gain_grad * gain_grad + tiny_term)
    gains = gains_ref[...]
    spread = jnp.sqrt(jnp.mean(gains * gains, axis=-1, keepdims=True))
    outs[27][...] = gains - step_rate * spread * gain_grad * lax.rsqrt(second_new)
    outs[28][...] = gain_grad
    outs[29][...] = second_new


def run_update(widths, sizes, across, along, raw_early, raw_late, masters, inner, outer, gains, second):
    vmem = pl.BlockSpec(memory_space=pltpu.VMEM)
    operands = [across, along, raw_early, raw_late] + masters + inner + outer + [gains, second]
    shapes = [(1, 1)] * 3
    for which in [4, 0, 1, 2, 3, 5]:
        shapes = shapes + [masters[which].shape] * 2
        pair = [inner[which].shape, outer[which].shape]
        shapes = shapes + (pair if ROW_IS_INNER[which] else pair[::-1])
    shapes = shapes + [gains.shape] * 3
    return pl.pallas_call(
        functools.partial(update_kernel, widths, sizes),
        in_specs=[vmem] * len(operands),
        out_specs=[vmem] * len(shapes),
        out_shape=[jax.ShapeDtypeStruct(item, jnp.float32) for item in shapes],
        name="update",
    )(*operands)


def swap(value, axis, bit):
    pairs = [(place, place ^ bit) for place in range(lax.axis_size(axis))]
    return lax.ppermute(value, axis, pairs)


def tie(*values):
    return lax.optimization_barrier(values)


class Gather:
    def __init__(self, piece, steps):
        self.held, self.steps, self.at = piece[None], steps, 0

    def send(self):
        axis, bit = self.steps[self.at]
        self.other = swap(self.held, axis, 1 << bit)

    def join(self):
        axis, bit = self.steps[self.at]
        upper = (lax.axis_index(axis) >> bit) & 1 == 1
        self.held = jnp.where(
            upper,
            jnp.concatenate([self.other, self.held]),
            jnp.concatenate([self.held, self.other]),
        )
        self.at += 1

    def step(self, after=None):
        if after is not None:
            self.held, _ = tie(self.held, after.other)
        self.send()
        self.join()


class Scatter:
    def __init__(self, sent, kept, steps):
        self.sent, self.kept, self.steps, self.at = sent, kept, steps, 0

    def send(self):
        axis, bit = self.steps[self.at]
        self.other = swap(self.sent, axis, 1 << bit)

    def join(self):
        self.at += 1
        summed = self.kept + self.other.astype(jnp.float32)
        if self.at == len(self.steps):
            self.kept = summed
            return
        axis, bit = self.steps[self.at]
        side = (lax.axis_index(axis) >> bit) & 1
        half = summed.shape[0] // 2
        parts = summed.reshape((2, half) + summed.shape[1:])
        self.sent = jnp.where(side == 1, parts[0], parts[1]).astype(jnp.bfloat16)
        self.kept = jnp.where(side == 1, parts[1], parts[0])


def merged(parts):
    whole = Scatter(
        jnp.concatenate([part.sent for part in parts], axis=2),
        jnp.concatenate([part.kept for part in parts], axis=2),
        parts[0].steps,
    )
    whole.at = parts[0].at
    return whole


def shards(
    latents,
    targets,
    horizon,
    memory_valid,
    embed,
    qkv_weight,
    out_weight,
    up_weight,
    down_weight,
    head_weight,
    gains,
    embed_rows,
    embed_cols,
    qkv_rows,
    qkv_cols,
    out_rows,
    out_cols,
    up_rows,
    up_cols,
    down_rows,
    down_cols,
    head_rows,
    head_cols,
    gain_second,
):
    samples = latents.shape[0]
    sizes = (lax.axis_size("dp"), lax.axis_size("fsdp"))
    bits = (sizes[0].bit_length() - 1, sizes[1].bit_length() - 1)
    gather_steps = [("dp", bit) for bit in reversed(range(bits[0]))]
    gather_steps = gather_steps + [("fsdp", bit) for bit in reversed(range(bits[1]))]
    scatter_steps = gather_steps[::-1]
    core = (lax.axis_index("fsdp") & 1).astype(jnp.int32).reshape(1)

    low = lambda item: item.astype(jnp.bfloat16)
    out_turned = jnp.swapaxes(out_weight, 1, 2)
    down_turned = jnp.swapaxes(down_weight, 1, 2)
    masters = [qkv_weight, out_turned, up_weight, down_turned, embed.T, head_weight]
    widths = [qkv_weight.shape[2], out_weight.shape[2], up_weight.shape[2], down_weight.shape[1]]
    widths = widths + [embed.shape[0], head_weight.shape[1]]
    att_parts = [[qkv_weight[at], out_weight[at]] for at in range(LAYERS)]
    ffn_parts = [[up_weight[at], down_turned[at]] for at in range(LAYERS)]
    pieces = [
        att_parts[0] + [embed.T],
        ffn_parts[0] + att_parts[1],
        ffn_parts[1] + att_parts[2] + ffn_parts[2] + [head_weight],
    ]
    att_widths, ffn_widths = widths[0:2], widths[2:4]
    first, second, third = [
        Gather(low(jnp.concatenate(piece, axis=1)), gather_steps) for piece in pieces
    ]
    chunk_widths = [
        att_widths + widths[4:5],
        ffn_widths + att_widths,
        ffn_widths + att_widths + ffn_widths + widths[5:6],
    ]

    latent_rows = low(latents).reshape(samples * CTX, CATS)
    target_rows = targets.transpose(2, 0, 1).reshape(CATS, samples * SEG)
    counted = jnp.arange(SEG, dtype=jnp.int32)[None, :] < horizon[:, None]
    counted = counted.astype(jnp.float32).reshape(1, samples * SEG)
    shared = (gains, memory_valid, core)

    count = len(gather_steps)
    for at in range(count - 1):
        first.step()
        if at < count - 2:
            second.step(first)
        if at < count - 3:
            third.step(second)
    first.send()
    second.step(first)
    third.step(second)
    first.held, first.other, second.held, third.held = tie(
        first.held, first.other, second.held, third.held
    )
    second.send()
    third.send()
    kept = [run_forward(0, chunk_widths[0], bits, latent_rows, first.held, first.other, *shared)]
    middle, second.other, third.other = tie(kept[0][1], second.other, third.other)
    third.join()
    second.held, third.held = tie(second.held, third.held)
    third.send()
    kept.append(run_forward(1, chunk_widths[1], bits, middle, second.held, second.other, *shared))
    middle, third.other = tie(kept[1][1], third.other)
    kept.append(run_forward(2, chunk_widths[2], bits, middle, third.held, third.other, *shared))

    dmiddle, sent, held, gain_top, loss = run_top(
        ffn_widths + widths[5:6],
        bits,
        sum(ffn_widths + att_widths),
        kept[2][1],
        third.held,
        third.other,
        target_rows,
        counted,
        gains,
        core,
    )
    top = Scatter(sent, held, scatter_steps)
    top.send()
    like = first.held
    dmiddle, sent, held, gain_two = run_backward(
        2, chunk_widths[1], bits, like, kept[2], dmiddle, *shared, (kept[1][1], kept[2][6])
    )
    dmiddle, top.other = tie(dmiddle, top.other)
    top.join()
    two = Scatter(sent, held, scatter_steps)
    dmiddle, top.sent = tie(dmiddle, top.sent)
    top.send()
    two.send()
    dmiddle, sent, held, gain_one = run_backward(
        1, chunk_widths[1], bits, like, kept[1], dmiddle, *shared, (kept[0][1], kept[1][6])
    )
    dmiddle, top.other, two.other = tie(dmiddle, top.other, two.other)
    top.join()
    two.join()
    one = Scatter(sent, held, scatter_steps)
    dmiddle, top.sent, two.sent = tie(dmiddle, top.sent, two.sent)
    top.send()
    two.send()
    one.send()
    sent, held, gain_zero = run_backward(
        0, chunk_widths[0], bits, like, kept[0], dmiddle, *shared, latent_rows
    )
    sent, top.other, two.other, one.other = tie(sent, top.other, two.other, one.other)
    zero = Scatter(sent, held, scatter_steps)
    zero.send()
    two.join()
    two.send()
    one.join()
    one.send()
    top.join()
    zero.join()
    zero.send()
    one.join()
    one.send()
    two.join()
    zero.join()
    zero.send()
    one.join()
    early = merged([top, two, one])
    while early.at < count:
        early.send()
        early.join()
        zero.join()
        if zero.at < count:
            zero.send()
    while zero.at < count:
        zero.join()
        if zero.at < count:
            zero.send()
    raw_early, raw_late = early.kept[0], zero.kept[0]

    flat = lambda item: item if item.ndim == 2 else item.reshape(1, -1)
    inner = [flat(item) for item in (qkv_rows, out_rows, up_rows, down_cols, embed_cols, head_rows)]
    outer = [flat(item) for item in (qkv_cols, out_cols, up_cols, down_rows, embed_rows, head_cols)]
    row_stats = [inner[at] if ROW_IS_INNER[at] else outer[at] for at in range(6)]
    gain_parts = [gain_top, gain_two, gain_one, gain_zero]
    packet = run_stats(widths, raw_early, raw_late, masters, row_stats, gain_parts, loss, counted)
    edge = INNER_ROWS + COMMON_ROWS
    across = packet[:edge]
    for axis, bit in scatter_steps[bits[1] :]:
        across = across + swap(across, axis, 1 << bit)
    along = jnp.concatenate([across[INNER_ROWS:], packet[edge:]])
    for axis, bit in scatter_steps[: bits[1]][::-1]:
        along = along + swap(along, axis, 1 << bit)
    results = run_update(
        widths, sizes, across, along, raw_early, raw_late, masters, inner, outer, gains, gain_second
    )
    results = list(results)
    for at in range(3):
        results[at] = results[at].reshape(())
    for at in (3, 4, 11, 12, 19, 20):
        results[at] = jnp.swapaxes(results[at], -1, -2)
    for at in (5, 6, 25, 26):
        results[at] = results[at].reshape(-1)
    return tuple(results)


def solution(mesh):
    return jax.shard_map(
        shards,
        mesh=mesh,
        in_specs=(
            P(("dp", "fsdp"), None, None),
            P(("dp", "fsdp"), None, None),
            P(("dp", "fsdp")),
            P(("dp", "fsdp")),
            P("dp", "fsdp"),
            P(None, "fsdp", "dp"),
            P(None, "fsdp", "dp"),
            P(None, "fsdp", "dp"),
            P(None, "dp", "fsdp"),
            P("fsdp", "dp"),
            P(),
            P("dp"),
            P("fsdp"),
            P(None, "fsdp"),
            P(None, "dp"),
            P(None, "fsdp"),
            P(None, "dp"),
            P(None, "fsdp"),
            P(None, "dp"),
            P(None, "dp"),
            P(None, "fsdp"),
            P("fsdp"),
            P("dp"),
            P(),
        ),
        out_specs=(
            P(),
            P(),
            P(),
            P("dp", "fsdp"),
            P("dp", "fsdp"),
            P("dp"),
            P("fsdp"),
            P(None, "fsdp", "dp"),
            P(None, "fsdp", "dp"),
            P(None, "fsdp"),
            P(None, "dp"),
            P(None, "fsdp", "dp"),
            P(None, "fsdp", "dp"),
            P(None, "fsdp"),
            P(None, "dp"),
            P(None, "fsdp", "dp"),
            P(None, "fsdp", "dp"),
            P(None, "fsdp"),
            P(None, "dp"),
            P(None, "dp", "fsdp"),
            P(None, "dp", "fsdp"),
            P(None, "dp"),
            P(None, "fsdp"),
            P("fsdp", "dp"),
            P("fsdp", "dp"),
            P("fsdp"),
            P("dp"),
            P(),
            P(),
            P(),
        ),
        check_vma=False,
    )
```

time: 644 us -> 266 us (0.41)
  local copies, waits for them, and re-layouts: 272 us -> 7.32 us
  matrix products: 138 us -> 0 us
  Pallas kernels: 0 us -> 133 us
  other arithmetic: 95.4 us -> 9.49 us
  starting transfers between devices: 59.3 us -> 38.1 us
  waiting for transfers between devices: 51.5 us -> 71.3 us
  between operations: 16.7 us -> 1.46 us
    dot_general x83 -> x0, matrix products: 138 us -> none  [the longest x13 37.5 us: matmul_nt(): lax.dot_general(left, right, (((1,), (1,)), ((), ())), preferred_element_...]
    pallas_call x0 -> x9, Pallas kernels: none -> 133 us  [the longest x3 70.5 us: run_backward(): pl.pallas_call(functools.partial(backward_kernel, layer, widths, bits), g...]
    another operation x46 -> x0, local copies, waits for them, and re-layouts: 47.7 us -> none
    convert_element_type x12 -> x2, local copies, waits for them, and re-layouts: 37.8 us -> 1.6 us  [the longest x1 0.93 us: shards(): low = lambda item: item.astype(jnp.bfloat16)]
    transpose x31 -> x1, local copies, waits for them, and re-layouts: 33.5 us -> 0.16 us  [shards(): target_rows = targets.transpose(2, 0, 1).reshape(CATS, samples * SEG)]
    reduce_sum x36 -> x0, other arithmetic: 31.1 us -> none  [the longest x6 8.85 us: shards(): jnp.sum(master * master, axis=(-2, -1))]
    reshape x32 -> x1, local copies, waits for them, and re-layouts: 29.4 us -> 0.78 us  [shards(): target_rows = targets.transpose(2, 0, 1).reshape(CATS, samples * SEG)]
    while x105 -> x0, local copies, waits for them, and re-layouts: 26.1 us -> none
  transfers between devices with their start and end apart: 50 -> 36, of which waited for: 20 -> 23; matrix products, arithmetic and copies ran while one was open for 16% -> 3% of each run, Pallas kernels for 0% -> 38%
where the time goes in v3:
time: 266 us; the launch traced here: 261 us
  Pallas kernels  133 us (50%)
  waiting for transfers between devices  71.3 us (27%)
  starting transfers between devices  38.1 us (14%)
  other arithmetic  9.49 us (4%)
  local copies, waits for them, and re-layouts  7.32 us (3%)
    ppermute x36, waiting for transfers between devices, swap(): return lax.ppermute(value, axis, pairs)  71.3 us
    pallas_call x3, Pallas kernels, run_backward(): pl.pallas_call(functools.partial(backward_kernel, layer, widths, bits), g...  70.5 us
    pallas_call x3, Pallas kernels, run_forward(): pl.pallas_call(functools.partial(forward_kernel, layer, widths, bits), gr...  45 us
    ppermute x36, starting transfers between devices, swap(): return lax.ppermute(value, axis, pairs)  38.1 us
    pallas_call x1, Pallas kernels, run_top(): pl.pallas_call(functools.partial(top_kernel, widths, bits, start), in_spe...  11.1 us
  transfers between devices with their start and end apart: 36, of which 23 were waited for; matrix products, arithmetic and copies ran while one was open for 3% of the time, Pallas kernels for 38%

profile of v3, /device:TPU:0, one launch (start us, length us, event | category | flops | bytes accessed | tf_op | source)
XLA Modules:
  0.0 261.0 jit_solution(4466014685008466065)
XLA Ops:
  3.3 4.1 %collective-permute-start = (bf16[1,64,256]{2,1,0:T(8,128)(2,1)S(1)}, bf16[1,64,256]{2,1,0:T(8,128)(2,1)S(1)}, u32[]{:S(2)}, u32[]{:S(2)}) collective-permute-start(bf16[1,64,256]{2,1,0:T(8,128)(2,1)S(1)} %pad_maximum_fusion.2), channel_id=1, source_target_pairs={{0,16},{4,20},{8,24},{12,28},{16,0},{20,4},{24,8},{28,12},{1,17},{... | collective-permute-start | bytes 98312 | tf_op jit(solution)/shard_map/ppermute | solution.py:836
  7.4 2.2 collective-permute-done
  9.8 1.6 collective-permute-start.1
  14.1 1.8 collective-permute-start.2
  15.9 3.3 %collective-permute-done.2 = bf16[4,64,256]{2,1,0:T(8,128)(2,1)S(1)} collective-permute-done((bf16[4,64,256]{2,1,0:T(8,128)(2,1)S(1)}, bf16[4,64,256]{2,1,0:T(8,128)(2,1)S(1)}, u32[]{:S(2)}, u32[]{:S(2)}) %collective-permute-start.2) | collective-permute-done | bytes 131104 | tf_op jit(solution)/shard_map/ppermute | solution.py:836
  19.2 1.8 collective-permute-start.3
  21.1 2.4 collective-permute-start.5
  23.5 2.6 collective-permute-done.5
  26.1 1.9 collective-permute-start.6
  28.2 2.6 collective-permute-done.6
  30.8 1.6 collective-permute-start.7
  32.4 2.8 %collective-permute-start.9 = (bf16[1,64,768]{2,1,0:T(8,128)(2,1)S(1)}, bf16[1,64,768]{2,1,0:T(8,128)(2,1)S(1)}, u32[]{:S(2)}, u32[]{:S(2)}) collective-permute-start(bf16[1,64,768]{2,1,0:T(8,128)(2,1)S(1)} %concatenate.138), channel_id=1, source_target_pairs={{0,16},{4,20},{8,24},{12,28},{16,0},{20,4},{24,8},{28,12},{1,17},{... | collective-permute-start | bytes 294920 | tf_op jit(solution)/shard_map/ppermute | solution.py:836
  35.2 1.3 collective-permute-done.7
  37.0 1.3 collective-permute-done.9
  38.4 1.8 collective-permute-start.10
  40.2 4.0 %collective-permute-done.10 = bf16[2,64,768]{2,1,0:T(8,128)(2,1)S(1)} collective-permute-done((bf16[2,64,768]{2,1,0:T(8,128)(2,1)S(1)}, bf16[2,64,768]{2,1,0:T(8,128)(2,1)S(1)}, u32[]{:S(2)}, u32[]{:S(2)}) %collective-permute-start.10) | collective-permute-done | bytes 196640 | tf_op jit(solution)/shard_map/ppermute | solution.py:836
  44.5 1.5 collective-permute-start.11
  46.2 6.1 %collective-permute-done.11 = bf16[4,64,768]{2,1,0:T(8,128)(2,1)S(1)} collective-permute-done((bf16[4,64,768]{2,1,0:T(8,128)(2,1)S(1)}, bf16[4,64,768]{2,1,0:T(8,128)(2,1)S(1)}, u32[]{:S(2)}, u32[]{:S(2)}) %collective-permute-start.11) | collective-permute-done | bytes 393248 | tf_op jit(solution)/shard_map/ppermute | solution.py:836
  54.0 13.9 %forward_part.3 = (f32[1536,256]{1,0:T(8,128)}, f32[1536,256]{1,0:T(8,128)}, bf16[1536,768]{1,0:T(8,128)(2,1)}, bf16[1536,256]{1,0:T(8,128)(2,1)}, f32[16,1,768]{2,1,0:T(1,128)}, /*index=5*/bf16[256,1024]{1,0:T(8,128)(2,1)}) custom-call(bf16[1536,32]{1,0:T(8,128)(2,1)} %bitcast.37, bf16[16,64,256]{2,1,0:T(8,128)(2,1)} %copy-done.6, ...), custom_call_target="tpu_custom_call" | custom-call | flops 2415919104 | bytes 9437184 | tf_op jit(solution)/shard_map/forward_part/pallas_call | solution.py:360
  67.9 4.5 %collective-permute-done.13 = bf16[8,64,768]{2,1,0:T(8,128)(2,1)S(1)} collective-permute-done((bf16[8,64,768]{2,1,0:T(8,128)(2,1)S(1)}, bf16[8,64,768]{2,1,0:T(8,128)(2,1)S(1)}, u32[]{:S(2)}, u32[]{:S(2)}) %collective-permute-start.13) | collective-permute-done | bytes 786464 | tf_op jit(solution)/shard_map/ppermute | solution.py:836
  74.8 15.1 %forward_part.4 = (f32[1536,256]{1,0:T(8,128)}, f32[1536,256]{1,0:T(8,128)}, bf16[1536,768]{1,0:T(8,128)(2,1)}, bf16[1536,256]{1,0:T(8,128)(2,1)}, f32[16,1,768]...) custom-call(f32[1536,256]{1,0:T(8,128)} %get-tuple-element.140.source_ref.refs_9_, ...), custom_call_target="tpu_custom_call" | custom-call | flops 2415919104 | bytes 9437184 | tf_op jit(solution)/shard_map/forward_part/pallas_call | solution.py:360
  89.9 16.0 %forward_part.5 = (f32[1536,256]{1,0:T(8,128)}, f32[768,256]{1,0:T(8,128)}, bf16[1536,768]{1,0:T(8,128)(2,1)}, bf16[768,256]{1,0:T(8,128)(2,1)}, f32[16,1,384]{2...) custom-call(f32[1536,256]{1,0:T(8,128)} %get-tuple-element.146.source_ref.refs_9_, ...), custom_call_target="tpu_custom_call" | custom-call | flops 2415919104 | bytes 9437184 | tf_op jit(solution)/shard_map/forward_part/pallas_call | solution.py:360
  105.9 11.1 %loss_part.1 = (f32[768,256]{1,0:T(8,128)}, bf16[16,64,384]{2,1,0:T(8,128)(2,1)}, f32[16,64,384]{2,1,0:T(8,128)}, f32[2,256]{1,0:T(2,128)}, f32[1,1]{1,0:T(1,128)}) custom-call(f32[768,256]{1,0:T(8,128)} %get-tuple-element.148.middle_ref, bf16[16,64,768]{2,1,0:T(8,128)(2,1)} %copy-done.2, bf16[16,64,768]{2,1,0:T(8,128)(2,1)} %collective-permute-done.14.other_ref, ...), custom_call_target="tpu_custom_call" | custom-call | flops 3623878656 | bytes 9437184 | tf_op jit(solution)/shard_map/loss_part/pallas_call | solution.py:482
  117.2 23.3 %backward_part.3 = (f32[1536,256]{1,0:T(8,128)}, bf16[16,64,384]{2,1,0:T(8,128)(2,1)}, f32[16,64,384]{2,1,0:T(8,128)}, f32[2,256]{1,0:T(2,128)}) custom-call(f32[1536,256]{1,0:T(8,128)} %get-tuple-element.150.refs_0_, bf16[1536,768]{1,0:T(8,128)(2,1)} %get-tuple-element.151.refs_1_, bf16[768,256]{1,0:T(8,128)(2,1)} %get-tuple-element.152.refs_2_, ...), custom_call_target="tpu_custom_call" | custom-call | flops 7247757312 | bytes 14155776 | tf_op jit(solution)/shard_map/backward_part/pallas_call | solution.py:623
  141.8 31.8 %backward_part.4 = (f32[1536,256]{1,0:T(8,128)}, bf16[16,64,384]{2,1,0:T(8,128)(2,1)}, f32[16,64,384]{2,1,0:T(8,128)}, f32[2,256]{1,0:T(2,128)}) custom-call(f32[1536,256]{1,0:T(8,128)} %get-tuple-element.160.refs_0_, bf16[1536,768]{1,0:T(8,128)(2,1)} %get-tuple-element.161.refs_1_, bf16[1536,256]{1,0:T(8,128)(2,1)} %get-tuple-element.162.refs_2_, ...), custom_call_target="tpu_custom_call" | custom-call | flops 7247757312 | bytes 14155776 | tf_op jit(solution)/shard_map/backward_part/pallas_call | solution.py:623
  173.8 1.2 copy-done.1
  175.4 1.6 collective-permute-start.18
  176.9 1.5 collective-permute-start.19
  178.4 15.4 %backward_part.5 = (bf16[16,64,256]{2,1,0:T(8,128)(2,1)}, f32[16,64,256]{2,1,0:T(8,128)}, f32[2,256]{1,0:T(2,128)}) custom-call(f32[1536,256]{1,0:T(8,128)} %get-tuple-element.172.refs_0_, bf16[1536,768]{1,0:T(8,128)(2,1)} %get-tuple-element.173.refs_1_, bf16[1536,256]{1,0:T(8,128)(2,1)} %get-tuple-element.174.refs_2_, ...), custom_call_target="tpu_custom_call" | custom-call | flops 4831838208 | bytes 12582912 | tf_op jit(solution)/shard_map/backward_part/pallas_call | solution.py:623
  196.4 3.9 %collective-permute-done.21 = bf16[4,64,384]{2,1,0:T(8,128)(2,1)S(1)} collective-permute-done((bf16[4,64,384]{2,1,0:T(8,128)(2,1)S(1)}, bf16[4,64,384]{2,1,0:T(8,128)(2,1)S(1)}, u32[]{:S(2)}, u32[]{:S(2)}) %collective-permute-start.21) | collective-permute-done | bytes 196640 | tf_op jit(solution)/shard_map/ppermute | solution.py:836
  200.4 5.6 %collective-permute-done.22 = bf16[8,64,384]{2,1,0:T(8,128)(2,1)S(1)} collective-permute-done((bf16[8,64,384]{2,1,0:T(8,128)(2,1)S(1)}, bf16[8,64,384]{2,1,0:T(8,128)(2,1)S(1)}, u32[]{:S(2)}, u32[]{:S(2)}) %collective-permute-start.22) | collective-permute-done | bytes 393248 | tf_op jit(solution)/shard_map/ppermute | solution.py:836
  207.7 4.4 %collective-permute-done.23 = bf16[4,64,384]{2,1,0:T(8,128)(2,1)S(1)} collective-permute-done((bf16[4,64,384]{2,1,0:T(8,128)(2,1)S(1)}, bf16[4,64,384]{2,1,0:T(8,128)(2,1)S(1)}, u32[]{:S(2)}, u32[]{:S(2)}) %collective-permute-start.23) | collective-permute-done | bytes 196640 | tf_op jit(solution)/shard_map/ppermute | solution.py:836
  212.1 1.9 collective-permute-start.24
  214.2 1.0 collective-permute-start.28
  215.2 4.0 %collective-permute-done.28 = bf16[4,64,256]{2,1,0:T(8,128)(2,1)S(1)} collective-permute-done((bf16[4,64,256]{2,1,0:T(8,128)(2,1)S(1)}, bf16[4,64,256]{2,1,0:T(8,128)(2,1)S(1)}, u32[]{:S(2)}, u32[]{:S(2)}) %collective-permute-start.28) | collective-permute-done | bytes 131104 | tf_op jit(solution)/shard_map/ppermute | solution.py:836
  219.3 1.4 collective-permute-start.29
  220.7 3.2 %collective-permute-done.29 = bf16[2,64,256]{2,1,0:T(8,128)(2,1)S(1)} collective-permute-done((bf16[2,64,256]{2,1,0:T(8,128)(2,1)S(1)}, bf16[2,64,256]{2,1,0:T(8,128)(2,1)S(1)}, u32[]{:S(2)}, u32[]{:S(2)}) %collective-permute-start.29) | collective-permute-done | bytes 65568 | tf_op jit(solution)/shard_map/ppermute | solution.py:836
  224.0 2.3 collective-permute-start.30
  227.1 2.5 collective-permute-done.30
  230.2 3.9 %collective-permute-done.25 = bf16[1,64,1152]{2,1,0:T(8,128)(2,1)S(1)} collective-permute-done((bf16[1,64,1152]{2,1,0:T(8,128)(2,1)S(1)}, bf16[1,64,1152]{2,1,0:T(8,128)(2,1)S(1)}, u32[]{:S(2)}, u32[]{:S(2)}) %collective-permute-start.25) | collective-permute-done | bytes 147488 | tf_op jit(solution)/shard_map/ppermute | solution.py:836
  234.8 3.2 %statistics.1 = f32[48,128]{1,0:T(8,128)} custom-call(f32[64,1152]{1,0:T(8,128)} %add_bitcast_fusion.refs_0_.refs_2_, f32[64,256]{1,0:T(8,128)} %add_bitcast_fusion.1.refs_1_.refs_3_, f32[3,64,96]{2,1,0:T(8,128)} %refs_4_.3, f32[3,32,64]{2,1,0:T(8,128)} %bitcast.35, f32[3,64,128]{2,1,0:T(8,128)} %refs_6_.7, f32[3,64,128]{2,1,0:T(8,128)} %bitcast.33, ...), custom_call_target="tpu_custom_call" | custom-call | tf_op jit(solution)/shard_map/statistics/pallas_call | solution.py:717
  238.8 1.1 collective-permute-start.31
  239.9 2.7 %collective-permute-done.31 = f32[32,128]{1,0:T(8,128)S(1)} collective-permute-done((f32[32,128]{1,0:T(8,128)S(1)}, f32[32,128]{1,0:T(8,128)S(1)}, u32[]{:S(2)}, u32[]{:S(2)}) %collective-permute-start.31) | collective-permute-done | bytes 16416 | tf_op jit(solution)/shard_map/ppermute | solution.py:836
  243.4 3.6 %collective-permute-done.32 = f32[32,128]{1,0:T(8,128)S(1)} collective-permute-done((f32[32,128]{1,0:T(8,128)S(1)}, f32[32,128]{1,0:T(8,128)S(1)}, u32[]{:S(2)}, u32[]{:S(2)}) %collective-permute-start.32) | collective-permute-done | bytes 16416 | tf_op jit(solution)/shard_map/ppermute | solution.py:836
  247.7 3.9 %collective-permute-done.33 = f32[32,128]{1,0:T(8,128)S(1)} collective-permute-done((f32[32,128]{1,0:T(8,128)S(1)}, f32[32,128]{1,0:T(8,128)S(1)}, u32[]{:S(2)}, u32[]{:S(2)}) %collective-permute-start.33) | collective-permute-done | bytes 16416 | tf_op jit(solution)/shard_map/ppermute | solution.py:836
  252.1 3.3 %collective-permute-done.34 = f32[32,128]{1,0:T(8,128)S(1)} collective-permute-done((f32[32,128]{1,0:T(8,128)S(1)}, f32[32,128]{1,0:T(8,128)S(1)}, u32[]{:S(2)}, u32[]{:S(2)}) %collective-permute-start.34) | collective-permute-done | bytes 16416 | tf_op jit(solution)/shard_map/ppermute | solution.py:836
  255.5 1.2 collective-permute-done.35
  257.3 3.5 %update.1 = (f32[1,1]{1,0:T(1,128)}, f32[1,1]{1,0:T(1,128)}, f32[1,1]{1,0:T(1,128)}, f32[64,128]{1,0:T(8,128)}, f32[64,128]{1,0:T(8,128)}, /*index=5*/f32[1,128]...) custom-call(f32[32,128]{1,0:T(8,128)} %copy-done.10, ...), custom_call_target="tpu_custom_call" | custom-call | tf_op jit(solution)/shard_map/update/pallas_call | solution.py:825
  (134 shorter events, 23.0 us)
Async XLA Ops:
  3.3 6.3 %collective-permute-start = (bf16[1,64,256]{2,1,0:T(8,128)(2,1)S(1)}, bf16[1,64,256]{2,1,0:T(8,128)(2,1)S(1)}, u32[]{:S(2)}, u32[]{:S(2)}) collective-permute-start(bf16[1,64,256]{2,1,0:T(8,128)(2,1)S(1)} %pad_maximum_fusion.2), channel_id=1, source_target_pairs={{0,16},{4,20},{8,24},{12,28},{16,0},{20,4},{24,8},{28,12},{1,17},{... | collective-permute-start | bytes 98312 | tf_op jit(solution)/shard_map/ppermute | solution.py:836
  7.4 24.9 %copy-start.7 = (f32[64,128]{1,0:T(8,128)S(1)}, f32[64,128]{1,0:T(8,128)}, u32[]{:S(2)}) copy-start(f32[64,128]{1,0:T(8,128)} %refs_9_.3) | copy-start | bytes 98308
  9.8 4.3 %collective-permute-start.1 = (bf16[2,64,256]{2,1,0:T(8,128)(2,1)S(1)}, bf16[2,64,256]{2,1,0:T(8,128)(2,1)S(1)}, u32[]{:S(2)}, u32[]{:S(2)}) collective-permute-start(bf16[2,64,256]{2,1,0:T(8,128)(2,1)S(1)} %maximum_select_fusion.11), channel_id=1, source_target_pairs={{0,8},{4,12},{8,0},{12,4},{16,24},{20,28},{24,16},{28,20},{1,9},{5... | collective-permute-start | bytes 196616 | tf_op jit(solution)/shard_map/ppermute | solution.py:836
  14.1 5.0 %collective-permute-start.2 = (bf16[4,64,256]{2,1,0:T(8,128)(2,1)S(1)}, bf16[4,64,256]{2,1,0:T(8,128)(2,1)S(1)}, u32[]{:S(2)}, u32[]{:S(2)}) collective-permute-start(bf16[4,64,256]{2,1,0:T(8,128)(2,1)S(1)} %maximum_select_fusion.9), channel_id=1, source_target_pairs={{0,4},{4,0},{8,12},{12,8},{16,20},{20,16},{24,28},{28,24},{1,5},{5... | collective-permute-start | bytes 393224 | tf_op jit(solution)/shard_map/ppermute | solution.py:836
  19.2 8.8 %collective-permute-start.3 = (bf16[8,64,256]{2,1,0:T(8,128)(2,1)S(1)}, bf16[8,64,256]{2,1,0:T(8,128)(2,1)S(1)}, u32[]{:S(2)}, u32[]{:S(2)}) collective-permute-start(bf16[8,64,256]{2,1,0:T(8,128)(2,1)S(1)} %maximum_select_fusion.6), channel_id=1, source_target_pairs={{0,2},{1,3},{2,0},{3,1},{4,6},{5,7},{6,4},{7,5},{8,10},{9,11},{10,... | collective-permute-start | bytes 786440 | tf_op jit(solution)/shard_map/ppermute | solution.py:836
  21.1 5.0 %collective-permute-start.5 = (bf16[1,64,384]{2,1,0:T(8,128)(2,1)S(1)}, bf16[1,64,384]{2,1,0:T(8,128)(2,1)S(1)}, u32[]{:S(2)}, u32[]{:S(2)}) collective-permute-start(bf16[1,64,384]{2,1,0:T(8,128)(2,1)S(1)} %pad_maximum_fusion.1), channel_id=1, source_target_pairs={{0,16},{4,20},{8,24},{12,28},{16,0},{20,4},{24,8},{28,12},{1,17},{... | collective-permute-start | bytes 147464 | tf_op jit(solution)/shard_map/ppermute | solution.py:836
  26.1 4.7 %collective-permute-start.6 = (bf16[2,64,384]{2,1,0:T(8,128)(2,1)S(1)}, bf16[2,64,384]{2,1,0:T(8,128)(2,1)S(1)}, u32[]{:S(2)}, u32[]{:S(2)}) collective-permute-start(bf16[2,64,384]{2,1,0:T(8,128)(2,1)S(1)} %maximum_select_fusion.10), channel_id=1, source_target_pairs={{0,8},{4,12},{8,0},{12,4},{16,24},{20,28},{24,16},{28,20},{1,9},{5... | collective-permute-start | bytes 294920 | tf_op jit(solution)/shard_map/ppermute | solution.py:836
  28.1 18.0 %copy-start.6 = (bf16[16,64,256]{2,1,0:T(8,128)(2,1)}, bf16[16,64,256]{2,1,0:T(8,128)(2,1)S(1)}, u32[]{:S(2)}) copy-start(bf16[16,64,256]{2,1,0:T(8,128)(2,1)S(1)} %maximum_select_fusion.3.own_ref) | copy-start | bytes 1572868
  28.1 8.5 %collective-permute-start.4 = (bf16[16,64,256]{2,1,0:T(8,128)(2,1)S(1)}, bf16[16,64,256]{2,1,0:T(8,128)(2,1)S(1)}, u32[]{:S(2)}, u32[]{:S(2)}) collective-permute-start(bf16[16,64,256]{2,1,0:T(8,128)(2,1)S(1)} %maximum_select_fusion.3.own_ref), channel_id=1, source_target_pairs={{0,1},{1,0},{2,3},{3,2},{4,5},{5,4},{6,7},{7,6},{8,9},{9,8},{10,11... | collective-permute-start | bytes 1572872 | tf_op jit(solution)/shard_map/ppermute | solution.py:836
  30.8 5.7 %collective-permute-start.7 = (bf16[4,64,384]{2,1,0:T(8,128)(2,1)S(1)}, bf16[4,64,384]{2,1,0:T(8,128)(2,1)S(1)}, u32[]{:S(2)}, u32[]{:S(2)}) collective-permute-start(bf16[4,64,384]{2,1,0:T(8,128)(2,1)S(1)} %maximum_select_fusion.7), channel_id=1, source_target_pairs={{0,4},{4,0},{8,12},{12,8},{16,20},{20,16},{24,28},{28,24},{1,5},{5... | collective-permute-start | bytes 589832 | tf_op jit(solution)/shard_map/ppermute | solution.py:836
  32.4 5.9 %collective-permute-start.9 = (bf16[1,64,768]{2,1,0:T(8,128)(2,1)S(1)}, bf16[1,64,768]{2,1,0:T(8,128)(2,1)S(1)}, u32[]{:S(2)}, u32[]{:S(2)}) collective-permute-start(bf16[1,64,768]{2,1,0:T(8,128)(2,1)S(1)} %concatenate.138), channel_id=1, source_target_pairs={{0,16},{4,20},{8,24},{12,28},{16,0},{20,4},{24,8},{28,12},{1,17},{... | collective-permute-start | bytes 294920 | tf_op jit(solution)/shard_map/ppermute | solution.py:836
  36.6 15.8 %copy-start.12 = (bf16[16,64,256]{2,1,0:T(8,128)(2,1)}, bf16[16,64,256]{2,1,0:T(8,128)(2,1)S(1)}, u32[]{:S(2)}) copy-start(bf16[16,64,256]{2,1,0:T(8,128)(2,1)S(1)} %collective-permute-done.4.other_ref) | copy-start | bytes 1572868
  36.6 7.9 %collective-permute-start.8 = (bf16[8,64,384]{2,1,0:T(8,128)(2,1)S(1)}, bf16[8,64,384]{2,1,0:T(8,128)(2,1)S(1)}, u32[]{:S(2)}, u32[]{:S(2)}) collective-permute-start(bf16[8,64,384]{2,1,0:T(8,128)(2,1)S(1)} %maximum_select_fusion.4), channel_id=1, source_target_pairs={{0,2},{1,3},{2,0},{3,1},{4,6},{5,7},{6,4},{7,5},{8,10},{9,11},{10,... | collective-permute-start | bytes 1179656 | tf_op jit(solution)/shard_map/ppermute | solution.py:836
  38.4 5.7 %collective-permute-start.10 = (bf16[2,64,768]{2,1,0:T(8,128)(2,1)S(1)}, bf16[2,64,768]{2,1,0:T(8,128)(2,1)S(1)}, u32[]{:S(2)}, u32[]{:S(2)}) collective-permute-start(bf16[2,64,768]{2,1,0:T(8,128)(2,1)S(1)} %maximum_select_fusion.8), channel_id=1, source_target_pairs={{0,8},{4,12},{8,0},{12,4},{16,24},{20,28},{24,16},{28,20},{1,9},{5... | collective-permute-start | bytes 589832 | tf_op jit(solution)/shard_map/ppermute | solution.py:836
  44.2 8.9 %copy-start.8 = (s32[16,96,32]{1,2,0:T(8,128)S(1)}, s32[16,96,32]{1,2,0:T(8,128)}, u32[]{:S(2)}) copy-start(s32[16,96,32]{1,2,0:T(8,128)} %param.24) | copy-start | bytes 589828
  44.5 7.8 %collective-permute-start.11 = (bf16[4,64,768]{2,1,0:T(8,128)(2,1)S(1)}, bf16[4,64,768]{2,1,0:T(8,128)(2,1)S(1)}, u32[]{:S(2)}, u32[]{:S(2)}) collective-permute-start(bf16[4,64,768]{2,1,0:T(8,128)(2,1)S(1)} %maximum_select_fusion.5), channel_id=1, source_target_pairs={{0,4},{4,0},{8,12},{12,8},{16,20},{20,16},{24,28},{28,24},{1,5},{5... | collective-permute-start | bytes 1179656 | tf_op jit(solution)/shard_map/ppermute | solution.py:836
  46.1 21.8 %copy-start.5 = (bf16[16,64,384]{2,1,0:T(8,128)(2,1)}, bf16[16,64,384]{2,1,0:T(8,128)(2,1)S(1)}, u32[]{:S(2)}) copy-start(bf16[16,64,384]{2,1,0:T(8,128)(2,1)S(1)} %maximum_select_fusion.1.own_ref) | copy-start | bytes 2359300
  52.4 15.5 %collective-permute-start.12 = (bf16[16,64,384]{2,1,0:T(8,128)(2,1)S(1)}, bf16[16,64,384]{2,1,0:T(8,128)(2,1)}, u32[]{:S(2)}, u32[]{:S(2)}) collective-permute-start(bf16[16,64,384]{2,1,0:T(8,128)(2,1)S(1)} %maximum_select_fusion.1.own_ref), channel_id=1, source_target_pairs={{0,1},{1,0},{2,3},{3,2},{4,5},{5,4},{6,7},{7,6},{8,9},{9,8},{10,11... | collective-permute-start | bytes 2359304 | tf_op jit(solution)/shard_map/ppermute | solution.py:836
  52.5 20.0 %collective-permute-start.13 = (bf16[8,64,768]{2,1,0:T(8,128)(2,1)S(1)}, bf16[8,64,768]{2,1,0:T(8,128)(2,1)S(1)}, u32[]{:S(2)}, u32[]{:S(2)}) collective-permute-start(bf16[8,64,768]{2,1,0:T(8,128)(2,1)S(1)} %maximum_select_fusion.2), channel_id=1, source_target_pairs={{0,2},{1,3},{2,0},{3,1},{4,6},{5,7},{6,4},{7,5},{8,10},{9,11},{10,... | collective-permute-start | bytes 2359304 | tf_op jit(solution)/shard_map/ppermute | solution.py:836
  72.4 1.4 copy-start.9
  72.7 17.2 %copy-start.2 = (bf16[16,64,768]{2,1,0:T(8,128)(2,1)}, bf16[16,64,768]{2,1,0:T(8,128)(2,1)S(1)}, u32[]{:S(2)}) copy-start(bf16[16,64,768]{2,1,0:T(8,128)(2,1)S(1)} %maximum_select_fusion.own_ref) | copy-start | bytes 4718596
  72.7 17.2 %collective-permute-start.14 = (bf16[16,64,768]{2,1,0:T(8,128)(2,1)S(1)}, bf16[16,64,768]{2,1,0:T(8,128)(2,1)}, u32[]{:S(2)}, u32[]{:S(2)}) collective-permute-start(bf16[16,64,768]{2,1,0:T(8,128)(2,1)S(1)} %maximum_select_fusion.own_ref), channel_id=1, source_target_pairs={{0,1},{1,0},{2,3},{3,2},{4,5},{5,4},{6,7},{7,6},{8,9},{9,8},{10,11... | collective-permute-start | bytes 4718600 | tf_op jit(solution)/shard_map/ppermute | solution.py:836
  117.0 23.9 %collective-permute-start.15 = (bf16[16,64,384]{2,1,0:T(8,128)(2,1)}, bf16[16,64,384]{2,1,0:T(8,128)(2,1)S(1)}, u32[]{:S(2)}, u32[]{:S(2)}) collective-permute-start(bf16[16,64,384]{2,1,0:T(8,128)(2,1)} %get-tuple-element.158), channel_id=1, source_target_pairs={{0,1},{1,0},{2,3},{3,2},{4,5},{5,4},{6,7},{7,6},{8,9},{9,8},{10,11... | collective-permute-start | bytes 2359304 | tf_op jit(solution)/shard_map/ppermute | solution.py:836
  117.2 23.7 %copy-start.3 = (f32[16,64,384]{2,1,0:T(8,128)S(1)}, f32[16,64,384]{2,1,0:T(8,128)}, u32[]{:S(2)}) copy-start(f32[16,64,384]{2,1,0:T(8,128)} %get-tuple-element.149) | copy-start | bytes 4718596
  140.5 33.2 %collective-permute-start.17 = (bf16[16,64,384]{2,1,0:T(8,128)(2,1)}, bf16[16,64,384]{2,1,0:T(8,128)(2,1)S(1)}, u32[]{:S(2)}, u32[]{:S(2)}) collective-permute-start(bf16[16,64,384]{2,1,0:T(8,128)(2,1)} %get-tuple-element.170), channel_id=1, source_target_pairs={{0,1},{1,0},{2,3},{3,2},{4,5},{5,4},{6,7},{7,6},{8,9},{9,8},{10,11... | collective-permute-start | bytes 2359304 | tf_op jit(solution)/shard_map/ppermute | solution.py:836
  141.2 32.5 %collective-permute-start.16 = (bf16[8,64,384]{2,1,0:T(8,128)(2,1)S(1)}, bf16[8,64,384]{2,1,0:T(8,128)(2,1)S(1)}, u32[]{:S(2)}, u32[]{:S(2)}) collective-permute-start(bf16[8,64,384]{2,1,0:T(8,128)(2,1)S(1)} %select_convert_fusion.2), channel_id=1, source_target_pairs={{0,2},{1,3},{2,0},{3,1},{4,6},{5,7},{6,4},{7,5},{8,10},{9,11},{10,... | collective-permute-start | bytes 1179656 | tf_op jit(solution)/shard_map/ppermute | solution.py:836
  173.6 1.4 copy-start.1
  173.6 20.2 %collective-permute-start.20 = (bf16[16,64,384]{2,1,0:T(8,128)(2,1)}, bf16[16,64,384]{2,1,0:T(8,128)(2,1)S(1)}, u32[]{:S(2)}, u32[]{:S(2)}) collective-permute-start(bf16[16,64,384]{2,1,0:T(8,128)(2,1)} %get-tuple-element.184), channel_id=1, source_target_pairs={{0,1},{1,0},{2,3},{3,2},{4,5},{5,4},{6,7},{7,6},{8,9},{9,8},{10,11... | collective-permute-start | bytes 2359304 | tf_op jit(solution)/shard_map/ppermute | solution.py:836
  175.4 18.4 %collective-permute-start.18 = (bf16[4,64,384]{2,1,0:T(8,128)(2,1)S(1)}, bf16[4,64,384]{2,1,0:T(8,128)(2,1)S(1)}, u32[]{:S(2)}, u32[]{:S(2)}) collective-permute-start(bf16[4,64,384]{2,1,0:T(8,128)(2,1)S(1)} %select_convert_fusion.6), channel_id=1, source_target_pairs={{0,4},{4,0},{8,12},{12,8},{16,20},{20,16},{24,28},{28,24},{1,5},{5... | collective-permute-start | bytes 589832 | tf_op jit(solution)/shard_map/ppermute | solution.py:836
  176.9 16.9 %collective-permute-start.19 = (bf16[8,64,384]{2,1,0:T(8,128)(2,1)S(1)}, bf16[8,64,384]{2,1,0:T(8,128)(2,1)S(1)}, u32[]{:S(2)}, u32[]{:S(2)}) collective-permute-start(bf16[8,64,384]{2,1,0:T(8,128)(2,1)S(1)} %select_convert_fusion.1), channel_id=1, source_target_pairs={{0,2},{1,3},{2,0},{3,1},{4,6},{5,7},{6,4},{7,5},{8,10},{9,11},{10,... | collective-permute-start | bytes 1179656 | tf_op jit(solution)/shard_map/ppermute | solution.py:836
  193.9 1.4 copy-start
  194.1 6.2 %collective-permute-start.21 = (bf16[4,64,384]{2,1,0:T(8,128)(2,1)S(1)}, bf16[4,64,384]{2,1,0:T(8,128)(2,1)S(1)}, u32[]{:S(2)}, u32[]{:S(2)}) collective-permute-start(bf16[4,64,384]{2,1,0:T(8,128)(2,1)S(1)} %select_convert_fusion.5), channel_id=1, source_target_pairs={{0,4},{4,0},{8,12},{12,8},{16,20},{20,16},{24,28},{28,24},{1,5},{5... | collective-permute-start | bytes 589832 | tf_op jit(solution)/shard_map/ppermute | solution.py:836
  195.7 10.4 %collective-permute-start.22 = (bf16[8,64,384]{2,1,0:T(8,128)(2,1)S(1)}, bf16[8,64,384]{2,1,0:T(8,128)(2,1)S(1)}, u32[]{:S(2)}, u32[]{:S(2)}) collective-permute-start(bf16[8,64,384]{2,1,0:T(8,128)(2,1)S(1)} %select_convert_fusion), channel_id=1, source_target_pairs={{0,2},{1,3},{2,0},{3,1},{4,6},{5,7},{6,4},{7,5},{8,10},{9,11},{10,... | collective-permute-start | bytes 1179656 | tf_op jit(solution)/shard_map/ppermute | solution.py:836
  196.4 10.5 %collective-permute-start.26 = (bf16[16,64,256]{2,1,0:T(8,128)(2,1)S(1)}, bf16[16,64,256]{2,1,0:T(8,128)(2,1)S(1)}, u32[]{:S(2)}, u32[]{:S(2)}) collective-permute-start(bf16[16,64,256]{2,1,0:T(8,128)(2,1)S(1)} %copy-done.13), channel_id=1, source_target_pairs={{0,1},{1,0},{2,3},{3,2},{4,5},{5,4},{6,7},{7,6},{8,9},{9,8},{10,11... | collective-permute-start | bytes 1572872 | tf_op jit(solution)/shard_map/ppermute | solution.py:836
  200.4 6.5 %copy-start.4 = (f32[16,64,256]{2,1,0:T(8,128)S(1)}, f32[16,64,256]{2,1,0:T(8,128)}, u32[]{:S(2)}) copy-start(f32[16,64,256]{2,1,0:T(8,128)} %get-tuple-element.189) | copy-start | bytes 3145732
  206.3 5.7 %collective-permute-start.23 = (bf16[4,64,384]{2,1,0:T(8,128)(2,1)S(1)}, bf16[4,64,384]{2,1,0:T(8,128)(2,1)S(1)}, u32[]{:S(2)}, u32[]{:S(2)}) collective-permute-start(bf16[4,64,384]{2,1,0:T(8,128)(2,1)S(1)} %select_convert_fusion.4), channel_id=1, source_target_pairs={{0,4},{4,0},{8,12},{12,8},{16,20},{20,16},{24,28},{28,24},{1,5},{5... | collective-permute-start | bytes 589832 | tf_op jit(solution)/shard_map/ppermute | solution.py:836
  207.1 7.0 %collective-permute-start.27 = (bf16[8,64,256]{2,1,0:T(8,128)(2,1)S(1)}, bf16[8,64,256]{2,1,0:T(8,128)(2,1)S(1)}, u32[]{:S(2)}, u32[]{:S(2)}) collective-permute-start(bf16[8,64,256]{2,1,0:T(8,128)(2,1)S(1)} %select_convert_fusion.3), channel_id=1, source_target_pairs={{0,2},{1,3},{2,0},{3,1},{4,6},{5,7},{6,4},{7,5},{8,10},{9,11},{10,... | collective-permute-start | bytes 786440 | tf_op jit(solution)/shard_map/ppermute | solution.py:836
  212.1 8.5 %collective-permute-start.24 = (bf16[2,64,1152]{2,1,0:T(8,128)(2,1)S(1)}, bf16[2,64,1152]{2,1,0:T(8,128)(2,1)S(1)}, u32[]{:S(2)}, u32[]{:S(2)}) collective-permute-start(bf16[2,64,1152]{2,1,0:T(8,128)(2,1)S(1)} %pad_maximum_fusion), channel_id=1, source_target_pairs={{0,8},{4,12},{8,0},{12,4},{16,24},{20,28},{24,16},{28,20},{1,9},{5... | collective-permute-start | bytes 884744 | tf_op jit(solution)/shard_map/ppermute | solution.py:836
  214.2 5.0 %collective-permute-start.28 = (bf16[4,64,256]{2,1,0:T(8,128)(2,1)S(1)}, bf16[4,64,256]{2,1,0:T(8,128)(2,1)S(1)}, u32[]{:S(2)}, u32[]{:S(2)}) collective-permute-start(bf16[4,64,256]{2,1,0:T(8,128)(2,1)S(1)} %select_convert_fusion.8), channel_id=1, source_target_pairs={{0,4},{4,0},{8,12},{12,8},{16,20},{20,16},{24,28},{28,24},{1,5},{5... | collective-permute-start | bytes 393224 | tf_op jit(solution)/shard_map/ppermute | solution.py:836
  219.3 4.7 %collective-permute-start.29 = (bf16[2,64,256]{2,1,0:T(8,128)(2,1)S(1)}, bf16[2,64,256]{2,1,0:T(8,128)(2,1)S(1)}, u32[]{:S(2)}, u32[]{:S(2)}) collective-permute-start(bf16[2,64,256]{2,1,0:T(8,128)(2,1)S(1)} %select_convert_fusion.12), channel_id=1, source_target_pairs={{0,8},{4,12},{8,0},{12,4},{16,24},{20,28},{24,16},{28,20},{1,9},{5... | collective-permute-start | bytes 196616 | tf_op jit(solution)/shard_map/ppermute | solution.py:836
  224.0 5.5 %collective-permute-start.30 = (bf16[1,64,256]{2,1,0:T(8,128)(2,1)S(1)}, bf16[1,64,256]{2,1,0:T(8,128)(2,1)S(1)}, u32[]{:S(2)}, u32[]{:S(2)}) collective-permute-start(bf16[1,64,256]{2,1,0:T(8,128)(2,1)S(1)} %select_convert_fusion.13), channel_id=1, source_target_pairs={{0,16},{4,20},{8,24},{12,28},{16,0},{20,4},{24,8},{28,12},{1,17},{... | collective-permute-start | bytes 98312 | tf_op jit(solution)/shard_map/ppermute | solution.py:836
  226.4 7.7 %collective-permute-start.25 = (bf16[1,64,1152]{2,1,0:T(8,128)(2,1)S(1)}, bf16[1,64,1152]{2,1,0:T(8,128)(2,1)S(1)}, u32[]{:S(2)}, u32[]{:S(2)}) collective-permute-start(bf16[1,64,1152]{2,1,0:T(8,128)(2,1)S(1)} %select_convert_fusion.7), channel_id=1, source_target_pairs={{0,16},{4,20},{8,24},{12,28},{16,0},{20,4},{24,8},{28,12},{1,17},{... | collective-permute-start | bytes 442376 | tf_op jit(solution)/shard_map/ppermute | solution.py:836
  238.8 3.7 %collective-permute-start.31 = (f32[32,128]{1,0:T(8,128)S(1)}, f32[32,128]{1,0:T(8,128)S(1)}, u32[]{:S(2)}, u32[]{:S(2)}) collective-permute-start(f32[32,128]{1,0:T(8,128)S(1)} %slice.280), channel_id=1, source_target_pairs={{0,4},{4,0},{8,12},{12,8},{16,20},{20,16},{24,28},{28,24},{1,5},{5... | collective-permute-start | bytes 49160 | tf_op jit(solution)/shard_map/ppermute | solution.py:836
  243.3 3.7 %collective-permute-start.32 = (f32[32,128]{1,0:T(8,128)S(1)}, f32[32,128]{1,0:T(8,128)S(1)}, u32[]{:S(2)}, u32[]{:S(2)}) collective-permute-start(f32[32,128]{1,0:T(8,128)S(1)} %slice_add_fusion), channel_id=1, source_target_pairs={{0,8},{4,12},{8,0},{12,4},{16,24},{20,28},{24,16},{28,20},{1,9},{5... | collective-permute-start | bytes 49160 | tf_op jit(solution)/shard_map/ppermute | solution.py:836
  247.0 4.6 %collective-permute-start.33 = (f32[32,128]{1,0:T(8,128)S(1)}, f32[32,128]{1,0:T(8,128)S(1)}, u32[]{:S(2)}, u32[]{:S(2)}) collective-permute-start(f32[32,128]{1,0:T(8,128)S(1)} %add.80), channel_id=1, source_target_pairs={{0,16},{4,20},{8,24},{12,28},{16,0},{20,4},{24,8},{28,12},{1,17},{... | collective-permute-start | bytes 49160 | tf_op jit(solution)/shard_map/ppermute | solution.py:836
  251.7 5.6 %copy-start.10 = (f32[32,128]{1,0:T(8,128)}, f32[32,128]{1,0:T(8,128)S(1)}, u32[]{:S(2)}) copy-start(f32[32,128]{1,0:T(8,128)S(1)} %add.81.refs_0_) | copy-start | bytes 49156
  251.7 3.8 %collective-permute-start.34 = (f32[32,128]{1,0:T(8,128)S(1)}, f32[32,128]{1,0:T(8,128)S(1)}, u32[]{:S(2)}, u32[]{:S(2)}) collective-permute-start(f32[32,128]{1,0:T(8,128)S(1)} %pad_maximum_fusion.3), channel_id=1, source_target_pairs={{0,2},{1,3},{2,0},{3,1},{4,6},{5,7},{6,4},{7,5},{8,10},{9,11},{10,... | collective-permute-start | bytes 49160 | tf_op jit(solution)/shard_map/ppermute | solution.py:836
  255.5 1.2 collective-permute-start.35
  (2 other events, 1.7 us)

commit v4 on v3

--- a/solution.py
+++ b/solution.py
@@ -112,9 +112,7 @@
 
 
 def block_place(outer_at, inner_high, outer_bits, inner_bits):
-    place = 0
-    for bit in range(outer_bits):
-        place |= ((outer_at >> bit) & 1) << (outer_bits - 1 - bit)
+    place = outer_at
     for bit in range(inner_bits - 1):
         place |= ((inner_high >> bit) & 1) << (outer_bits + inner_bits - 2 - bit)
     return place
@@ -840,22 +838,36 @@
     return lax.optimization_barrier(values)
 
 
+def exchange(blocks, axis):
+    return lax.all_to_all(blocks, axis, split_axis=0, concat_axis=0, tiled=True)
+
+
+def sum_over(value, axis):
+    size = lax.axis_size(axis)
+    return jnp.sum(exchange(jnp.broadcast_to(value, (size,) + value.shape), axis), axis=0)
+
+
 class Gather:
     def __init__(self, piece, steps):
         self.held, self.steps, self.at = piece[None], steps, 0
 
     def send(self):
-        axis, bit = self.steps[self.at]
-        self.other = swap(self.held, axis, 1 << bit)
+        if self.at == 0:
+            size = lax.axis_size("dp")
+            self.other = exchange(jnp.broadcast_to(self.held, (size,) + self.held.shape[1:]), "dp")
+        else:
+            self.other = swap(self.held, "fsdp", 1 << self.steps[self.at - 1])
 
     def join(self):
-        axis, bit = self.steps[self.at]
-        upper = (lax.axis_index(axis) >> bit) & 1 == 1
-        self.held = jnp.where(
-            upper,
-            jnp.concatenate([self.other, self.held]),
-            jnp.concatenate([self.held, self.other]),
-        )
+        if self.at == 0:
+            self.held = self.other
+        else:
+            upper = (lax.axis_index("fsdp") >> self.steps[self.at - 1]) & 1 == 1
+            self.held = jnp.where(
+                upper,
+                jnp.concatenate([self.other, self.held]),
+                jnp.concatenate([self.held, self.other]),
+            )
         self.at += 1
 
     def step(self, after=None):
@@ -870,31 +882,25 @@
         self.sent, self.kept, self.steps, self.at = sent, kept, steps, 0
 
     def send(self):
-        axis, bit = self.steps[self.at]
-        self.other = swap(self.sent, axis, 1 << bit)
+        if self.at == len(self.steps):
+            self.other = exchange(self.sent, "dp")
+        else:
+            self.other = swap(self.sent, "fsdp", 1 << self.steps[self.at])
 
     def join(self):
         self.at += 1
+        if self.at > len(self.steps):
+            self.kept = jnp.sum(self.other.astype(jnp.float32), axis=0)
+            return
         summed = self.kept + self.other.astype(jnp.float32)
         if self.at == len(self.steps):
-            self.kept = summed
+            self.sent = summed.astype(jnp.bfloat16)
             return
-        axis, bit = self.steps[self.at]
-        side = (lax.axis_index(axis) >> bit) & 1
+        side = (lax.axis_index("fsdp") >> self.steps[self.at]) & 1
         half = summed.shape[0] // 2
         parts = summed.reshape((2, half) + summed.shape[1:])
         self.sent = jnp.where(side == 1, parts[0], parts[1]).astype(jnp.bfloat16)
         self.kept = jnp.where(side == 1, parts[1], parts[0])
-
-
-def merged(parts):
-    whole = Scatter(
-        jnp.concatenate([part.sent for part in parts], axis=2),
-        jnp.concatenate([part.kept for part in parts], axis=2),
-        parts[0].steps,
-    )
-    whole.at = parts[0].at
-    return whole
 
 
 def shards(
@@ -926,9 +932,8 @@
     samples = latents.shape[0]
     sizes = (lax.axis_size("dp"), lax.axis_size("fsdp"))
     bits = (sizes[0].bit_length() - 1, sizes[1].bit_length() - 1)
-    gather_steps = [("dp", bit) for bit in reversed(range(bits[0]))]
-    gather_steps = gather_steps + [("fsdp", bit) for bit in reversed(range(bits[1]))]
-    scatter_steps = gather_steps[::-1]
+    scatter_steps = list(range(bits[1]))
+    gather_steps = scatter_steps[::-1]
     core = (lax.axis_index("fsdp") & 1).astype(jnp.int32).reshape(1)
 
     low = lambda item: item.astype(jnp.bfloat16)
@@ -960,7 +965,7 @@
     counted = counted.astype(jnp.float32).reshape(1, samples * SEG)
     shared = (gains, memory_valid, core)
 
-    count = len(gather_steps)
+    count = len(gather_steps) + 1
     for at in range(count - 1):
         first.step()
         if at < count - 2:
@@ -1025,31 +1030,23 @@
     sent, top.other, two.other, one.other = tie(sent, top.other, two.other, one.other)
     zero = Scatter(sent, held, scatter_steps)
     zero.send()
+    chunks = [top, two, one, zero]
+    top.join()
     two.join()
     two.send()
     one.join()
     one.send()
-    top.join()
-    zero.join()
-    zero.send()
-    one.join()
-    one.send()
-    two.join()
-    zero.join()
-    zero.send()
-    one.join()
-    early = merged([top, two, one])
-    while early.at < count:
-        early.send()
-        early.join()
-        zero.join()
-        if zero.at < count:
-            zero.send()
     while zero.at < count:
-        zero.join()
-        if zero.at < count:
-            zero.send()
-    raw_early, raw_late = early.kept[0], zero.kept[0]
+        for chunk in chunks[1:]:
+            if chunk.at < count:
+                chunk.join()
+                if chunk.at < count:
+                    chunk.send()
+    while top.at < count:
+        top.send()
+        top.join()
+    raw_early = jnp.concatenate([top.kept, two.kept, one.kept], axis=1)
+    raw_late = zero.kept
 
     flat = lambda item: item if item.ndim == 2 else item.reshape(1, -1)
     inner = [flat(item) for item in (qkv_rows, out_rows, up_rows, down_cols, embed_cols, head_rows)]
@@ -1058,12 +1055,8 @@
     gain_parts = [gain_top, gain_two, gain_one, gain_zero]
     packet = run_stats(widths, raw_early, raw_late, masters, row_stats, gain_parts, loss, counted)
     edge = INNER_ROWS + COMMON_ROWS
-    across = packet[:edge]
-    for axis, bit in scatter_steps[bits[1] :]:
-        across = across + swap(across, axis, 1 << bit)
-    along = jnp.concatenate([across[INNER_ROWS:], packet[edge:]])
-    for axis, bit in scatter_steps[: bits[1]][::-1]:
-        along = along + swap(along, axis, 1 << bit)
+    across = sum_over(packet[:edge], "dp")
+    along = sum_over(jnp.concatenate([across[INNER_ROWS:], packet[edge:]]), "fsdp")
     results = run_update(
         widths, sizes, across, along, raw_early, raw_late, masters, inner, outer, gains, gain_second
     )

time: 266 us -> 300 us (1.13)
  waiting for transfers between devices: 71.3 us -> 81.9 us
  starting transfers between devices: 38.1 us -> 45 us
  blocking collectives: 0 us -> 6.72 us
  other arithmetic: 9.49 us -> 15.3 us
  local copies, waits for them, and re-layouts: 7.32 us -> 11.6 us
    all_to_all x0 -> x8, waiting for transfers between devices: none -> 60.8 us  [exchange(): return lax.all_to_all(blocks, axis, split_axis=0, concat_axis=0, tiled=True)]
    ppermute x36 -> x14, waiting for transfers between devices: 71.3 us -> 21 us  [swap(): return lax.ppermute(value, axis, pairs)]
    all_to_all x0 -> x8, starting transfers between devices: none -> 37.5 us  [exchange(): return lax.all_to_all(blocks, axis, split_axis=0, concat_axis=0, tiled=True)]
    ppermute x36 -> x14, starting transfers between devices: 38.1 us -> 7.53 us  [swap(): return lax.ppermute(value, axis, pairs)]
    all_to_all x0 -> x1, blocking collectives: none -> 6.72 us  [exchange(): return lax.all_to_all(blocks, axis, split_axis=0, concat_axis=0, tiled=True)]
    convert_element_type x0 -> x4, other arithmetic: none -> 4.5 us  [join(): self.sent = summed.astype(jnp.bfloat16)]
    broadcast_in_dim x0 -> x5, local copies, waits for them, and re-layouts: none -> 3.14 us  [the longest x3 2.46 us: send(): jnp.broadcast_to(self.held, (size,) + self.held.shape[1:])]
  transfers between devices with their start and end apart: 36 -> 22, of which waited for: 23 -> 12; matrix products, arithmetic and copies ran while one was open for 3% -> 5% of each run, Pallas kernels for 38% -> 34%
where the time goes in v4:
time: 300 us; the launch traced here: 295 us
  Pallas kernels  134 us (45%)
  waiting for transfers between devices  81.9 us (27%)
  starting transfers between devices  45 us (15%)
  other arithmetic  15.3 us (5%)
  local copies, waits for them, and re-layouts  11.6 us (4%)
  blocking collectives  6.72 us (2%)
    pallas_call x3, Pallas kernels, run_backward(): pl.pallas_call(functools.partial(backward_kernel, layer, widths, bits), g...  70.9 us
    all_to_all x8, waiting for transfers between devices, exchange(): return lax.all_to_all(blocks, axis, split_axis=0, concat_axis=0, tiled=True)  60.8 us
    pallas_call x3, Pallas kernels, run_forward(): pl.pallas_call(functools.partial(forward_kernel, layer, widths, bits), gr...  45 us
    all_to_all x8, starting transfers between devices, exchange(): return lax.all_to_all(blocks, axis, split_axis=0, concat_axis=0, tiled=True)  37.5 us
    ppermute x14, waiting for transfers between devices, swap(): return lax.ppermute(value, axis, pairs)  21 us
    pallas_call x1, Pallas kernels, run_top(): pl.pallas_call(functools.partial(top_kernel, widths, bits, start), in_spe...  11.1 us
    ppermute x14, starting transfers between devices, swap(): return lax.ppermute(value, axis, pairs)  7.53 us
    all_to_all x1, blocking collectives, exchange(): return lax.all_to_all(blocks, axis, split_axis=0, concat_axis=0, tiled=True)  6.72 us
  transfers between devices with their start and end apart: 22, of which 12 were waited for; matrix products, arithmetic and copies ran while one was open for 5% of the time, Pallas kernels for 34%

profile of v4, /device:TPU:0, one launch (start us, length us, event | category | flops | bytes accessed | tf_op | source)
XLA Modules:
  0.0 295.5 jit_solution(7721454491082892619)
XLA Ops:
  1.5 0.9 copy.58
  2.4 0.9 convert.42
  4.1 7.3 %all-to-all-start = ((bf16[8,64,256]{2,1,0:T(8,128)(2,1)}), bf16[8,64,256]{2,1,0:T(8,128)(2,1)S(1)}, u32[]{:S(2)}, u32[]{:S(2)}) async-start(bf16[8,64,256]{2,1,0:T(8,128)(2,1)} %broadcast_in_dim.14), calls=%async_computation | async-start | bytes 524288 | tf_op jit(solution)/shard_map/all_to_all | solution.py:842
  11.4 0.9 convert.45
  12.3 8.0 %all-to-all-done = bf16[8,64,256]{2,1,0:T(8,128)(2,1)S(1)} async-done(((bf16[8,64,256]{2,1,0:T(8,128)(2,1)}), bf16[8,64,256]{2,1,0:T(8,128)(2,1)S(1)}, u32[]{:S(2)}, u32[]{:S(2)}) %all-to-all-start) | async-done | bytes 262176 | tf_op jit(solution)/shard_map/all_to_all | solution.py:842
  20.3 1.5 collective-permute-start
  21.9 0.8 broadcast_in_dim.32
  22.7 3.6 %all-to-all-start.1 = ((bf16[8,64,384]{2,1,0:T(8,128)(2,1)}), bf16[8,64,384]{2,1,0:T(8,128)(2,1)S(1)}, u32[]{:S(2)}, u32[]{:S(2)}) async-start(bf16[8,64,384]{2,1,0:T(8,128)(2,1)} %broadcast_in_dim.32), calls=%async_computation.1 | async-start | bytes 786432 | tf_op jit(solution)/shard_map/all_to_all | solution.py:842
  26.8 10.5 %all-to-all-done.1 = bf16[8,64,384]{2,1,0:T(8,128)(2,1)S(1)} async-done(((bf16[8,64,384]{2,1,0:T(8,128)(2,1)}), bf16[8,64,384]{2,1,0:T(8,128)(2,1)S(1)}, u32[]{:S(2)}, u32[]{:S(2)}) %all-to-all-start.1) | async-done | bytes 393248 | tf_op jit(solution)/shard_map/all_to_all | solution.py:842
  37.9 7.4 %collective-permute-done.2 = bf16[8,64,384]{2,1,0:T(8,128)(2,1)S(1)} collective-permute-done((bf16[8,64,384]{2,1,0:T(8,128)(2,1)S(1)}, bf16[8,64,384]{2,1,0:T(8,128)(2,1)S(1)}, u32[]{:S(2)}, u32[]{:S(2)}) %collective-permute-start.2) | collective-permute-done | bytes 393248 | tf_op jit(solution)/shard_map/ppermute | solution.py:834
  45.3 0.9 broadcast_in_dim.34
  46.2 6.0 %all-to-all-start.2 = ((bf16[8,64,768]{2,1,0:T(8,128)(2,1)}), bf16[8,64,768]{2,1,0:T(8,128)(2,1)S(1)}, u32[]{:S(2)}, u32[]{:S(2)}) async-start(bf16[8,64,768]{2,1,0:T(8,128)(2,1)} %broadcast_in_dim.34), calls=%async_computation.2 | async-start | bytes 1572864 | tf_op jit(solution)/shard_map/all_to_all | solution.py:842
  52.4 18.6 %all-to-all-done.2 = bf16[8,64,768]{2,1,0:T(8,128)(2,1)S(1)} async-done(((bf16[8,64,768]{2,1,0:T(8,128)(2,1)}), bf16[8,64,768]{2,1,0:T(8,128)(2,1)S(1)}, u32[]{:S(2)}, u32[]{:S(2)}) %all-to-all-start.2) | async-done | bytes 786464 | tf_op jit(solution)/shard_map/all_to_all | solution.py:842
  71.5 1.0 convert_element_type.97
  72.5 1.0 copy.57
  73.4 13.9 %forward_part.3 = (f32[1536,256]{1,0:T(8,128)}, f32[1536,256]{1,0:T(8,128)}, bf16[1536,768]{1,0:T(8,128)(2,1)}, bf16[1536,256]{1,0:T(8,128)(2,1)}, f32[16,1,768]{2,1,0:T(1,128)}, /*index=5*/bf16[256,1024]{1,0:T(8,128)(2,1)}) custom-call(bf16[1536,32]{1,0:T(8,128)(2,1)} %bitcast.38, bf16[16,64,256]{2,1,0:T(8,128)(2,1)} %copy-done.7, ...), custom_call_target="tpu_custom_call" | custom-call | flops 2415919104 | bytes 9437184 | tf_op jit(solution)/shard_map/forward_part/pallas_call | solution.py:358
  87.3 3.6 %collective-permute-done.4 = bf16[8,64,768]{2,1,0:T(8,128)(2,1)S(1)} collective-permute-done((bf16[8,64,768]{2,1,0:T(8,128)(2,1)S(1)}, bf16[8,64,768]{2,1,0:T(8,128)(2,1)S(1)}, u32[]{:S(2)}, u32[]{:S(2)}) %collective-permute-start.4) | collective-permute-done | bytes 786464 | tf_op jit(solution)/shard_map/ppermute | solution.py:834
  92.3 1.1 copy.59
  94.2 15.1 %forward_part.4 = (f32[1536,256]{1,0:T(8,128)}, f32[1536,256]{1,0:T(8,128)}, bf16[1536,768]{1,0:T(8,128)(2,1)}, bf16[1536,256]{1,0:T(8,128)(2,1)}, f32[16,1,768]...) custom-call(f32[1536,256]{1,0:T(8,128)} %get-tuple-element.136.source_ref.refs_9_, ...), custom_call_target="tpu_custom_call" | custom-call | flops 2415919104 | bytes 9437184 | tf_op jit(solution)/shard_map/forward_part/pallas_call | solution.py:358
  109.3 16.0 %forward_part.5 = (f32[1536,256]{1,0:T(8,128)}, f32[768,256]{1,0:T(8,128)}, bf16[1536,768]{1,0:T(8,128)(2,1)}, bf16[768,256]{1,0:T(8,128)(2,1)}, f32[16,1,384]{2...) custom-call(f32[1536,256]{1,0:T(8,128)} %get-tuple-element.146.source_ref.refs_9_, ...), custom_call_target="tpu_custom_call" | custom-call | flops 2415919104 | bytes 9437184 | tf_op jit(solution)/shard_map/forward_part/pallas_call | solution.py:358
  125.4 11.1 %loss_part.1 = (f32[768,256]{1,0:T(8,128)}, bf16[16,64,384]{2,1,0:T(8,128)(2,1)}, f32[16,64,384]{2,1,0:T(8,128)}, f32[2,256]{1,0:T(2,128)}, f32[1,1]{1,0:T(1,128)}) custom-call(f32[768,256]{1,0:T(8,128)} %get-tuple-element.152.middle_ref, bf16[16,64,768]{2,1,0:T(8,128)(2,1)} %copy-done.1, bf16[16,64,768]{2,1,0:T(8,128)(2,1)} %collective-permute-done.5.other_ref, ...), custom_call_target="tpu_custom_call" | custom-call | flops 3623878656 | bytes 9437184 | tf_op jit(solution)/shard_map/loss_part/pallas_call | solution.py:480
  136.6 23.3 %backward_part.3 = (f32[1536,256]{1,0:T(8,128)}, bf16[16,64,384]{2,1,0:T(8,128)(2,1)}, f32[16,64,384]{2,1,0:T(8,128)}, f32[2,256]{1,0:T(2,128)}) custom-call(f32[1536,256]{1,0:T(8,128)} %get-tuple-element.148.refs_0_, bf16[1536,768]{1,0:T(8,128)(2,1)} %get-tuple-element.149.refs_1_, bf16[768,256]{1,0:T(8,128)(2,1)} %get-tuple-element.150.refs_2_, ...), custom_call_target="tpu_custom_call" | custom-call | flops 7247757312 | bytes 14155776 | tf_op jit(solution)/shard_map/backward_part/pallas_call | solution.py:621
  161.2 32.4 %backward_part.4 = (f32[1536,256]{1,0:T(8,128)}, bf16[16,64,384]{2,1,0:T(8,128)(2,1)}, f32[16,64,384]{2,1,0:T(8,128)}, f32[2,256]{1,0:T(2,128)}) custom-call(f32[1536,256]{1,0:T(8,128)} %get-tuple-element.140.refs_0_, bf16[1536,768]{1,0:T(8,128)(2,1)} %get-tuple-element.141.refs_1_, bf16[1536,256]{1,0:T(8,128)(2,1)} %get-tuple-element.142.refs_2_, ...), custom_call_target="tpu_custom_call" | custom-call | flops 7247757312 | bytes 14155776 | tf_op jit(solution)/shard_map/backward_part/pallas_call | solution.py:621
  193.7 0.9 add_convert_fusion.2
  195.4 3.6 %all-to-all-start.3 = ((bf16[8,64,384]{2,1,0:T(8,128)(2,1)}), bf16[8,64,384]{2,1,0:T(8,128)(2,1)S(1)}, u32[]{:S(2)}, u32[]{:S(2)}) async-start(bf16[8,64,384]{2,1,0:T(8,128)(2,1)} %add_convert_fusion.2), calls=%async_computation.3 | async-start | bytes 786432 | tf_op jit(solution)/shard_map/all_to_all | solution.py:842
  198.9 1.5 collective-permute-start.9
  200.5 15.2 %backward_part.5 = (bf16[16,64,256]{2,1,0:T(8,128)(2,1)}, f32[16,64,256]{2,1,0:T(8,128)}, f32[2,256]{1,0:T(2,128)}) custom-call(f32[1536,256]{1,0:T(8,128)} %get-tuple-element.129.refs_0_, bf16[1536,768]{1,0:T(8,128)(2,1)} %get-tuple-element.130.refs_1_, bf16[1536,256]{1,0:T(8,128)(2,1)} %get-tuple-element.131.refs_2_, ...), custom_call_target="tpu_custom_call" | custom-call | flops 4831838208 | bytes 12582912 | tf_op jit(solution)/shard_map/backward_part/pallas_call | solution.py:621
  216.4 0.9 copy-done.6
  217.3 1.8 convert_add_fusion
  219.1 0.8 select_convert_fusion
  220.5 0.9 add_convert_fusion.1
  221.4 6.2 %all-to-all-start.4 = ((bf16[8,64,384]{2,1,0:T(8,128)(2,1)}), bf16[8,64,384]{2,1,0:T(8,128)(2,1)S(1)}, u32[]{:S(2)}, u32[]{:S(2)}) async-start(bf16[8,64,384]{2,1,0:T(8,128)(2,1)} %add_convert_fusion.1), calls=%async_computation.4 | async-start | bytes 786432 | tf_op jit(solution)/shard_map/all_to_all | solution.py:842
  227.6 3.3 %collective-permute-done.11 = bf16[8,64,384]{2,1,0:T(8,128)(2,1)} collective-permute-done((bf16[8,64,384]{2,1,0:T(8,128)(2,1)}, bf16[8,64,384]{2,1,0:T(8,128)(2,1)}, u32[]{:S(2)}, u32[]{:S(2)}) %collective-permute-start.11) | collective-permute-done | bytes 393248 | tf_op jit(solution)/shard_map/ppermute | solution.py:834
  230.9 1.9 add_convert_fusion
  232.8 1.2 convert_add_fusion.3
  234.0 6.0 %all-to-all-done.4 = bf16[8,64,384]{2,1,0:T(8,128)(2,1)S(1)} async-done(((bf16[8,64,384]{2,1,0:T(8,128)(2,1)}), bf16[8,64,384]{2,1,0:T(8,128)(2,1)S(1)}, u32[]{:S(2)}, u32[]{:S(2)}) %all-to-all-start.4) | async-done | bytes 393248 | tf_op jit(solution)/shard_map/all_to_all | solution.py:842
  239.9 3.6 %all-to-all-start.5 = ((bf16[8,64,384]{2,1,0:T(8,128)(2,1)}), bf16[8,64,384]{2,1,0:T(8,128)(2,1)S(1)}, u32[]{:S(2)}, u32[]{:S(2)}) async-start(bf16[8,64,384]{2,1,0:T(8,128)(2,1)} %add_convert_fusion), calls=%async_computation.5 | async-start | bytes 786432 | tf_op jit(solution)/shard_map/all_to_all | solution.py:842
  243.6 1.6 collective-permute-start.13
  245.3 6.4 %collective-permute-done.13 = bf16[8,64,256]{2,1,0:T(8,128)(2,1)S(1)} collective-permute-done((bf16[8,64,256]{2,1,0:T(8,128)(2,1)S(1)}, bf16[8,64,256]{2,1,0:T(8,128)(2,1)S(1)}, u32[]{:S(2)}, u32[]{:S(2)}) %collective-permute-start.13) | collective-permute-done | bytes 262176 | tf_op jit(solution)/shard_map/ppermute | solution.py:834
  251.6 0.8 add_convert_fusion.3
  252.5 3.0 %all-to-all-done.5 = bf16[8,64,384]{2,1,0:T(8,128)(2,1)S(1)} async-done(((bf16[8,64,384]{2,1,0:T(8,128)(2,1)}), bf16[8,64,384]{2,1,0:T(8,128)(2,1)S(1)}, u32[]{:S(2)}, u32[]{:S(2)}) %all-to-all-start.5) | async-done | bytes 393248 | tf_op jit(solution)/shard_map/all_to_all | solution.py:842
  255.4 3.6 %all-to-all-start.6 = ((bf16[8,64,256]{2,1,0:T(8,128)(2,1)}), bf16[8,64,256]{2,1,0:T(8,128)(2,1)S(1)}, u32[]{:S(2)}, u32[]{:S(2)}) async-start(bf16[8,64,256]{2,1,0:T(8,128)(2,1)} %add_convert_fusion.3), calls=%async_computation.6 | async-start | bytes 524288 | tf_op jit(solution)/shard_map/all_to_all | solution.py:842
  259.9 8.2 %all-to-all-done.6 = bf16[8,64,256]{2,1,0:T(8,128)(2,1)S(1)} async-done(((bf16[8,64,256]{2,1,0:T(8,128)(2,1)}), bf16[8,64,256]{2,1,0:T(8,128)(2,1)S(1)}, u32[]{:S(2)}, u32[]{:S(2)}) %all-to-all-start.6) | async-done | bytes 262176 | tf_op jit(solution)/shard_map/all_to_all | solution.py:842
  268.8 3.2 %statistics.1 = f32[48,128]{1,0:T(8,128)} custom-call(f32[64,1152]{1,0:T(8,128)} %pad_maximum_fusion.refs_0_.refs_2_, f32[64,256]{1,0:T(8,128)} %convert_reduce_fusion.3.refs_1_.refs_3_, f32[3,64,96]{2,1,0:T(8,128)} %refs_4_.3, f32[3,32,64]{2,1,0:T(8,128)} %bitcast.35, f32[3,64,128]{2,1,0:T(8,128)} %refs_6_.7, f32[3,64,128]{2,1,0:T(8,128)} %bitcast.33, ...), custom_call_target="tpu_custom_call" | custom-call | tf_op jit(solution)/shard_map/statistics/pallas_call | solution.py:715
  273.4 3.6 %all-to-all-start.7 = ((f32[8,32,128]{2,1,0:T(8,128)}), f32[8,32,128]{2,1,0:T(8,128)S(1)}, u32[]{:S(2)}, u32[]{:S(2)}) async-start(f32[8,32,128]{2,1,0:T(8,128)} %broadcast_in_dim.35), calls=%async_computation.7 | async-start | bytes 262144 | tf_op jit(solution)/shard_map/all_to_all | solution.py:842
  277.7 6.6 %all-to-all-done.7 = f32[8,32,128]{2,1,0:T(8,128)S(1)} async-done(((f32[8,32,128]{2,1,0:T(8,128)}), f32[8,32,128]{2,1,0:T(8,128)S(1)}, u32[]{:S(2)}, u32[]{:S(2)}) %all-to-all-start.7) | async-done | bytes 131104 | tf_op jit(solution)/shard_map/all_to_all | solution.py:842
  284.4 6.7 %all_to_all.45 = f32[4,32,128]{2,1,0:T(8,128)S(1)} all-to-all(f32[4,32,128]{2,1,0:T(8,128)S(1)} %broadcast_in_dim.36), channel_id=1, replica_groups=mesh['dp'=8,'fsdp'=4] {'fsdp'}, dimensions={0} | all-to-all | bytes 131072 | tf_op jit(solution)/shard_map/all_to_all | solution.py:842
  291.7 3.5 %update.1 = (f32[1,1]{1,0:T(1,128)}, f32[1,1]{1,0:T(1,128)}, f32[1,1]{1,0:T(1,128)}, f32[64,128]{1,0:T(8,128)}, f32[64,128]{1,0:T(8,128)}, /*index=5*/f32[1,128]...) custom-call(f32[32,128]{1,0:T(8,128)} %copy-done.11, ...), custom_call_target="tpu_custom_call" | custom-call | tf_op jit(solution)/shard_map/update/pallas_call | solution.py:823
  (85 shorter events, 13.6 us)
Async XLA Ops:
  0.7 11.6 %copy-start.4 = (f32[3,128,64]{1,2,0:T(8,128)S(1)}, f32[3,128,64]{1,2,0:T(8,128)}, u32[]{:S(2)}) copy-start(f32[3,128,64]{1,2,0:T(8,128)} %param.32) | copy-start | bytes 294916
  4.1 16.2 %all-to-all-start = ((bf16[8,64,256]{2,1,0:T(8,128)(2,1)}), bf16[8,64,256]{2,1,0:T(8,128)(2,1)S(1)}, u32[]{:S(2)}, u32[]{:S(2)}) async-start(bf16[8,64,256]{2,1,0:T(8,128)(2,1)} %broadcast_in_dim.14), calls=%async_computation | async-start | bytes 524288 | tf_op jit(solution)/shard_map/all_to_all | solution.py:842
  11.4 26.5 %copy-start.10 = (f32[64,128]{1,0:T(8,128)S(1)}, f32[64,128]{1,0:T(8,128)}, u32[]{:S(2)}) copy-start(f32[64,128]{1,0:T(8,128)} %refs_9_.3) | copy-start | bytes 98308
  20.3 6.4 %collective-permute-start = (bf16[8,64,256]{2,1,0:T(8,128)(2,1)S(1)}, bf16[8,64,256]{2,1,0:T(8,128)(2,1)S(1)}, u32[]{:S(2)}, u32[]{:S(2)}) collective-permute-start(bf16[8,64,256]{2,1,0:T(8,128)(2,1)S(1)} %all-to-all-done), channel_id=1, source_target_pairs={{0,2},{1,3},{2,0},{3,1},{4,6},{5,7},{6,4},{7,5},{8,10},{9,11},{10,... | collective-permute-start | bytes 786440 | tf_op jit(solution)/shard_map/ppermute | solution.py:834
  22.7 14.6 %all-to-all-start.1 = ((bf16[8,64,384]{2,1,0:T(8,128)(2,1)}), bf16[8,64,384]{2,1,0:T(8,128)(2,1)S(1)}, u32[]{:S(2)}, u32[]{:S(2)}) async-start(bf16[8,64,384]{2,1,0:T(8,128)(2,1)} %broadcast_in_dim.32), calls=%async_computation.1 | async-start | bytes 786432 | tf_op jit(solution)/shard_map/all_to_all | solution.py:842
  26.7 25.6 %copy-start.7 = (bf16[16,64,256]{2,1,0:T(8,128)(2,1)}, bf16[16,64,256]{2,1,0:T(8,128)(2,1)S(1)}, u32[]{:S(2)}) copy-start(bf16[16,64,256]{2,1,0:T(8,128)(2,1)S(1)} %maximum_select_fusion.2.own_ref) | copy-start | bytes 1572868
  26.7 10.6 %collective-permute-start.1 = (bf16[16,64,256]{2,1,0:T(8,128)(2,1)S(1)}, bf16[16,64,256]{2,1,0:T(8,128)(2,1)S(1)}, u32[]{:S(2)}, u32[]{:S(2)}) collective-permute-start(bf16[16,64,256]{2,1,0:T(8,128)(2,1)S(1)} %maximum_select_fusion.2.own_ref), channel_id=1, source_target_pairs={{0,1},{1,0},{2,3},{3,2},{4,5},{5,4},{6,7},{7,6},{8,9},{9,8},{10,11... | collective-permute-start | bytes 1572872 | tf_op jit(solution)/shard_map/ppermute | solution.py:834
  37.3 8.9 %copy-start.14 = (bf16[16,64,256]{2,1,0:T(8,128)(2,1)}, bf16[16,64,256]{2,1,0:T(8,128)(2,1)S(1)}, u32[]{:S(2)}) copy-start(bf16[16,64,256]{2,1,0:T(8,128)(2,1)S(1)} %collective-permute-done.1.other_ref) | copy-start | bytes 1572868
  37.3 8.0 %collective-permute-start.2 = (bf16[8,64,384]{2,1,0:T(8,128)(2,1)S(1)}, bf16[8,64,384]{2,1,0:T(8,128)(2,1)S(1)}, u32[]{:S(2)}, u32[]{:S(2)}) collective-permute-start(bf16[8,64,384]{2,1,0:T(8,128)(2,1)S(1)} %all-to-all-done.1), channel_id=1, source_target_pairs={{0,2},{1,3},{2,0},{3,1},{4,6},{5,7},{6,4},{7,5},{8,10},{9,11},{10,... | collective-permute-start | bytes 1179656 | tf_op jit(solution)/shard_map/ppermute | solution.py:834
  46.2 24.8 %all-to-all-start.2 = ((bf16[8,64,768]{2,1,0:T(8,128)(2,1)}), bf16[8,64,768]{2,1,0:T(8,128)(2,1)S(1)}, u32[]{:S(2)}, u32[]{:S(2)}) async-start(bf16[8,64,768]{2,1,0:T(8,128)(2,1)} %broadcast_in_dim.34), calls=%async_computation.2 | async-start | bytes 1572864 | tf_op jit(solution)/shard_map/all_to_all | solution.py:842
  52.4 34.9 %copy-start.5 = (bf16[16,64,384]{2,1,0:T(8,128)(2,1)}, bf16[16,64,384]{2,1,0:T(8,128)(2,1)S(1)}, u32[]{:S(2)}) copy-start(bf16[16,64,384]{2,1,0:T(8,128)(2,1)S(1)} %maximum_select_fusion.1.own_ref) | copy-start | bytes 2359300
  71.0 16.3 %collective-permute-start.3 = (bf16[16,64,384]{2,1,0:T(8,128)(2,1)S(1)}, bf16[16,64,384]{2,1,0:T(8,128)(2,1)S(1)}, u32[]{:S(2)}, u32[]{:S(2)}) collective-permute-start(bf16[16,64,384]{2,1,0:T(8,128)(2,1)S(1)} %maximum_select_fusion.1.own_ref), channel_id=1, source_target_pairs={{0,1},{1,0},{2,3},{3,2},{4,5},{5,4},{6,7},{7,6},{8,9},{9,8},{10,11... | collective-permute-start | bytes 2359304 | tf_op jit(solution)/shard_map/ppermute | solution.py:834
  71.0 20.0 %collective-permute-start.4 = (bf16[8,64,768]{2,1,0:T(8,128)(2,1)S(1)}, bf16[8,64,768]{2,1,0:T(8,128)(2,1)S(1)}, u32[]{:S(2)}, u32[]{:S(2)}) collective-permute-start(bf16[8,64,768]{2,1,0:T(8,128)(2,1)S(1)} %all-to-all-done.2), channel_id=1, source_target_pairs={{0,2},{1,3},{2,0},{3,1},{4,6},{5,7},{6,4},{7,5},{8,10},{9,11},{10,... | collective-permute-start | bytes 2359304 | tf_op jit(solution)/shard_map/ppermute | solution.py:834
  87.3 3.6 %copy-start.13 = (bf16[16,64,384]{2,1,0:T(8,128)(2,1)}, bf16[16,64,384]{2,1,0:T(8,128)(2,1)S(1)}, u32[]{:S(2)}) copy-start(bf16[16,64,384]{2,1,0:T(8,128)(2,1)S(1)} %collective-permute-done.3.other_ref) | copy-start | bytes 2359300
  90.9 0.7 copy-start.12
  91.2 18.1 %copy-start.1 = (bf16[16,64,768]{2,1,0:T(8,128)(2,1)}, bf16[16,64,768]{2,1,0:T(8,128)(2,1)S(1)}, u32[]{:S(2)}) copy-start(bf16[16,64,768]{2,1,0:T(8,128)(2,1)S(1)} %maximum_select_fusion.own_ref) | copy-start | bytes 4718596
  91.2 18.1 %collective-permute-start.5 = (bf16[16,64,768]{2,1,0:T(8,128)(2,1)S(1)}, bf16[16,64,768]{2,1,0:T(8,128)(2,1)}, u32[]{:S(2)}, u32[]{:S(2)}) collective-permute-start(bf16[16,64,768]{2,1,0:T(8,128)(2,1)S(1)} %maximum_select_fusion.own_ref), channel_id=1, source_target_pairs={{0,1},{1,0},{2,3},{3,2},{4,5},{5,4},{6,7},{7,6},{8,9},{9,8},{10,11... | collective-permute-start | bytes 4718600 | tf_op jit(solution)/shard_map/ppermute | solution.py:834
  136.5 23.9 %collective-permute-start.6 = (bf16[16,64,384]{2,1,0:T(8,128)(2,1)}, bf16[16,64,384]{2,1,0:T(8,128)(2,1)S(1)}, u32[]{:S(2)}, u32[]{:S(2)}) collective-permute-start(bf16[16,64,384]{2,1,0:T(8,128)(2,1)} %get-tuple-element.157), channel_id=1, source_target_pairs={{0,1},{1,0},{2,3},{3,2},{4,5},{5,4},{6,7},{7,6},{8,9},{9,8},{10,11... | collective-permute-start | bytes 2359304 | tf_op jit(solution)/shard_map/ppermute | solution.py:834
  136.6 23.7 %copy-start.2 = (f32[16,64,384]{2,1,0:T(8,128)S(1)}, f32[16,64,384]{2,1,0:T(8,128)}, u32[]{:S(2)}) copy-start(f32[16,64,384]{2,1,0:T(8,128)} %get-tuple-element.159) | copy-start | bytes 4718596
  160.0 33.7 %collective-permute-start.8 = (bf16[16,64,384]{2,1,0:T(8,128)(2,1)}, bf16[16,64,384]{2,1,0:T(8,128)(2,1)S(1)}, u32[]{:S(2)}, u32[]{:S(2)}) collective-permute-start(bf16[16,64,384]{2,1,0:T(8,128)(2,1)} %get-tuple-element.166), channel_id=1, source_target_pairs={{0,1},{1,0},{2,3},{3,2},{4,5},{5,4},{6,7},{7,6},{8,9},{9,8},{10,11... | collective-permute-start | bytes 2359304 | tf_op jit(solution)/shard_map/ppermute | solution.py:834
  160.6 33.1 %collective-permute-start.7 = (bf16[8,64,384]{2,1,0:T(8,128)(2,1)S(1)}, bf16[8,64,384]{2,1,0:T(8,128)(2,1)S(1)}, u32[]{:S(2)}, u32[]{:S(2)}) collective-permute-start(bf16[8,64,384]{2,1,0:T(8,128)(2,1)S(1)} %select_convert_fusion.2), channel_id=1, source_target_pairs={{0,2},{1,3},{2,0},{3,1},{4,6},{5,7},{6,4},{7,5},{8,10},{9,11},{10,... | collective-permute-start | bytes 1179656 | tf_op jit(solution)/shard_map/ppermute | solution.py:834
  193.6 1.6 copy-start
  193.6 22.8 %collective-permute-start.10 = (bf16[16,64,384]{2,1,0:T(8,128)(2,1)}, bf16[16,64,384]{2,1,0:T(8,128)(2,1)S(1)}, u32[]{:S(2)}, u32[]{:S(2)}) collective-permute-start(bf16[16,64,384]{2,1,0:T(8,128)(2,1)} %get-tuple-element.176), channel_id=1, source_target_pairs={{0,1},{1,0},{2,3},{3,2},{4,5},{5,4},{6,7},{7,6},{8,9},{9,8},{10,11... | collective-permute-start | bytes 2359304 | tf_op jit(solution)/shard_map/ppermute | solution.py:834
  195.4 21.0 %all-to-all-start.3 = ((bf16[8,64,384]{2,1,0:T(8,128)(2,1)}), bf16[8,64,384]{2,1,0:T(8,128)(2,1)S(1)}, u32[]{:S(2)}, u32[]{:S(2)}) async-start(bf16[8,64,384]{2,1,0:T(8,128)(2,1)} %add_convert_fusion.2), calls=%async_computation.3 | async-start | bytes 786432 | tf_op jit(solution)/shard_map/all_to_all | solution.py:842
  198.9 16.7 %collective-permute-start.9 = (bf16[8,64,384]{2,1,0:T(8,128)(2,1)S(1)}, bf16[8,64,384]{2,1,0:T(8,128)(2,1)S(1)}, u32[]{:S(2)}, u32[]{:S(2)}) collective-permute-start(bf16[8,64,384]{2,1,0:T(8,128)(2,1)S(1)} %select_convert_fusion.1), channel_id=1, source_target_pairs={{0,2},{1,3},{2,0},{3,1},{4,6},{5,7},{6,4},{7,5},{8,10},{9,11},{10,... | collective-permute-start | bytes 1179656 | tf_op jit(solution)/shard_map/ppermute | solution.py:834
  215.6 0.8 copy-start.8
  216.4 0.9 copy-start.6
  217.3 3.2 %copy-start.9 = (bf16[8,64,384]{2,1,0:T(8,128)(2,1)S(1)}, bf16[8,64,384]{2,1,0:T(8,128)(2,1)}, u32[]{:S(2)}) copy-start(bf16[8,64,384]{2,1,0:T(8,128)(2,1)} %copy-done.8) | copy-start | bytes 1179652
  220.0 10.9 %collective-permute-start.11 = (bf16[8,64,384]{2,1,0:T(8,128)(2,1)}, bf16[8,64,384]{2,1,0:T(8,128)(2,1)}, u32[]{:S(2)}, u32[]{:S(2)}) collective-permute-start(bf16[8,64,384]{2,1,0:T(8,128)(2,1)} %select_convert_fusion), channel_id=1, source_target_pairs={{0,2},{1,3},{2,0},{3,1},{4,6},{5,7},{6,4},{7,5},{8,10},{9,11},{10,... | collective-permute-start | bytes 1179656 | tf_op jit(solution)/shard_map/ppermute | solution.py:834
  220.5 12.3 %collective-permute-start.12 = (bf16[16,64,256]{2,1,0:T(8,128)(2,1)}, bf16[16,64,256]{2,1,0:T(8,128)(2,1)}, u32[]{:S(2)}, u32[]{:S(2)}) collective-permute-start(bf16[16,64,256]{2,1,0:T(8,128)(2,1)} %get-tuple-element.182), channel_id=1, source_target_pairs={{0,1},{1,0},{2,3},{3,2},{4,5},{5,4},{6,7},{7,6},{8,9},{9,8},{10,11... | collective-permute-start | bytes 1572872 | tf_op jit(solution)/shard_map/ppermute | solution.py:834
  221.4 18.5 %all-to-all-start.4 = ((bf16[8,64,384]{2,1,0:T(8,128)(2,1)}), bf16[8,64,384]{2,1,0:T(8,128)(2,1)S(1)}, u32[]{:S(2)}, u32[]{:S(2)}) async-start(bf16[8,64,384]{2,1,0:T(8,128)(2,1)} %add_convert_fusion.1), calls=%async_computation.4 | async-start | bytes 786432 | tf_op jit(solution)/shard_map/all_to_all | solution.py:842
  227.6 5.2 %copy-start.3 = (f32[16,64,256]{2,1,0:T(8,128)S(1)}, f32[16,64,256]{2,1,0:T(8,128)}, u32[]{:S(2)}) copy-start(f32[16,64,256]{2,1,0:T(8,128)} %get-tuple-element.181) | copy-start | bytes 3145732
  239.9 15.5 %all-to-all-start.5 = ((bf16[8,64,384]{2,1,0:T(8,128)(2,1)}), bf16[8,64,384]{2,1,0:T(8,128)(2,1)S(1)}, u32[]{:S(2)}, u32[]{:S(2)}) async-start(bf16[8,64,384]{2,1,0:T(8,128)(2,1)} %add_convert_fusion), calls=%async_computation.5 | async-start | bytes 786432 | tf_op jit(solution)/shard_map/all_to_all | solution.py:842
  243.6 8.0 %collective-permute-start.13 = (bf16[8,64,256]{2,1,0:T(8,128)(2,1)S(1)}, bf16[8,64,256]{2,1,0:T(8,128)(2,1)S(1)}, u32[]{:S(2)}, u32[]{:S(2)}) collective-permute-start(bf16[8,64,256]{2,1,0:T(8,128)(2,1)S(1)} %select_convert_fusion.3), channel_id=1, source_target_pairs={{0,2},{1,3},{2,0},{3,1},{4,6},{5,7},{6,4},{7,5},{8,10},{9,11},{10,... | collective-permute-start | bytes 786440 | tf_op jit(solution)/shard_map/ppermute | solution.py:834
  255.4 12.7 %all-to-all-start.6 = ((bf16[8,64,256]{2,1,0:T(8,128)(2,1)}), bf16[8,64,256]{2,1,0:T(8,128)(2,1)S(1)}, u32[]{:S(2)}, u32[]{:S(2)}) async-start(bf16[8,64,256]{2,1,0:T(8,128)(2,1)} %add_convert_fusion.3), calls=%async_computation.6 | async-start | bytes 524288 | tf_op jit(solution)/shard_map/all_to_all | solution.py:842
  273.4 10.9 %all-to-all-start.7 = ((f32[8,32,128]{2,1,0:T(8,128)}), f32[8,32,128]{2,1,0:T(8,128)S(1)}, u32[]{:S(2)}, u32[]{:S(2)}) async-start(f32[8,32,128]{2,1,0:T(8,128)} %broadcast_in_dim.35), calls=%async_computation.7 | async-start | bytes 262144 | tf_op jit(solution)/shard_map/all_to_all | solution.py:842
  284.4 7.4 %copy-start.11 = (f32[32,128]{1,0:T(8,128)}, f32[32,128]{1,0:T(8,128)S(1)}, u32[]{:S(2)}) copy-start(f32[32,128]{1,0:T(8,128)S(1)} %reduce_sum.58.refs_0_) | copy-start | bytes 49156
